TPU v7x, 32 devices: a whole 2x2x4 slice. The times are simulated.
32 devices in a mesh: gx: 4 (over z), gy: 8 (over y, x, core).
Axes of the slice: x: 2, y: 2, z: 4, core: 2. Of those that a mesh axis runs over, the one named last changes fastest.
Arguments:
- blocks: float32 [192, 128, 4096], P(('gx', 'gy')), may hold values from -0.046875 to 0.046875
- features: float32 [512, 128, 512], P(('gx', 'gy')), may hold values from -6 to 6
- col_ids: int32 [192, 32], P(('gx', 'gy')), may hold values from 0 to 15
- row_ids: int32 [192], P(('gx', 'gy')), may hold values from 0 to 31
- factor: float32 [512, 512], replicated, may hold values from -0.25 to 0.25
Outputs:
- owned_rows: float32 [4096, 512], P(('gx', 'gy'))
- returned: float32 [24576, 512], P(('gx', 'gy'))
Inputs may be any that keep to these rules, and one draw needn't show every extreme that they name: `row_ids`: row block r is owned by device r, counted over gx+gy with gx slowest. Row blocks are named with a power-law skew; one device may name a row block more than once. `col_ids`: indices into the device's own feature tiles.
All inputs are finite; a program needn't handle non-finite values.
Results may differ from a plain program's by a relative error of at most 0.00013.
Values sent between devices are 32-bit elements; how exact they have to be, the bound alone decides.
No kernel may reach another device: no remote copies, remote signals or barrier semaphores. Data moves between devices by JAX's collectives and lax.ppermute only.
A program may use at most 192 MiB of HBM per device.

v0:
```python
import jax
import jax.numpy as jnp
from jax import lax
from jax.sharding import PartitionSpec as P

HIGHEST = lax.Precision.HIGHEST


def partner(value, axis, bit):
    mask = 2**bit
    pairs = [(source, source ^ mask) for source in range(lax.axis_size(axis))]
    return lax.ppermute(value, axis, pairs)


def to_dense(labels, values, range_base, range_size):
    one_hot = (
        labels[None, :] - range_base == jnp.arange(range_size, dtype=jnp.int32)[:, None]
    ).astype(jnp.float32)
    flat = values.reshape(values.shape[0], -1)
    summed = jnp.einsum("sk,kx->sx", one_hot, flat, precision=HIGHEST)
    return summed.reshape((range_size,) + values.shape[1:])


def from_dense(labels, dense_rows, range_base):
    range_size = dense_rows.shape[0]
    one_hot = (
        labels[:, None] - range_base == jnp.arange(range_size, dtype=jnp.int32)[None, :]
    ).astype(jnp.float32)
    flat = dense_rows.reshape(range_size, -1)
    picked = jnp.einsum("ks,sx->kx", one_hot, flat, precision=HIGHEST)
    return picked.reshape((labels.shape[0],) + dense_rows.shape[1:])


def local(blocks, features, col_ids, row_ids, factor):
    slot_count = row_ids.shape[0]
    tile_rows = blocks.shape[1]
    feat_width = features.shape[2]
    per_row = col_ids.shape[1]
    levels = (lax.axis_size("gx") * lax.axis_size("gy")).bit_length() - 1
    my_index = lax.axis_index("gx") * lax.axis_size("gy") + lax.axis_index("gy")
    partial_rows = []
    for slot_num in range(slot_count):
        stacked = features[col_ids[slot_num]].reshape(per_row * tile_rows, feat_width)
        partial_rows.append(
            jnp.dot(
                blocks[slot_num], stacked, precision=HIGHEST, preferred_element_type=jnp.float32
            )
        )
    values = jnp.stack(partial_rows)
    labels = row_ids
    dense_rows = None
    records = []
    for section_num in range(levels):
        bit_level = levels - 1 - section_num
        my_bit = my_index >> bit_level & 1
        if dense_rows is None and labels.shape[0] * 2 > 2 ** (bit_level + 1):
            range_base = my_index >> bit_level + 1 << bit_level + 1
            dense_rows = to_dense(labels, values, range_base, 2 ** (bit_level + 1))
            records.append(("lookup", labels, range_base, 0))
        if dense_rows is None:
            valid = labels >= 0
            kept_mask = (labels >> bit_level & 1 == my_bit) & valid
            sent_mask = jnp.logical_not(kept_mask) & valid
            send_labels = jnp.where(sent_mask, labels, -1).astype(jnp.float32)
            send_values = jnp.where(sent_mask[:, None, None], values, 0.0)
            got_labels, got_values = partner((send_labels, send_values), ("gx", "gy"), bit_level)
            labels = jnp.concatenate(
                [jnp.where(kept_mask, labels, -1), got_labels.astype(jnp.int32)]
            )
            values = jnp.concatenate([jnp.where(kept_mask[:, None, None], values, 0.0), got_values])
            records.append(("list", kept_mask, 0, bit_level))
        else:
            half_size = dense_rows.shape[0] // 2
            is_upper = my_bit == 1
            outgoing = jnp.where(is_upper, dense_rows[:half_size], dense_rows[half_size:])
            staying = jnp.where(is_upper, dense_rows[half_size:], dense_rows[:half_size])
            dense_rows = staying + partner(outgoing, ("gx", "gy"), bit_level)
            records.append(("halve", is_upper, 0, bit_level))
    owned_rows = jnp.dot(
        jnp.tanh(dense_rows[0]), factor, precision=HIGHEST, preferred_element_type=jnp.float32
    )
    answers = owned_rows[None]
    for record in reversed(records):
        if record[0] == "halve":
            is_upper = record[1]
            incoming = partner(answers, ("gx", "gy"), record[3])
            answers = jnp.where(
                is_upper, jnp.concatenate([incoming, answers]), jnp.concatenate([answers, incoming])
            )
        elif record[0] == "lookup":
            answers = from_dense(record[1], answers, record[2])
        else:
            kept_mask = record[1]
            count_kept = kept_mask.shape[0]
            incoming = partner(answers[count_kept:], ("gx", "gy"), record[3])
            answers = jnp.where(kept_mask[:, None, None], answers[:count_kept], incoming)
    returned = answers.reshape(slot_count * tile_rows, feat_width)
    return (owned_rows, returned)


def solution(mesh):
    return jax.shard_map(
        local,
        mesh=mesh,
        in_specs=(
            P(("gx", "gy"), None, None),
            P(("gx", "gy"), None, None),
            P(("gx", "gy"), None),
            P(("gx", "gy")),
            P(),
        ),
        out_specs=(P(("gx", "gy"), None), P(("gx", "gy"), None)),
        check_vma=False,
    )
```

profile of v0, /device:TPU:0, one launch (start us, length us, event | category | flops | bytes accessed | tf_op | source)
XLA Modules:
  0.0 492.4 jit_solution(14669131378984071601)
XLA Ops:
  1.6 6.6 %gather_fusion = f32[32,128,512]{2,1,0:T(8,128)} fusion(f32[16,128,512]{2,1,0:T(8,128)} %param.6, s32[1024]{0:T(1024)S(1)} %get-tuple-element.21), kind=kCustom, calls=%fused_computation | custom fusion | bytes 16777344 | tf_op jit(solution)/shard_map/gather | solution.py:43
  8.1 6.5 %gather_fusion.1 = f32[32,128,512]{2,1,0:T(8,128)} fusion(f32[16,128,512]{2,1,0:T(8,128)} %param.6, s32[1024]{0:T(1024)S(1)} %get-tuple-element.20), kind=kCustom, calls=%fused_computation.1 | custom fusion | bytes 16777344 | tf_op jit(solution)/shard_map/gather | solution.py:43
  14.7 6.6 %gather_fusion.2 = f32[32,128,512]{2,1,0:T(8,128)} fusion(f32[16,128,512]{2,1,0:T(8,128)} %param.6, s32[1024]{0:T(1024)S(1)} %get-tuple-element.19), kind=kCustom, calls=%fused_computation.2 | custom fusion | bytes 16777344 | tf_op jit(solution)/shard_map/gather | solution.py:43
  21.2 6.5 %gather_fusion.3 = f32[32,128,512]{2,1,0:T(8,128)} fusion(f32[16,128,512]{2,1,0:T(8,128)} %param.6, s32[1024]{0:T(1024)S(1)} %get-tuple-element.18), kind=kCustom, calls=%fused_computation.3 | custom fusion | bytes 16777344 | tf_op jit(solution)/shard_map/gather | solution.py:43
  27.7 6.5 %gather_fusion.4 = f32[32,128,512]{2,1,0:T(8,128)} fusion(f32[16,128,512]{2,1,0:T(8,128)} %param.6, s32[1024]{0:T(1024)S(1)} %get-tuple-element.17), kind=kCustom, calls=%fused_computation.4 | custom fusion | bytes 16777344 | tf_op jit(solution)/shard_map/gather | solution.py:43
  34.2 6.5 %gather_fusion.5 = f32[32,128,512]{2,1,0:T(8,128)} fusion(f32[16,128,512]{2,1,0:T(8,128)} %param.6, s32[1024]{0:T(1024)S(1)} %get-tuple-element.16), kind=kCustom, calls=%fused_computation.5 | custom fusion | bytes 16777344 | tf_op jit(solution)/shard_map/gather | solution.py:43
  40.8 16.0 %fusion.28 = f32[6,128,512]{1,2,0:T(8,128)S(1)} fusion(f32[4096,512]{1,0:T(8,128)} %bitcast.145, f32[6,128,4096]{2,1,0:T(8,128)} %param.5), kind=kOutput, calls=%fused_computation.40 | convolution fusion | flops 3221225472 | bytes 10747904 | tf_op jit(solution)/shard_map/dot_general | solution.py:45
  56.8 16.4 %fusion.34 = f32[6,128,512]{1,2,0:T(8,128)S(1)} fusion(f32[6,128,512]{1,2,0:T(8,128)S(1)} %fusion.28, f32[4096,512]{1,0:T(8,128)} %bitcast.146, f32[6,128,4096]{2,1,0:T(8,128)} %param.5), kind=kOutput, calls=%fused_computation.42 | convolution fusion | flops 3221225472 | bytes 10747904 | tf_op jit(solution)/shard_map/dot_general | solution.py:45
  73.2 15.3 %fusion.40 = f32[6,128,512]{1,2,0:T(8,128)S(1)} fusion(f32[6,128,512]{1,2,0:T(8,128)S(1)} %fusion.34, f32[4096,512]{1,0:T(8,128)S(1)} %bitcast.149, f32[6,128,4096]{2,1,0:T(8,128)} %param.5), kind=kOutput, calls=%fused_computation.44 | convolution fusion | flops 3221225472 | bytes 10747904 | tf_op jit(solution)/shard_map/dot_general | solution.py:45
  88.6 15.0 %fusion.46 = f32[6,128,512]{1,2,0:T(8,128)S(1)} fusion(f32[6,128,512]{1,2,0:T(8,128)S(1)} %fusion.40, f32[4096,512]{1,0:T(8,128)S(1)} %bitcast.152, f32[6,128,4096]{2,1,0:T(8,128)} %param.5), kind=kOutput, calls=%fused_computation.46 | convolution fusion | flops 3221225472 | bytes 10747904 | tf_op jit(solution)/shard_map/dot_general | solution.py:45
  103.6 15.3 %fusion.52 = f32[6,128,512]{1,2,0:T(8,128)S(1)} fusion(f32[6,128,512]{1,2,0:T(8,128)S(1)} %fusion.46, f32[4096,512]{1,0:T(8,128)S(1)} %bitcast.155, f32[6,128,4096]{2,1,0:T(8,128)} %param.5), kind=kOutput, calls=%fused_computation.48 | convolution fusion | flops 3221225472 | bytes 10747904 | tf_op jit(solution)/shard_map/dot_general | solution.py:45
  118.9 14.9 %fusion.58 = f32[6,128,512]{1,2,0:T(8,128)S(1)} fusion(f32[6,128,512]{1,2,0:T(8,128)S(1)} %fusion.52, f32[4096,512]{1,0:T(8,128)S(1)} %bitcast.158, f32[6,128,4096]{2,1,0:T(8,128)} %param.5), kind=kOutput, calls=%fused_computation.50 | convolution fusion | flops 3221225472 | bytes 10747904 | tf_op jit(solution)/shard_map/dot_general | solution.py:45
  135.3 4.0 collective-permute-start.1
  139.4 68.4 %collective-permute-done = f32[6]{0:T(128)S(1)} collective-permute-done((f32[6]{0:T(128)S(1)}, f32[6]{0:T(128)S(1)}, u32[]{:S(2)}, u32[]{:S(2)}) %collective-permute-start) | collective-permute-done | bytes 56 | tf_op jit(solution)/shard_map/ppermute | solution.py:12
  207.9 3.2 pad_maximum_fusion
  211.1 3.6 copy.7
  214.7 2.5 pad.38
  217.2 2.4 copy.12
  224.9 46.3 %collective-permute-done.2 = f32[8,128,512]{2,0,1:T(8,128)S(1)} collective-permute-done((f32[8,128,512]{2,0,1:T(8,128)}, f32[8,128,512]{2,0,1:T(8,128)S(1)}, u32[]{:S(2)}, u32[]{:S(2)}) %collective-permute-start.2) | collective-permute-done | bytes 2097184 | tf_op jit(solution)/shard_map/ppermute | solution.py:12
  272.5 2.7 add.82
  277.7 22.5 %collective-permute-done.3 = f32[4,128,512]{2,0,1:T(4,128)} collective-permute-done((f32[4,128,512]{2,0,1:T(4,128)}, f32[4,128,512]{2,0,1:T(4,128)}, u32[]{:S(2)}, u32[]{:S(2)}) %collective-permute-start.3) | collective-permute-done | bytes 1048608 | tf_op jit(solution)/shard_map/ppermute | solution.py:12
  304.5 9.9 %collective-permute-done.4 = f32[2,128,512]{2,0,1:T(2,128)S(1)} collective-permute-done((f32[2,128,512]{2,0,1:T(2,128)S(1)}, f32[2,128,512]{2,0,1:T(2,128)S(1)}, u32[]{:S(2)}, u32[]{:S(2)}) %collective-permute-start.4) | collective-permute-done | bytes 524320 | tf_op jit(solution)/shard_map/ppermute | solution.py:12
  323.7 11.4 %collective-permute-done.7 = f32[2,128,512]{2,1,0:T(8,128)S(1)} collective-permute-done((f32[2,128,512]{2,1,0:T(8,128)S(1)}, f32[2,128,512]{2,1,0:T(8,128)S(1)}, u32[]{:S(2)}, u32[]{:S(2)}) %collective-permute-start.7) | collective-permute-done | bytes 524320 | tf_op jit(solution)/shard_map/ppermute | solution.py:12
  338.2 21.4 %collective-permute-done.8 = f32[4,128,512]{2,1,0:T(8,128)S(1)} collective-permute-done((f32[4,128,512]{2,1,0:T(8,128)S(1)}, f32[4,128,512]{2,1,0:T(8,128)S(1)}, u32[]{:S(2)}, u32[]{:S(2)}) %collective-permute-start.8) | collective-permute-done | bytes 1048608 | tf_op jit(solution)/shard_map/ppermute | solution.py:12
  360.0 3.1 collective-permute-start.9
  364.6 42.7 %collective-permute-done.9 = f32[8,128,512]{2,1,0:T(8,128)S(1)} collective-permute-done((f32[8,128,512]{2,1,0:T(8,128)S(1)}, f32[8,128,512]{2,1,0:T(8,128)S(1)}, u32[]{:S(2)}, u32[]{:S(2)}) %collective-permute-start.9) | collective-permute-done | bytes 2097184 | tf_op jit(solution)/shard_map/ppermute | solution.py:12
  408.5 2.4 fusion
  413.3 3.0 copy.8
  416.3 4.0 collective-permute-start.10
  424.3 62.1 %collective-permute-done.10 = f32[6,128,512]{1,2,0:T(8,128)} collective-permute-done((f32[6,128,512]{1,2,0:T(8,128)}, f32[6,128,512]{1,2,0:T(8,128)}, u32[]{:S(2)}, u32[]{:S(2)}) %collective-permute-start.10) | collective-permute-done | bytes 1572896 | tf_op jit(solution)/shard_map/ppermute | solution.py:12
  486.4 2.8 broadcast_select_fusion.2
  489.1 3.0 copy.10
  (75 shorter events, 37.5 us)
Async XLA Ops:
  0.6 318.1 %copy-start = (f32[512,512]{1,0:T(8,128)S(1)}, f32[512,512]{1,0:T(8,128)}, u32[]{:S(2)}) copy-start(f32[512,512]{1,0:T(8,128)} %param.9) | copy-start | bytes 3145732
  34.2 6.5 %copy-start.4 = (s32[6]{0:T(128)S(1)}, s32[6]{0:T(128)}, u32[]{:S(2)}) copy-start(s32[6]{0:T(128)} %param.8) | copy-start | bytes 76
  40.8 32.4 %slice-start = ((s8[8388608]{0:T(1024)(128)(4,1)}), s8[4194304]{0:T(1024)(128)(4,1)S(1)}, s32[]{:S(2)}) async-start(s8[8388608]{0:T(1024)(128)(4,1)} %bitcast.147), calls=%async_computation | async-start | bytes 8388608
  56.8 16.4 %slice-start.1 = ((s8[8388608]{0:T(1024)(128)(4,1)}), s8[4194304]{0:T(1024)(128)(4,1)S(1)}, s32[]{:S(2)}) async-start(s8[8388608]{0:T(1024)(128)(4,1)} %bitcast.147), calls=%async_computation.1 | async-start | bytes 8388608
  56.8 31.7 %slice-start.2 = ((s8[8388608]{0:T(1024)(128)(4,1)}), s8[4194304]{0:T(1024)(128)(4,1)S(1)}, s32[]{:S(2)}) async-start(s8[8388608]{0:T(1024)(128)(4,1)} %bitcast.150), calls=%async_computation.2 | async-start | bytes 8388608
  73.2 15.3 %slice-start.3 = ((s8[8388608]{0:T(1024)(128)(4,1)}), s8[4194304]{0:T(1024)(128)(4,1)S(1)}, s32[]{:S(2)}) async-start(s8[8388608]{0:T(1024)(128)(4,1)} %bitcast.150), calls=%async_computation.3 | async-start | bytes 8388608
  73.2 30.4 %slice-start.4 = ((s8[8388608]{0:T(1024)(128)(4,1)}), s8[4194304]{0:T(1024)(128)(4,1)S(1)}, s32[]{:S(2)}) async-start(s8[8388608]{0:T(1024)(128)(4,1)} %bitcast.153), calls=%async_computation.4 | async-start | bytes 8388608
  88.5 15.1 %slice-start.5 = ((s8[8388608]{0:T(1024)(128)(4,1)}), s8[4194304]{0:T(1024)(128)(4,1)S(1)}, s32[]{:S(2)}) async-start(s8[8388608]{0:T(1024)(128)(4,1)} %bitcast.153), calls=%async_computation.5 | async-start | bytes 8388608
  88.6 30.4 %slice-start.6 = ((s8[8388608]{0:T(1024)(128)(4,1)}), s8[4194304]{0:T(1024)(128)(4,1)S(1)}, s32[]{:S(2)}) async-start(s8[8388608]{0:T(1024)(128)(4,1)} %bitcast.156), calls=%async_computation.6 | async-start | bytes 8388608
  103.6 15.3 %slice-start.7 = ((s8[8388608]{0:T(1024)(128)(4,1)}), s8[4194304]{0:T(1024)(128)(4,1)S(1)}, s32[]{:S(2)}) async-start(s8[8388608]{0:T(1024)(128)(4,1)} %bitcast.156), calls=%async_computation.7 | async-start | bytes 8388608
  135.3 72.6 %collective-permute-start.1 = (f32[6,128,512]{1,2,0:T(8,128)}, f32[6,128,512]{1,2,0:T(8,128)}, u32[]{:S(2)}, u32[]{:S(2)}) collective-permute-start(f32[6,128,512]{1,2,0:T(8,128)} %get-tuple-element.9), channel_id=1, source_target_pairs={{0,16},{1,17},{2,18},{3,19},{4,20},{5,21},{6,22},{7,23},{8,24},{9,... | collective-permute-start | bytes 4718600 | tf_op jit(solution)/shard_map/ppermute | solution.py:12
  139.4 68.4 %collective-permute-start = (f32[6]{0:T(128)S(1)}, f32[6]{0:T(128)S(1)}, u32[]{:S(2)}, u32[]{:S(2)}) collective-permute-start(f32[6]{0:T(128)S(1)} %select_convert_fusion), channel_id=1, source_target_pairs={{0,16},{1,17},{2,18},{3,19},{4,20},{5,21},{6,22},{7,23},{8,24},{9,... | collective-permute-start | bytes 80 | tf_op jit(solution)/shard_map/ppermute | solution.py:12
  224.2 47.0 %collective-permute-start.2 = (f32[8,128,512]{2,0,1:T(8,128)}, f32[8,128,512]{2,0,1:T(8,128)S(1)}, u32[]{:S(2)}, u32[]{:S(2)}) collective-permute-start(f32[8,128,512]{2,0,1:T(8,128)} %bitcast.37), channel_id=1, source_target_pairs={{0,8},{1,9},{2,10},{3,11},{4,12},{5,13},{6,14},{7,15},{8,0},{9,1},... | collective-permute-start | bytes 6291464 | tf_op jit(solution)/shard_map/ppermute | solution.py:12
  271.2 1.3 copy-start.3
  276.4 23.7 %collective-permute-start.3 = (f32[4,128,512]{2,0,1:T(4,128)}, f32[4,128,512]{2,0,1:T(4,128)}, u32[]{:S(2)}, u32[]{:S(2)}) collective-permute-start(f32[4,128,512]{2,0,1:T(4,128)} %slice_select_fusion.2), channel_id=1, source_target_pairs={{0,4},{1,5},{2,6},{3,7},{4,0},{5,1},{6,2},{7,3},{8,12},{9,13},{10,... | collective-permute-start | bytes 3145736 | tf_op jit(solution)/shard_map/ppermute | solution.py:12
  301.8 1.0 copy-start.1
  303.0 11.3 %collective-permute-start.4 = (f32[2,128,512]{2,0,1:T(2,128)S(1)}, f32[2,128,512]{2,0,1:T(2,128)S(1)}, u32[]{:S(2)}, u32[]{:S(2)}) collective-permute-start(f32[2,128,512]{2,0,1:T(2,128)S(1)} %broadcast_select_fusion.3), channel_id=1, source_target_pairs={{0,2},{1,3},{2,0},{3,1},{4,6},{5,7},{6,4},{7,5},{8,10},{9,11},{10,... | collective-permute-start | bytes 1572872 | tf_op jit(solution)/shard_map/ppermute | solution.py:12
  316.7 1.6 collective-permute-start.5
  319.4 17.8 %copy-start.2 = (f32[128,512]{1,0:T(8,128)}, f32[128,512]{1,0:T(8,128)S(1)}, u32[]{:S(2)}) copy-start(f32[128,512]{1,0:T(8,128)S(1)} %fusion.63) | copy-start | bytes 786436
  319.4 1.6 collective-permute-start.6
  321.1 14.0 %collective-permute-start.7 = (f32[2,128,512]{2,1,0:T(8,128)S(1)}, f32[2,128,512]{2,1,0:T(8,128)S(1)}, u32[]{:S(2)}, u32[]{:S(2)}) collective-permute-start(f32[2,128,512]{2,1,0:T(8,128)S(1)} %maximum_select_fusion.6), channel_id=1, source_target_pairs={{0,2},{1,3},{2,0},{3,1},{4,6},{5,7},{6,4},{7,5},{8,10},{9,11},{10,... | collective-permute-start | bytes 1572872 | tf_op jit(solution)/shard_map/ppermute | solution.py:12
  335.2 24.4 %collective-permute-start.8 = (f32[4,128,512]{2,1,0:T(8,128)S(1)}, f32[4,128,512]{2,1,0:T(8,128)S(1)}, u32[]{:S(2)}, u32[]{:S(2)}) collective-permute-start(f32[4,128,512]{2,1,0:T(8,128)S(1)} %maximum_select_fusion.4), channel_id=1, source_target_pairs={{0,4},{1,5},{2,6},{3,7},{4,0},{5,1},{6,2},{7,3},{8,12},{9,13},{10,... | collective-permute-start | bytes 3145736 | tf_op jit(solution)/shard_map/ppermute | solution.py:12
  360.0 47.3 %collective-permute-start.9 = (f32[8,128,512]{2,1,0:T(8,128)S(1)}, f32[8,128,512]{2,1,0:T(8,128)S(1)}, u32[]{:S(2)}, u32[]{:S(2)}) collective-permute-start(f32[8,128,512]{2,1,0:T(8,128)S(1)} %maximum_select_fusion.2), channel_id=1, source_target_pairs={{0,8},{1,9},{2,10},{3,11},{4,12},{5,13},{6,14},{7,15},{8,0},{9,1},... | collective-permute-start | bytes 6291464 | tf_op jit(solution)/shard_map/ppermute | solution.py:12
  416.3 70.1 %collective-permute-start.10 = (f32[6,128,512]{1,2,0:T(8,128)}, f32[6,128,512]{1,2,0:T(8,128)}, u32[]{:S(2)}, u32[]{:S(2)}) collective-permute-start(f32[6,128,512]{1,2,0:T(8,128)} %copy.8), channel_id=1, source_target_pairs={{0,16},{1,17},{2,18},{3,19},{4,20},{5,21},{6,22},{7,23},{8,24},{9,... | collective-permute-start | bytes 4718600 | tf_op jit(solution)/shard_map/ppermute | solution.py:12
where the time goes:
time: 500 us; the launch traced here: 492 us
  waiting for transfers between devices  287 us (57%)
  matrix products  98.1 us (20%)
  local copies, waits for them, and re-layouts  65.2 us (13%)
  other arithmetic  22.3 us (4%)
  starting transfers between devices  18.2 us (4%)
    ppermute x11, waiting for transfers between devices, partner(): return lax.ppermute(value, axis, pairs)  287 us
    dot_general x6, matrix products, local(): jnp.dot(blocks[slot_num], stacked, precision=HIGHEST, preferred_element_t...  92.8 us
    gather x6, local copies, waits for them, and re-layouts, local(): features[col_ids[slot_num]].reshape(per_row * tile_rows, feat_width)  39.2 us
    ppermute x11, starting transfers between devices, partner(): return lax.ppermute(value, axis, pairs)  18.2 us
    unnamed x35, local copies, waits for them, and re-layouts  14.3 us
  transfers between devices with their start and end apart: 11, of which 10 were waited for; matrix products, arithmetic and copies ran while one was open for 2% of the time, Pallas kernels for 0%

commit v1 on v0

v1 whole, which is shorter than its diff:
```python
import functools

import jax
import jax.numpy as jnp
from jax import lax
from jax.experimental import pallas as pl
from jax.experimental.pallas import tpu as pltpu
from jax.sharding import Mesh
from jax.sharding import PartitionSpec as P

F32 = jnp.float32
BF16 = jnp.bfloat16
VMEM_BYTES = 48 << 20


def split(value):
    high = value.astype(BF16)
    return high, (value - high.astype(F32)).astype(BF16)


def dot3(a_high, a_low, b_high, b_low):
    dot = functools.partial(jnp.dot, preferred_element_type=F32)
    return dot(a_high, b_high) + dot(a_high, b_low) + dot(a_low, b_high)


def product_kernel(
    group, peers, cols_ref, blocks_ref, features_ref, out_ref, total, a_high, a_low, f_high, f_low
):
    slot = pl.program_id(0)
    tiles, rows, feat = features_ref.shape
    per_row = cols_ref.shape[1]

    @pl.when(slot == 0)
    def _():
        def split_tile(tile, carry):
            high, low = split(features_ref[tile])
            at = pl.ds(pl.multiple_of(tile * rows, rows), rows)
            f_high[at, :] = high
            f_low[at, :] = low
            return carry

        lax.fori_loop(0, tiles, split_tile, 0)

    total[...] = jnp.zeros_like(total)
    for j in range(per_row):
        tile = cols_ref[slot, j]
        total[tile] = total[tile] + blocks_ref[0, :, j * rows : (j + 1) * rows]
    at = pl.ds(pl.multiple_of(lax.rem(slot, group) * rows, rows), rows)
    for tile in range(tiles):
        high, low = split(total[tile])
        a_high[at, tile * rows : (tile + 1) * rows] = high
        a_low[at, tile * rows : (tile + 1) * rows] = low

    @pl.when(lax.rem(slot, group) == group - 1)
    def _():
        width = min(feat, 256)
        for n in range(feat // width):
            cut = slice(n * width, (n + 1) * width)
            part = dot3(a_high[...], a_low[...], f_high[:, cut], f_low[:, cut])
            for g in range(group):
                out_ref[:, g, :, cut] = part[g * rows : (g + 1) * rows].reshape(
                    peers, rows // peers, width
                )


def product(blocks, features, col_ids, peers):
    slots, rows, width = blocks.shape
    tiles, _, feat = features.shape
    group = 2 if slots % 2 == 0 else 1
    return pl.pallas_call(
        functools.partial(product_kernel, group, peers),
        grid_spec=pltpu.PrefetchScalarGridSpec(
            num_scalar_prefetch=1,
            grid=(slots,),
            in_specs=[
                pl.BlockSpec((1, rows, width), lambda k, c: (k, 0, 0)),
                pl.BlockSpec(
                    (tiles, rows, feat), lambda k, c: (0, 0, 0), pipeline_mode=pl.Buffered(1)
                ),
            ],
            out_specs=pl.BlockSpec(
                (peers, group, rows // peers, feat), lambda k, c: (0, k // group, 0, 0)
            ),
            scratch_shapes=[
                pltpu.VMEM((tiles, rows, rows), F32),
                pltpu.VMEM((group * rows, tiles * rows), BF16),
                pltpu.VMEM((group * rows, tiles * rows), BF16),
                pltpu.VMEM((tiles * rows, feat), BF16),
                pltpu.VMEM((tiles * rows, feat), BF16),
            ],
        ),
        out_shape=jax.ShapeDtypeStruct((peers, slots, rows // peers, feat), F32),
        compiler_params=pltpu.CompilerParams(vmem_limit_bytes=VMEM_BYTES),
        name="product",
    )(col_ids, blocks, features)


def gather_sum_kernel(rows_ref, half_ref, pieces_ref, stay_ref, send_ref):
    peers, slots = pieces_ref.shape[:2]
    half_rows = stay_ref.shape[0]
    stay_ref[...] = jnp.zeros_like(stay_ref)
    send_ref[...] = jnp.zeros_like(send_ref)
    base = half_ref[0] * half_rows

    def add_peer(peer, carry):
        for slot in range(slots):
            row = rows_ref[peer * slots + slot] - base
            here = (row >= 0) & (row < half_rows)
            row = lax.select(row < 0, row + half_rows, row)
            row = lax.select(row >= half_rows, row - half_rows, row)

            @pl.when(here)
            def _():
                stay_ref[row] = stay_ref[row] + pieces_ref[peer, slot]

            @pl.when(jnp.logical_not(here))
            def _():
                send_ref[row] = send_ref[row] + pieces_ref[peer, slot]

        return carry

    lax.fori_loop(0, peers, add_peer, 0)


def gather_sum(group_rows, half, pieces, row_blocks):
    _, _, rows, feat = pieces.shape
    shape = jax.ShapeDtypeStruct((row_blocks // 2, rows, feat), F32)
    smem = pl.BlockSpec(memory_space=pltpu.SMEM)
    vmem = pl.BlockSpec(memory_space=pltpu.VMEM)
    return pl.pallas_call(
        gather_sum_kernel,
        in_specs=[smem, smem, vmem],
        out_specs=(vmem, vmem),
        out_shape=(shape, shape),
        compiler_params=pltpu.CompilerParams(vmem_limit_bytes=VMEM_BYTES),
        name="gather_sum",
    )(group_rows, half, pieces)


def update_kernel(mine_ref, theirs_ref, factor_ref, out_ref):
    count, rows, feat = out_ref.shape
    sums = jnp.tanh(mine_ref[...] + theirs_ref[...]).reshape(count * rows, feat)
    out = dot3(*split(sums), *split(factor_ref[...]))
    out_ref[...] = out.reshape(out_ref.shape)


def update(mine, theirs, factor):
    return pl.pallas_call(
        update_kernel,
        out_shape=jax.ShapeDtypeStruct(mine.shape, F32),
        compiler_params=pltpu.CompilerParams(vmem_limit_bytes=VMEM_BYTES),
        name="update",
    )(mine, theirs, factor)


def answer_kernel(rows_ref, half_ref, mine_ref, theirs_ref, out_ref):
    peers, places = out_ref.shape[:2]
    slots = places - 1
    half_rows = mine_ref.shape[0]
    base = half_ref[0] * half_rows

    def pick(peer, carry):
        for slot in range(slots):
            row = rows_ref[peer * slots + slot] - base
            here = (row >= 0) & (row < half_rows)
            row = lax.select(row < 0, row + half_rows, row)
            row = lax.select(row >= half_rows, row - half_rows, row)

            @pl.when(here)
            def _():
                out_ref[peer, slot] = mine_ref[row]

            @pl.when(jnp.logical_not(here))
            def _():
                out_ref[peer, slot] = theirs_ref[row]

        out_ref[peer, slots] = mine_ref[peer]
        return carry

    lax.fori_loop(0, peers, pick, 0)


def answer(group_rows, half, mine, theirs, peers, slots):
    _, rows, feat = mine.shape
    smem = pl.BlockSpec(memory_space=pltpu.SMEM)
    vmem = pl.BlockSpec(memory_space=pltpu.VMEM)
    return pl.pallas_call(
        answer_kernel,
        in_specs=[smem, smem, vmem, vmem],
        out_specs=vmem,
        out_shape=jax.ShapeDtypeStruct((peers, slots + 1, rows, feat), F32),
        compiler_params=pltpu.CompilerParams(vmem_limit_bytes=VMEM_BYTES),
        name="answer",
    )(group_rows, half, mine, theirs)


def local(axes, blocks, features, col_ids, row_ids, factor):
    half_axis, peer_axes = axes[0], axes[1:]
    slots, rows, _ = blocks.shape
    feat = features.shape[2]
    peers = lax.axis_size(peer_axes)
    halves = lax.axis_size(half_axis)
    row_blocks = peers * halves
    half = lax.axis_index(half_axis).astype(jnp.int32).reshape(1)
    group_rows = lax.all_gather(row_ids, peer_axes, tiled=True)

    pieces = product(blocks, features, col_ids, peers)
    pieces = lax.all_to_all(pieces, peer_axes, 0, 0)
    stay, send = gather_sum(group_rows, half, pieces, row_blocks)
    swap = [(0, 1), (1, 0)]
    got = lax.ppermute(send, half_axis, swap)
    mine = update(stay, got, factor)
    theirs = lax.ppermute(mine, half_axis, swap)
    answers = answer(group_rows, half, mine, theirs, peers, slots)
    answers = lax.all_to_all(answers, peer_axes, 0, 0)
    returned = answers[:, :slots].transpose(1, 0, 2, 3).reshape(slots * rows, feat)
    owned_rows = answers[:, slots].reshape(rows, feat)
    return owned_rows, returned


def solution(mesh):
    outer, inner = mesh.devices.shape
    devices = mesh.devices.reshape(2, outer // 2, inner)
    axes = ("half", "gx_low", "gy")
    split_mesh = Mesh(devices, axes)
    return jax.shard_map(
        functools.partial(local, axes),
        mesh=split_mesh,
        in_specs=(P(axes, None, None), P(axes, None, None), P(axes, None), P(axes), P()),
        out_specs=(P(axes, None), P(axes, None)),
        check_vma=False,
    )
```

time: 500 us -> 114 us (0.23); the launches traced: 492 us -> 113 us
  waiting for transfers between devices: 287 us -> 22.7 us
  matrix products: 98.1 us -> 0 us
  local copies, waits for them, and re-layouts: 65.2 us -> 5.88 us
  blocking collectives: 0 us -> 54.1 us
  other arithmetic: 22.3 us -> 0 us
  Pallas kernels: 0 us -> 19.9 us
  starting transfers between devices: 18.2 us -> 9.14 us
    ppermute x11 -> x2, waiting for transfers between devices: 287 us -> 22.7 us  [the longest x1 13.2 us: local(): theirs = lax.ppermute(mine, half_axis, swap)]
    dot_general x9 -> x0, matrix products: 98.1 us -> none  [the longest x6 92.8 us: local(): jnp.dot(blocks[slot_num], stacked, precision=HIGHEST, preferred_element_t...]
    gather x6 -> x0, local copies, waits for them, and re-layouts: 39.2 us -> none  [local(): features[col_ids[slot_num]].reshape(per_row * tile_rows, feat_width)]
    all_to_all x0 -> x1, blocking collectives: none -> 27.9 us  [local(): answers = lax.all_to_all(answers, peer_axes, 0, 0)]
    unnamed x0 -> x1, blocking collectives: none -> 26.2 us
    pallas_call x0 -> x4, Pallas kernels: none -> 19.9 us  [the longest x1 15.3 us: product(): pl.pallas_call(functools.partial(product_kernel, group, peers), grid_spec...]
    ppermute x11 -> x2, starting transfers between devices: 18.2 us -> 2.72 us  [the longest x1 2.65 us: local(): got = lax.ppermute(send, half_axis, swap)]
    select_n x14 -> x0, other arithmetic: 12.2 us -> none  [the longest x4 4.11 us: local(): jnp.where(is_upper, dense_rows[:half_size], dense_rows[half_size:])]
  transfers between devices with their start and end apart: 11 -> 3, of which waited for: 10 -> 2; matrix products, arithmetic and copies ran while one was open for 2% -> 1% of each run, Pallas kernels for 0% -> 0%
where the time goes in v1:
time: 114 us; the launch traced here: 113 us
  blocking collectives  54.1 us (47%)
  waiting for transfers between devices  22.7 us (20%)
  Pallas kernels  19.9 us (17%)
  starting transfers between devices  9.14 us (8%)
  local copies, waits for them, and re-layouts  5.88 us (5%)
  between operations  1.37 us (1%)
    all_to_all x1, blocking collectives, local(): answers = lax.all_to_all(answers, peer_axes, 0, 0)  27.9 us
    unnamed x1, blocking collectives  26.2 us
    pallas_call x1, Pallas kernels, product(): pl.pallas_call(functools.partial(product_kernel, group, peers), grid_spec...  15.3 us
    ppermute x1, waiting for transfers between devices, local(): theirs = lax.ppermute(mine, half_axis, swap)  13.2 us
    ppermute x1, waiting for transfers between devices, local(): got = lax.ppermute(send, half_axis, swap)  9.52 us
    all_to_all x1, starting transfers between devices, local(): pieces = lax.all_to_all(pieces, peer_axes, 0, 0)  6.42 us
    unnamed x13, local copies, waits for them, and re-layouts  3.71 us
    ppermute x1, starting transfers between devices, local(): got = lax.ppermute(send, half_axis, swap)  2.65 us
  transfers between devices with their start and end apart: 3, of which 2 were waited for; matrix products, arithmetic and copies ran while one was open for 1% of the time, Pallas kernels for 0%

profile of v1, /device:TPU:0, one launch (start us, length us, event | category | flops | bytes accessed | tf_op | source)
XLA Modules:
  0.0 113.1 jit_solution(15722459273534365463)
XLA Ops:
  0.6 0.0 copy-start
  0.6 2.2 %copy-done = f32[16,128,512]{2,1,0:T(8,128)S(1)} copy-done((f32[16,128,512]{2,1,0:T(8,128)S(1)}, f32[16,128,512]{2,1,0:T(8,128)}, u32[]{:S(2)}) %copy-start) | copy-done | bytes 4194328
  2.8 0.0 copy-start.2
  2.8 0.7 copy-done.2
  3.5 15.3 %product.1 = f32[16,6,8,512]{3,2,1,0:T(8,128)} custom-call(s32[6,32]{1,0:T(8,128)S(1)} %copy-done.2, f32[6,128,4096]{2,1,0:T(8,128)} %blocks_ref.1, f32[16,128,512]{2,1,0:T(8,128)S(1)} %copy-done), custom_call_target="tpu_custom_call" | custom-call | tf_op jit(solution)/shard_map/product/pallas_call | solution.py:70
  18.8 0.0 copy-start.4
  18.8 0.0 copy-start.3
  18.8 0.0 copy-start.1
  18.8 6.4 %all-to-all-start = ((f32[16,6,8,512]{3,2,1,0:T(8,128)}), f32[16,6,8,512]{3,2,1,0:T(8,128)S(1)}, u32[]{:S(2)}, u32[]{:S(2)}) async-start(f32[16,6,8,512]{3,2,1,0:T(8,128)} %product.1), calls=%async_computation | async-start | bytes 3145728 | tf_op jit(solution)/shard_map/all_to_all | solution.py:208
  25.2 0.0 copy-done.4
  25.2 0.6 dynamic-slice
  26.5 0.0 copy-done.3
  26.5 0.2 dynamic-update-slice
  26.7 26.2 %all-reduce.rows_ref = s32[96]{0:T(128)S(1)} all-reduce(s32[96]{0:T(128)S(1)} %dynamic-update-slice), channel_id=1, replica_groups=mesh['half'=2,'gx_low'=2,'gy'=8] {'gx_low','gy'}, use_global_device_ids=true, to_apply=%add | all-reduce | flops 96 | bytes 768
  52.9 0.0 all-to-all-done.pieces_ref
  53.0 2.2 %gather_sum.1 = (f32[16,8,512]{2,1,0:T(8,128)S(1)}, f32[16,8,512]{2,1,0:T(8,128)S(1)}) custom-call(s32[96]{0:T(128)S(1)} %all-reduce.rows_ref, s32[1]{0:T(128)} %bitcast.1.half_ref, f32[16,6,8,512]{3,2,1,0:T(8,128)S(1)} %all-to-all-done.pieces_ref), custom_call_target="tpu_custom_call" | custom-call | tf_op jit(solution)/shard_map/gather_sum/pallas_call | solution.py:130
  55.1 2.7 %collective-permute-start = (f32[16,8,512]{2,1,0:T(8,128)S(1)}, f32[16,8,512]{2,1,0:T(8,128)S(1)}, u32[]{:S(2)}, u32[]{:S(2)}) collective-permute-start(f32[16,8,512]{2,1,0:T(8,128)S(1)} %get-tuple-element.5), channel_id=1, source_target_pairs={{0,16},{16,0},{1,17},{17,1},{2,18},{18,2},{3,19},{19,3},{4,20},{20... | collective-permute-start | bytes 786440 | tf_op jit(solution)/shard_map/ppermute | solution.py:211
  57.8 9.5 %collective-permute-done.theirs_ref = f32[16,8,512]{2,1,0:T(8,128)S(1)} collective-permute-done((f32[16,8,512]{2,1,0:T(8,128)S(1)}, f32[16,8,512]{2,1,0:T(8,128)S(1)}, u32[]{:S(2)}, u32[]{:S(2)}) %collective-permute-start) | collective-permute-done | bytes 262176 | tf_op jit(solution)/shard_map/ppermute | solution.py:211
  67.3 0.0 copy-done.1
  67.3 0.4 update.1.mine_ref
  67.7 0.1 collective-permute-start.1
  67.8 13.2 %collective-permute-done.1.theirs_ref = f32[16,8,512]{2,1,0:T(8,128)S(1)} collective-permute-done((f32[16,8,512]{2,1,0:T(8,128)S(1)}, f32[16,8,512]{2,1,0:T(8,128)S(1)}, u32[]{:S(2)}, u32[]{:S(2)}) %collective-permute-start.1) | collective-permute-done | bytes 262176 | tf_op jit(solution)/shard_map/ppermute | solution.py:213
  81.0 2.1 %answer.1 = f32[16,7,8,512]{3,2,1,0:T(8,128)S(1)} custom-call(s32[96]{0:T(128)S(1)} %all-reduce.rows_ref, s32[1]{0:T(128)} %bitcast.1.half_ref, f32[16,8,512]{2,1,0:T(8,128)S(1)} %update.1.mine_ref, f32[16,8,512]{2,1,0:T(8,128)S(1)} %collective-permute-done.1.theirs_ref), custom_call_target="tpu_custom_call" | custom-call | tf_op jit(solution)/shard_map/answer/pallas_call | solution.py:187
  83.1 27.9 %all_to_all.10 = f32[16,7,8,512]{3,2,1,0:T(8,128)S(1)} all-to-all(f32[16,7,8,512]{3,2,1,0:T(8,128)S(1)} %answer.1), channel_id=1, replica_groups=mesh['half'=2,'gx_low'=2,'gy'=8] {'gx_low','gy'}, dimensions={0} | all-to-all | bytes 3670016 | tf_op jit(solution)/shard_map/all_to_all | solution.py:215
  111.0 0.2 slice_bitcast_fusion
  111.1 1.3 %copy.7 = f32[6,16,8,512]{3,2,1,0:T(8,128)} copy(f32[6,16,8,512]{3,2,0,1:T(8,128)S(1)} %slice_bitcast_fusion) | data formatting | bytes 3145728 | tf_op jit(solution)/shard_map/transpose | solution.py:216
  112.4 0.7 slice_bitcast_fusion.1
  (1 shorter events, 0.0 us)
Async XLA Ops:
  0.6 2.2 %copy-start = (f32[16,128,512]{2,1,0:T(8,128)S(1)}, f32[16,128,512]{2,1,0:T(8,128)}, u32[]{:S(2)}) copy-start(f32[16,128,512]{2,1,0:T(8,128)} %features_ref.1) | copy-start | bytes 12582916
  2.8 0.7 copy-start.2
  18.8 6.4 %copy-start.4 = (u32[32]{0:T(128)S(1)}, u32[32]{0:T(128)}, u32[]{:S(2)}) copy-start(u32[32]{0:T(128)} %constant.12) | copy-start | bytes 388
  18.8 7.7 %copy-start.3 = (s32[6]{0:T(128)S(1)}, s32[6]{0:T(128)}, u32[]{:S(2)}) copy-start(s32[6]{0:T(128)} %param.8) | copy-start | bytes 76
  18.8 48.6 %copy-start.1 = (f32[512,512]{1,0:T(8,128)S(1)}, f32[512,512]{1,0:T(8,128)}, u32[]{:S(2)}) copy-start(f32[512,512]{1,0:T(8,128)} %factor_ref.1) | copy-start | bytes 3145732
  18.8 34.2 %all-to-all-start = ((f32[16,6,8,512]{3,2,1,0:T(8,128)}), f32[16,6,8,512]{3,2,1,0:T(8,128)S(1)}, u32[]{:S(2)}, u32[]{:S(2)}) async-start(f32[16,6,8,512]{3,2,1,0:T(8,128)} %product.1), calls=%async_computation | async-start | bytes 3145728 | tf_op jit(solution)/shard_map/all_to_all | solution.py:208
  55.1 12.2 %collective-permute-start = (f32[16,8,512]{2,1,0:T(8,128)S(1)}, f32[16,8,512]{2,1,0:T(8,128)S(1)}, u32[]{:S(2)}, u32[]{:S(2)}) collective-permute-start(f32[16,8,512]{2,1,0:T(8,128)S(1)} %get-tuple-element.5), channel_id=1, source_target_pairs={{0,16},{16,0},{1,17},{17,1},{2,18},{18,2},{3,19},{19,3},{4,20},{20... | collective-permute-start | bytes 786440 | tf_op jit(solution)/shard_map/ppermute | solution.py:211
  67.7 13.3 %collective-permute-start.1 = (f32[16,8,512]{2,1,0:T(8,128)S(1)}, f32[16,8,512]{2,1,0:T(8,128)S(1)}, u32[]{:S(2)}, u32[]{:S(2)}) collective-permute-start(f32[16,8,512]{2,1,0:T(8,128)S(1)} %update.1.mine_ref), channel_id=1, source_target_pairs={{0,16},{16,0},{1,17},{17,1},{2,18},{18,2},{3,19},{19,3},{4,20},{20... | collective-permute-start | bytes 786440 | tf_op jit(solution)/shard_map/ppermute | solution.py:213

commit v2 on v1

v2 whole, which is shorter than its diff:
```python
import functools

import jax
import jax.numpy as jnp
from jax import lax
from jax.experimental import pallas as pl
from jax.experimental.pallas import tpu as pltpu
from jax.sharding import Mesh
from jax.sharding import PartitionSpec as P

F32 = jnp.float32
BF16 = jnp.bfloat16
I32 = jnp.int32
LANES = 128
VMEM_BYTES = 40 << 20


def split(value):
    high = value.astype(BF16)
    return high, (value - high.astype(F32)).astype(BF16)


def dot3(a_high, a_low, b_high, b_low):
    dot = functools.partial(jnp.dot, preferred_element_type=F32)
    return dot(a_high, b_high) + dot(a_high, b_low) + dot(a_low, b_high)


def spec(space):
    return pl.BlockSpec(memory_space=space)


def params():
    return pltpu.CompilerParams(vmem_limit_bytes=VMEM_BYTES)


def product_kernel(
    with_ids, part_ref, ids_ref, blocks_ref, cols_hbm, features_hbm, out_ref,
    total, a_high, a_low, f_high, f_low, features, cols, sems,
):
    slot = pl.program_id(0)
    slots, per_row = cols.shape
    tiles, depth, feat = features.shape
    rows = blocks_ref.shape[1]
    peers, _, piece_rows, _ = out_ref.shape
    features_copy = pltpu.make_async_copy(features_hbm, features, sems.at[0])

    @pl.when(slot == 0)
    def _():
        cols_copy = pltpu.make_async_copy(cols_hbm, cols, sems.at[1])
        cols_copy.start()
        features_copy.start()
        cols_copy.wait()

    total[...] = jnp.zeros_like(total)
    for j in range(per_row):
        tile = cols[slot, j]
        total[tile] = total[tile] + blocks_ref[0, :, j * depth : (j + 1) * depth]
    at = pl.ds(pl.multiple_of(slot * rows, rows), rows)
    for tile in range(tiles):
        high, low = split(total[tile])
        a_high[at, tile * depth : (tile + 1) * depth] = high
        a_low[at, tile * depth : (tile + 1) * depth] = low

    @pl.when(slot == slots - 1)
    def _():
        features_copy.wait()

        def split_tile(tile, carry):
            high, low = split(features[tile])
            here = pl.ds(pl.multiple_of(tile * depth, depth), depth)
            f_high[here, :] = high
            f_low[here, :] = low
            return carry

        lax.fori_loop(0, tiles, split_tile, 0)
        width = min(feat, 2 * LANES)
        for n in range(0, feat, width):
            cut = slice(n, n + width)
            part = dot3(a_high[...], a_low[...], f_high[:, cut], f_low[:, cut])
            for g in range(slots):
                for t in range(0, width, LANES):
                    piece = part[g * rows : (g + 1) * rows, t : t + LANES]
                    place = (g * feat + n + t) // LANES
                    out_ref[:, place] = piece.reshape(peers, piece_rows, LANES)
        if with_ids:
            lane = lax.broadcasted_iota(I32, (peers, piece_rows, LANES), 2)
            ids = jnp.zeros((peers, piece_rows, LANES), I32)
            for g in range(slots):
                ids = jnp.where(lane == g, ids_ref[g], ids)
            out_ref[:, slots * feat // LANES] = ids.astype(F32)


def product(blocks, features, col_ids, row_ids, part, peers, with_ids):
    slots, rows, width = blocks.shape
    tiles, depth, feat = features.shape
    rows //= 2
    out = (peers, slots * feat // LANES + int(with_ids), rows // peers, LANES)
    return pl.pallas_call(
        functools.partial(product_kernel, with_ids),
        grid_spec=pltpu.PrefetchScalarGridSpec(
            num_scalar_prefetch=2,
            grid=(slots,),
            in_specs=[
                pl.BlockSpec((1, rows, width), lambda k, part, ids: (k, part[0], 0)),
                spec(pltpu.HBM),
                spec(pltpu.HBM),
            ],
            out_specs=pl.BlockSpec(out, lambda k, part, ids: (0, 0, 0, 0)),
            scratch_shapes=[
                pltpu.VMEM((tiles, rows, depth), F32),
                pltpu.VMEM((slots * rows, tiles * depth), BF16),
                pltpu.VMEM((slots * rows, tiles * depth), BF16),
                pltpu.VMEM((tiles * depth, feat), BF16),
                pltpu.VMEM((tiles * depth, feat), BF16),
                pltpu.VMEM(features.shape, F32),
                pltpu.SMEM(col_ids.shape, I32),
                pltpu.SemaphoreType.DMA((2,)),
            ],
        ),
        out_shape=jax.ShapeDtypeStruct(out, F32),
        compiler_params=params(),
        cost_estimate=pl.CostEstimate(
            flops=6 * slots * rows * tiles * depth * feat,
            bytes_accessed=4 * (slots * rows * width + tiles * depth * feat),
            transcendentals=0,
        ),
        name="product",
    )(part, row_ids, blocks, col_ids, features)


def sum_kernel(slots, pieces_ref, out_ref, ids_out, ids, sem):
    peers, places = pieces_ref.shape[:2]
    tiles = out_ref.shape[1]
    ids_copy = pltpu.make_async_copy(pieces_ref.at[:, places - 1], ids, sem)
    ids_copy.start()
    out_ref[...] = jnp.zeros_like(out_ref)
    ids_copy.wait()

    def add_peer(peer, carry):
        for slot in range(slots):
            row = ids[peer, 0, slot].astype(I32)
            ids_out[peer * slots + slot] = row
            out_ref[row] = out_ref[row] + pieces_ref[peer, slot * tiles : (slot + 1) * tiles]
        return carry

    lax.fori_loop(0, peers, add_peer, 0)


def sum_pieces(pieces, row_blocks, slots):
    peers, places, rows, _ = pieces.shape
    tiles = (places - 1) // slots
    return pl.pallas_call(
        functools.partial(sum_kernel, slots),
        in_specs=[spec(pltpu.VMEM)],
        out_specs=(spec(pltpu.VMEM), spec(pltpu.SMEM)),
        out_shape=(
            jax.ShapeDtypeStruct((row_blocks, tiles, rows, LANES), F32),
            jax.ShapeDtypeStruct((peers * slots,), I32),
        ),
        scratch_shapes=[pltpu.SMEM((peers, rows, LANES), F32), pltpu.SemaphoreType.DMA],
        compiler_params=params(),
        name="sum_pieces",
    )(pieces)


def update_kernel(slots, ids_ref, pieces_ref, got_ref, factor_ref, out_ref, total, left):
    peers = pieces_ref.shape[0]
    row_blocks, tiles, rows, _ = out_ref.shape
    total[...] = got_ref[...]

    def add_peer(peer, carry):
        for slot in range(slots):
            row = ids_ref[peer * slots + slot]
            total[row] = total[row] + pieces_ref[peer, slot * tiles : (slot + 1) * tiles]
        return carry

    lax.fori_loop(0, peers, add_peer, 0)
    for row in range(row_blocks):
        for t in range(tiles):
            left[row * rows : (row + 1) * rows, t * LANES : (t + 1) * LANES] = total[row, t]
    out = dot3(*split(jnp.tanh(left[...])), *split(factor_ref[...]))
    for row in range(row_blocks):
        for t in range(tiles):
            out_ref[row, t] = out[row * rows : (row + 1) * rows, t * LANES : (t + 1) * LANES]


def update(ids, pieces, got, factor, slots):
    row_blocks, tiles, rows, _ = got.shape
    return pl.pallas_call(
        functools.partial(update_kernel, slots),
        in_specs=[spec(pltpu.SMEM), spec(pltpu.VMEM), spec(pltpu.VMEM), spec(pltpu.VMEM)],
        out_specs=spec(pltpu.VMEM),
        out_shape=jax.ShapeDtypeStruct(got.shape, F32),
        scratch_shapes=[
            pltpu.VMEM(got.shape, F32),
            pltpu.VMEM((row_blocks * rows, tiles * LANES), F32),
        ],
        compiler_params=params(),
        name="update",
    )(ids, pieces, got, factor)


def answer_kernel(slots, ids_ref, half_ref, table_ref, out_ref):
    peers = out_ref.shape[0]
    tiles = table_ref.shape[1]
    first = half_ref[0] * peers

    def pick(peer, carry):
        for slot in range(slots):
            row = ids_ref[peer * slots + slot]
            out_ref[peer, slot * tiles : (slot + 1) * tiles] = table_ref[row]
        out_ref[peer, slots * tiles :] = table_ref[first + peer]
        return carry

    lax.fori_loop(0, peers, pick, 0)


def answer(ids, half, table, peers, slots):
    _, tiles, rows, _ = table.shape
    return pl.pallas_call(
        functools.partial(answer_kernel, slots),
        in_specs=[spec(pltpu.SMEM), spec(pltpu.SMEM), spec(pltpu.VMEM)],
        out_specs=spec(pltpu.VMEM),
        out_shape=jax.ShapeDtypeStruct((peers, (slots + 1) * tiles, rows, LANES), F32),
        compiler_params=params(),
        name="answer",
    )(ids, half, table)


def place_kernel(slots, part_ref, answers_ref, *refs):
    owned_ref, returned_ref = refs[-2:]
    peers, places, rows, _ = answers_ref.shape
    tiles = places // (slots + 1)

    def copy_out(peer, carry):
        here = pl.ds(peer * rows, rows)
        for t in range(tiles):
            cut = slice(t * LANES, (t + 1) * LANES)
            for slot in range(slots):
                returned_ref[slot, here, cut] = answers_ref[peer, slot * tiles + t]
            owned_ref[here, cut] = answers_ref[peer, slots * tiles + t]
        return carry

    for peer in range(peers):
        copy_out(peer, 0)


def place(part, answers, slots, earlier=()):
    peers, places, rows, _ = answers.shape
    feat = places // (slots + 1) * LANES
    half_rows = peers * rows
    return pl.pallas_call(
        functools.partial(place_kernel, slots),
        grid_spec=pltpu.PrefetchScalarGridSpec(
            num_scalar_prefetch=1,
            grid=(1,),
            in_specs=[pl.BlockSpec(answers.shape, lambda i, part: (0, 0, 0, 0))]
            + [spec(pltpu.HBM)] * len(earlier),
            out_specs=(
                pl.BlockSpec((half_rows, feat), lambda i, part: (part[0], 0)),
                pl.BlockSpec((slots, half_rows, feat), lambda i, part: (0, part[0], 0)),
            ),
        ),
        out_shape=(
            jax.ShapeDtypeStruct((2 * half_rows, feat), F32),
            jax.ShapeDtypeStruct((slots, 2 * half_rows, feat), F32),
        ),
        input_output_aliases={2 + i: i for i in range(len(earlier))},
        compiler_params=params(),
        name="place",
    )(part, answers, *earlier)


def local(axes, blocks, features, col_ids, row_ids, factor):
    half_axis, peer_axes = axes[0], axes[1:]
    slots, rows, _ = blocks.shape
    feat = features.shape[2]
    peers = lax.axis_size(peer_axes)
    row_blocks = peers * lax.axis_size(half_axis)
    here = lax.axis_index(half_axis).astype(I32).reshape(1)
    there = 1 - here
    swap = [(0, 1), (1, 0)]
    exchange = lambda pieces: lax.all_to_all(pieces, peer_axes, 0, 0)

    far = exchange(product(blocks, features, col_ids, row_ids, there, peers, True))
    near = exchange(product(blocks, features, col_ids, row_ids, here, peers, False))
    far_sums, ids = sum_pieces(far, row_blocks, slots)
    got = lax.ppermute(far_sums, half_axis, swap)
    near_rows = update(ids, near, got, factor, slots)
    far_rows = lax.ppermute(near_rows, half_axis, swap)
    near_answers = exchange(answer(ids, here, near_rows, peers, slots))
    far_answers = exchange(answer(ids, here, far_rows, peers, slots))
    outputs = place(here, near_answers, slots)
    owned_rows, returned = place(there, far_answers, slots, outputs)
    return owned_rows, returned.reshape(slots * rows, feat)


def solution(mesh):
    outer, inner = mesh.devices.shape
    devices = mesh.devices.reshape(2, outer // 2, inner)
    axes = ("half", "gx_low", "gy")
    split_mesh = Mesh(devices, axes)
    return jax.shard_map(
        functools.partial(local, axes),
        mesh=split_mesh,
        in_specs=(P(axes, None, None), P(axes, None, None), P(axes, None), P(axes), P()),
        out_specs=(P(axes, None), P(axes, None)),
        check_vma=False,
    )
```

time: 114 us -> 107 us (0.939)
  blocking collectives: 54.1 us -> 0 us
  waiting for transfers between devices: 22.7 us -> 45.5 us
  starting transfers between devices: 9.14 us -> 24.1 us
  Pallas kernels: 19.9 us -> 30.2 us
    all_to_all x1 -> x4, waiting for transfers between devices: 0.01 us -> 31 us  [local(): exchange = lambda pieces: lax.all_to_all(pieces, peer_axes, 0, 0)]
    all_to_all x1 -> x0, blocking collectives: 27.9 us -> none  [local(): answers = lax.all_to_all(answers, peer_axes, 0, 0)]
    unnamed x1 -> x0, blocking collectives: 26.2 us -> none
    all_to_all x1 -> x4, starting transfers between devices: 6.42 us -> 19.4 us  [local(): exchange = lambda pieces: lax.all_to_all(pieces, peer_axes, 0, 0)]
    pallas_call x4 -> x8, Pallas kernels: 19.9 us -> 30.2 us  [the longest x2 21 us: product(): pl.pallas_call(functools.partial(product_kernel, with_ids), grid_spec=plt...]
    ppermute x2, waiting for transfers between devices: 22.7 us -> 14.4 us  [the longest x1 14.4 us: local(): far_rows = lax.ppermute(near_rows, half_axis, swap)]
    unnamed x13 -> x14, local copies, waits for them, and re-layouts: 3.71 us -> 5.72 us
    ppermute x2, starting transfers between devices: 2.72 us -> 4.65 us  [the longest x1 2.63 us: local(): got = lax.ppermute(far_sums, half_axis, swap)]
  transfers between devices with their start and end apart: 3 -> 6, of which waited for: 2 -> 5; matrix products, arithmetic and copies ran while one was open for 1% -> 0% of each run, Pallas kernels for 0% -> 15%
where the time goes in v2:
time: 107 us; the launch traced here: 106 us
  waiting for transfers between devices  45.5 us (43%)
  Pallas kernels  30.2 us (28%)
  starting transfers between devices  24.1 us (23%)
  local copies, waits for them, and re-layouts  5.72 us (5%)
    all_to_all x4, waiting for transfers between devices, local(): exchange = lambda pieces: lax.all_to_all(pieces, peer_axes, 0, 0)  31 us
    pallas_call x2, Pallas kernels, product(): pl.pallas_call(functools.partial(product_kernel, with_ids), grid_spec=plt...  21 us
    all_to_all x4, starting transfers between devices, local(): exchange = lambda pieces: lax.all_to_all(pieces, peer_axes, 0, 0)  19.4 us
    ppermute x1, waiting for transfers between devices, local(): far_rows = lax.ppermute(near_rows, half_axis, swap)  14.4 us
    unnamed x14, local copies, waits for them, and re-layouts  5.72 us
    pallas_call x2, Pallas kernels, answer(): pl.pallas_call(functools.partial(answer_kernel, slots), in_specs=[spec(pl...  3.35 us
    ppermute x1, starting transfers between devices, local(): got = lax.ppermute(far_sums, half_axis, swap)  2.63 us
    pallas_call x2, Pallas kernels, place(): pl.pallas_call(functools.partial(place_kernel, slots), grid_spec=pltpu.Pr...  2.2 us
  transfers between devices with their start and end apart: 6, of which 5 were waited for; matrix products, arithmetic and copies ran while one was open for 0% of the time, Pallas kernels for 15%

profile of v2, /device:TPU:0, one launch (start us, length us, event | category | flops | bytes accessed | tf_op | source)
XLA Modules:
  0.0 106.2 jit_solution(16740553345140305955)
XLA Ops:
  0.6 0.0 copy-start
  0.6 2.2 %copy-done = f32[16,128,512]{2,1,0:T(8,128)S(1)} copy-done((f32[16,128,512]{2,1,0:T(8,128)S(1)}, f32[16,128,512]{2,1,0:T(8,128)}, u32[]{:S(2)}) %copy-start) | copy-done | bytes 4194328
  2.8 0.0 copy-start.3
  2.8 0.7 copy-done.3
  3.5 0.0 copy-start.5
  3.5 0.7 copy-done.5
  4.2 0.0 copy-start.4
  4.2 10.5 %product.2 = f32[16,25,4,128]{3,2,1,0:T(4,128)} custom-call(s32[1]{0:T(128)S(6)} %sub.3.part_ref, s32[6]{0:T(128)S(1)} %copy-done.5, f32[6,128,4096]{2,1,0:T(8,128)} %blocks_ref.3, s32[6,32]{1,0:T(8,128)S(1)} %copy-done.3, f32[16,128,512]{2,1,0:T(8,128)S(1)} %copy-done), custom_call_target="tpu_custom_call" | custom-call | flops 2415919104 | bytes 10485760 | tf_op jit(solution)/shard_map/product/pallas_call | solution.py:98
  14.7 6.3 %all-to-all-start = ((f32[16,25,4,128]{3,2,1,0:T(4,128)}), f32[16,25,4,128]{3,2,1,0:T(4,128)S(1)}, u32[]{:S(2)}, u32[]{:S(2)}) async-start(f32[16,25,4,128]{3,2,1,0:T(4,128)} %product.2), calls=%async_computation | async-start | bytes 1638400 | tf_op jit(solution)/shard_map/all_to_all | solution.py:283
  21.0 0.0 copy-done.4
  21.0 0.0 copy-done.6
  21.0 0.0 copy-start.1
  21.0 2.2 %copy-done.1 = f32[16,128,512]{2,1,0:T(8,128)S(1)} copy-done((f32[16,128,512]{2,1,0:T(8,128)S(1)}, f32[16,128,512]{2,1,0:T(8,128)}, u32[]{:S(2)}) %copy-start.1) | copy-done | bytes 4194328
  23.2 10.5 %product.3 = f32[16,24,4,128]{3,2,1,0:T(4,128)} custom-call(s32[1]{0:T(128)} %bitcast.part_ref.half_ref, s32[6]{0:T(128)S(1)} %copy-done.6, f32[6,128,4096]{2,1,0:T(8,128)} %blocks_ref.3, s32[6,32]{1,0:T(8,128)S(1)} %copy-done.4, f32[16,128,512]{2,1,0:T(8,128)S(1)} %copy-done.1), custom_call_target="tpu_custom_call" | custom-call | flops 2415919104 | bytes 10485760 | tf_op jit(solution)/shard_map/product/pallas_call | solution.py:98
  33.7 1.0 all-to-all-done.pieces_ref
  34.7 4.2 %all-to-all-start.1 = ((f32[16,24,4,128]{3,2,1,0:T(4,128)}), f32[16,24,4,128]{3,2,1,0:T(4,128)S(1)}, u32[]{:S(2)}, u32[]{:S(2)}) async-start(f32[16,24,4,128]{3,2,1,0:T(4,128)} %product.3), calls=%async_computation.1 | async-start | bytes 1572864 | tf_op jit(solution)/shard_map/all_to_all | solution.py:283
  38.9 2.2 %sum_pieces.1 = (f32[32,4,4,128]{3,2,1,0:T(4,128)S(1)}, s32[96]{0:T(128)S(1)}) custom-call(f32[16,25,4,128]{3,2,1,0:T(4,128)S(1)} %all-to-all-done.pieces_ref), custom_call_target="tpu_custom_call" | custom-call | tf_op jit(solution)/shard_map/sum_pieces/pallas_call | solution.py:152
  41.1 2.6 %collective-permute-start = (f32[32,4,4,128]{3,2,1,0:T(4,128)S(1)}, f32[32,4,4,128]{3,2,1,0:T(4,128)S(1)}, u32[]{:S(2)}, u32[]{:S(2)}) collective-permute-start(f32[32,4,4,128]{3,2,1,0:T(4,128)S(1)} %get-tuple-element.9), channel_id=1, source_target_pairs={{0,16},{16,0},{1,17},{17,1},{2,18},{18,2},{3,19},{19,3},{4,20},{20... | collective-permute-start | bytes 786440 | tf_op jit(solution)/shard_map/ppermute | solution.py:288
  43.7 14.1 %all-to-all-done.1.pieces_ref = f32[16,24,4,128]{3,2,1,0:T(4,128)S(1)} async-done(((f32[16,24,4,128]{3,2,1,0:T(4,128)}), f32[16,24,4,128]{3,2,1,0:T(4,128)S(1)}, u32[]{:S(2)}, u32[]{:S(2)}) %all-to-all-start.1) | async-done | bytes 786464 | tf_op jit(solution)/shard_map/all_to_all | solution.py:283
  57.9 0.0 collective-permute-done.got_ref
  57.9 0.0 copy-done.2
  57.9 1.4 %update.1.table_ref = f32[32,4,4,128]{3,2,1,0:T(4,128)S(1)} custom-call(s32[96]{0:T(128)S(1)} %get-tuple-element.8.ids_ref, f32[16,24,4,128]{3,2,1,0:T(4,128)S(1)} %all-to-all-done.1.pieces_ref, f32[32,4,4,128]{3,2,1,0:T(4,128)S(1)} %collective-permute-done.got_ref, f32[512,512]{1,0:T(8,128)S(1)} %copy-done.2), custom_call_target="tpu_custom_call" | custom-call | tf_op jit(solution)/shard_map/update/pallas_call | solution.py:189
  59.3 1.7 %answer.3 = f32[16,28,4,128]{3,2,1,0:T(4,128)} custom-call(s32[96]{0:T(128)S(1)} %get-tuple-element.8.ids_ref, s32[1]{0:T(128)} %bitcast.part_ref.half_ref, f32[32,4,4,128]{3,2,1,0:T(4,128)S(1)} %update.1.table_ref), custom_call_target="tpu_custom_call" | custom-call | tf_op jit(solution)/shard_map/answer/pallas_call | solution.py:220
  61.0 3.9 %all-to-all-start.3 = ((f32[16,28,4,128]{3,2,1,0:T(4,128)}), f32[16,28,4,128]{3,2,1,0:T(4,128)S(1)}, u32[]{:S(2)}, u32[]{:S(2)}) async-start(f32[16,28,4,128]{3,2,1,0:T(4,128)} %answer.3), calls=%async_computation.3 | async-start | bytes 1835008 | tf_op jit(solution)/shard_map/all_to_all | solution.py:283
  64.9 2.0 %collective-permute-start.1 = (f32[32,4,4,128]{3,2,1,0:T(4,128)S(1)}, f32[32,4,4,128]{3,2,1,0:T(4,128)S(1)}, u32[]{:S(2)}, u32[]{:S(2)}) collective-permute-start(f32[32,4,4,128]{3,2,1,0:T(4,128)S(1)} %update.1.table_ref), channel_id=1, source_target_pairs={{0,16},{16,0},{1,17},{17,1},{2,18},{18,2},{3,19},{19,3},{4,20},{20... | collective-permute-start | bytes 786440 | tf_op jit(solution)/shard_map/ppermute | solution.py:290
  67.0 14.4 %collective-permute-done.1.table_ref = f32[32,4,4,128]{3,2,1,0:T(4,128)S(1)} collective-permute-done((f32[32,4,4,128]{3,2,1,0:T(4,128)S(1)}, f32[32,4,4,128]{3,2,1,0:T(4,128)S(1)}, u32[]{:S(2)}, u32[]{:S(2)}) %collective-permute-start.1) | collective-permute-done | bytes 262176 | tf_op jit(solution)/shard_map/ppermute | solution.py:290
  81.4 1.7 %answer.2 = f32[16,28,4,128]{3,2,1,0:T(4,128)} custom-call(s32[96]{0:T(128)S(1)} %get-tuple-element.8.ids_ref, s32[1]{0:T(128)} %bitcast.part_ref.half_ref, f32[32,4,4,128]{3,2,1,0:T(4,128)S(1)} %collective-permute-done.1.table_ref), custom_call_target="tpu_custom_call" | custom-call | tf_op jit(solution)/shard_map/answer/pallas_call | solution.py:220
  83.1 2.2 %all-to-all-done.3.answers_ref = f32[16,28,4,128]{3,2,1,0:T(4,128)S(1)} async-done(((f32[16,28,4,128]{3,2,1,0:T(4,128)}), f32[16,28,4,128]{3,2,1,0:T(4,128)S(1)}, u32[]{:S(2)}, u32[]{:S(2)}) %all-to-all-start.3) | async-done | bytes 917536 | tf_op jit(solution)/shard_map/all_to_all | solution.py:283
  85.3 5.0 %all-to-all-start.2 = ((f32[16,28,4,128]{3,2,1,0:T(4,128)}), f32[16,28,4,128]{3,2,1,0:T(4,128)S(1)}, u32[]{:S(2)}, u32[]{:S(2)}) async-start(f32[16,28,4,128]{3,2,1,0:T(4,128)} %answer.2), calls=%async_computation.2 | async-start | bytes 1835008 | tf_op jit(solution)/shard_map/all_to_all | solution.py:283
  90.3 1.1 %place.2 = (f32[128,512]{1,0:T(8,128)}, f32[6,128,512]{2,1,0:T(8,128)}) custom-call(s32[1]{0:T(128)} %bitcast.part_ref.half_ref, f32[16,28,4,128]{3,2,1,0:T(4,128)S(1)} %all-to-all-done.3.answers_ref), custom_call_target="tpu_custom_call" | custom-call | tf_op jit(solution)/shard_map/place/pallas_call | solution.py:252
  91.4 13.7 %all-to-all-done.2.answers_ref = f32[16,28,4,128]{3,2,1,0:T(4,128)S(1)} async-done(((f32[16,28,4,128]{3,2,1,0:T(4,128)}), f32[16,28,4,128]{3,2,1,0:T(4,128)S(1)}, u32[]{:S(2)}, u32[]{:S(2)}) %all-to-all-start.2) | async-done | bytes 917536 | tf_op jit(solution)/shard_map/all_to_all | solution.py:283
  105.1 1.1 %place.3 = (f32[128,512]{1,0:T(8,128)}, f32[6,128,512]{2,1,0:T(8,128)}) custom-call(s32[1]{0:T(128)S(6)} %sub.3.part_ref, f32[16,28,4,128]{3,2,1,0:T(4,128)S(1)} %all-to-all-done.2.answers_ref, f32[128,512]{1,0:T(8,128)} %get-tuple-element.10.refs_0_, f32[6,128,512]{2,1,0:T(8,128)} %get-tuple-element.11.refs_1_), custom_call_target="tpu_custom_call", output_to_operand_aliasing={{0}: (2, {}), {1}: (3, {})} | custom-call | tf_op jit(solution)/shard_map/place/pallas_call | solution.py:252
  (2 shorter events, 0.0 us)
Async XLA Ops:
  0.6 2.2 %copy-start = (f32[16,128,512]{2,1,0:T(8,128)S(1)}, f32[16,128,512]{2,1,0:T(8,128)}, u32[]{:S(2)}) copy-start(f32[16,128,512]{2,1,0:T(8,128)} %features_hbm.3) | copy-start | bytes 12582916
  2.8 0.7 copy-start.3
  3.5 0.7 copy-start.5
  4.2 16.8 %copy-start.4 = (s32[6,32]{1,0:T(8,128)S(1)}, s32[6,32]{1,0:T(8,128)}, u32[]{:S(2)}) copy-start(s32[6,32]{1,0:T(8,128)} %cols_hbm.3) | copy-start | bytes 2308
  4.2 16.9 %copy-start.6 = (s32[6]{0:T(128)S(1)}, s32[6]{0:T(128)}, u32[]{:S(2)}) copy-start(s32[6]{0:T(128)} %ids_ref.3) | copy-start | bytes 76
  14.7 20.0 %all-to-all-start = ((f32[16,25,4,128]{3,2,1,0:T(4,128)}), f32[16,25,4,128]{3,2,1,0:T(4,128)S(1)}, u32[]{:S(2)}, u32[]{:S(2)}) async-start(f32[16,25,4,128]{3,2,1,0:T(4,128)} %product.2), calls=%async_computation | async-start | bytes 1638400 | tf_op jit(solution)/shard_map/all_to_all | solution.py:283
  21.0 2.2 %copy-start.1 = (f32[16,128,512]{2,1,0:T(8,128)S(1)}, f32[16,128,512]{2,1,0:T(8,128)}, u32[]{:S(2)}) copy-start(f32[16,128,512]{2,1,0:T(8,128)} %features_hbm.3) | copy-start | bytes 12582916
  23.2 34.6 %copy-start.2 = (f32[512,512]{1,0:T(8,128)S(1)}, f32[512,512]{1,0:T(8,128)}, u32[]{:S(2)}) copy-start(f32[512,512]{1,0:T(8,128)} %factor_ref.1) | copy-start | bytes 3145732
  34.7 23.1 %all-to-all-start.1 = ((f32[16,24,4,128]{3,2,1,0:T(4,128)}), f32[16,24,4,128]{3,2,1,0:T(4,128)S(1)}, u32[]{:S(2)}, u32[]{:S(2)}) async-start(f32[16,24,4,128]{3,2,1,0:T(4,128)} %product.3), calls=%async_computation.1 | async-start | bytes 1572864 | tf_op jit(solution)/shard_map/all_to_all | solution.py:283
  41.1 16.8 %collective-permute-start = (f32[32,4,4,128]{3,2,1,0:T(4,128)S(1)}, f32[32,4,4,128]{3,2,1,0:T(4,128)S(1)}, u32[]{:S(2)}, u32[]{:S(2)}) collective-permute-start(f32[32,4,4,128]{3,2,1,0:T(4,128)S(1)} %get-tuple-element.9), channel_id=1, source_target_pairs={{0,16},{16,0},{1,17},{17,1},{2,18},{18,2},{3,19},{19,3},{4,20},{20... | collective-permute-start | bytes 786440 | tf_op jit(solution)/shard_map/ppermute | solution.py:288
  61.0 24.3 %all-to-all-start.3 = ((f32[16,28,4,128]{3,2,1,0:T(4,128)}), f32[16,28,4,128]{3,2,1,0:T(4,128)S(1)}, u32[]{:S(2)}, u32[]{:S(2)}) async-start(f32[16,28,4,128]{3,2,1,0:T(4,128)} %answer.3), calls=%async_computation.3 | async-start | bytes 1835008 | tf_op jit(solution)/shard_map/all_to_all | solution.py:283
  64.9 16.5 %collective-permute-start.1 = (f32[32,4,4,128]{3,2,1,0:T(4,128)S(1)}, f32[32,4,4,128]{3,2,1,0:T(4,128)S(1)}, u32[]{:S(2)}, u32[]{:S(2)}) collective-permute-start(f32[32,4,4,128]{3,2,1,0:T(4,128)S(1)} %update.1.table_ref), channel_id=1, source_target_pairs={{0,16},{16,0},{1,17},{17,1},{2,18},{18,2},{3,19},{19,3},{4,20},{20... | collective-permute-start | bytes 786440 | tf_op jit(solution)/shard_map/ppermute | solution.py:290
  85.3 19.8 %all-to-all-start.2 = ((f32[16,28,4,128]{3,2,1,0:T(4,128)}), f32[16,28,4,128]{3,2,1,0:T(4,128)S(1)}, u32[]{:S(2)}, u32[]{:S(2)}) async-start(f32[16,28,4,128]{3,2,1,0:T(4,128)} %answer.2), calls=%async_computation.2 | async-start | bytes 1835008 | tf_op jit(solution)/shard_map/all_to_all | solution.py:283

commit v3 on v2

v3 whole, which is shorter than its diff:
```python
import functools

import jax
import jax.numpy as jnp
from jax import lax
from jax.experimental import pallas as pl
from jax.experimental.pallas import tpu as pltpu
from jax.sharding import Mesh
from jax.sharding import PartitionSpec as P

F32 = jnp.float32
BF16 = jnp.bfloat16
I32 = jnp.int32
LANES = 128
VMEM_BYTES = 24 << 20
PRODUCT_VMEM_BYTES = 60 << 20


def split(value):
    high = value.astype(BF16)
    return high, (value - high.astype(F32)).astype(BF16)


def dot3(a_high, a_low, b_high, b_low):
    dot = functools.partial(jnp.dot, preferred_element_type=F32)
    return dot(a_high, b_high) + dot(a_high, b_low) + dot(a_low, b_high)


def spec(space):
    return pl.BlockSpec(memory_space=space)


def params(vmem_bytes=VMEM_BYTES):
    return pltpu.CompilerParams(vmem_limit_bytes=vmem_bytes)


def product_kernel(
    with_ids, groups, feature_parts, part_ref, blocks_hbm, ids_hbm, cols_hbm, features_hbm, out_ref,
    blocks, total, left, f_high, f_low, features, ids, cols, block_sems, feature_sems, id_sems,
):
    slots, per_row = cols.shape
    tiles, depth, feat = features.shape
    rows = blocks.shape[1]
    peers, _, piece_rows, _ = out_ref.shape
    in_group = slots // groups
    height = in_group * rows
    part_tiles = tiles // feature_parts
    first = pl.multiple_of(part_ref[0] * rows, rows)
    block_copies = [
        pltpu.make_async_copy(
            blocks_hbm.at[k, pl.ds(first, rows)], blocks.at[k], block_sems.at[k]
        )
        for k in range(slots)
    ]
    feature_copies = [
        pltpu.make_async_copy(
            features_hbm.at[pl.ds(k * part_tiles, part_tiles)],
            features.at[pl.ds(k * part_tiles, part_tiles)],
            feature_sems.at[k],
        )
        for k in range(feature_parts)
    ]
    id_copies = [
        pltpu.make_async_copy(cols_hbm, cols, id_sems.at[0]),
        pltpu.make_async_copy(ids_hbm, ids, id_sems.at[1]),
    ]
    for copy in id_copies + block_copies[:in_group] + feature_copies + block_copies[in_group:]:
        copy.start()
    for copy in id_copies:
        copy.wait()

    def combine(group):
        for s in range(in_group):
            slot = group * in_group + s
            block_copies[slot].wait()
            total[s] = jnp.zeros_like(total[s])
            for j in range(per_row):
                tile = cols[slot, j]
                total[s, tile] = total[s, tile] + blocks[slot, :, j * depth : (j + 1) * depth]
            for tile in range(tiles):
                high, low = split(total[s, tile])
                cut = slice(tile * depth, (tile + 1) * depth)
                left[group % 2, s * rows : (s + 1) * rows, cut] = high
                left[group % 2, height + s * rows : height + (s + 1) * rows, cut] = low

    def multiply(group):
        width = min(feat, 2 * LANES)
        dot = functools.partial(jnp.dot, preferred_element_type=F32)
        for n in range(0, feat, width):
            cut = slice(n, n + width)
            both = dot(left[group % 2], f_high[:, cut])
            both = both[:height] + both[height:] + dot(left[group % 2, :height], f_low[:, cut])
            for s in range(in_group):
                for t in range(0, width, LANES):
                    piece = both[s * rows : (s + 1) * rows, t : t + LANES]
                    place = ((group * in_group + s) * feat + n + t) // LANES
                    out_ref[:, place] = piece.reshape(peers, piece_rows, LANES)

    def split_tile(tile, carry):
        high, low = split(features[tile])
        here = pl.ds(pl.multiple_of(tile * depth, depth), depth)
        f_high[here, :] = high
        f_low[here, :] = low
        return carry

    combine(0)
    for k in range(feature_parts):
        feature_copies[k].wait()
        lax.fori_loop(k * part_tiles, (k + 1) * part_tiles, split_tile, 0)
    for group in range(groups):
        if group + 1 < groups:
            combine(group + 1)
        multiply(group)
    if with_ids:
        lane = lax.broadcasted_iota(I32, (peers, piece_rows, LANES), 2)
        shown = jnp.zeros((peers, piece_rows, LANES), I32)
        for slot in range(slots):
            shown = jnp.where(lane == slot, ids[slot], shown)
        out_ref[:, slots * feat // LANES] = shown.astype(F32)


def product(blocks, features, col_ids, row_ids, part, peers, with_ids):
    slots, rows, width = blocks.shape
    tiles, depth, feat = features.shape
    rows //= 2
    groups = 2 if slots % 2 == 0 else 1
    feature_parts = 4 if tiles % 4 == 0 else 1
    height = slots // groups * rows
    out = (peers, slots * feat // LANES + int(with_ids), rows // peers, LANES)
    return pl.pallas_call(
        functools.partial(product_kernel, with_ids, groups, feature_parts),
        in_specs=[spec(pltpu.SMEM)] + [spec(pltpu.HBM)] * 4,
        out_specs=spec(pltpu.VMEM),
        out_shape=jax.ShapeDtypeStruct(out, F32),
        scratch_shapes=[
            pltpu.VMEM((slots, rows, width), F32),
            pltpu.VMEM((slots // groups, tiles, rows, depth), F32),
            pltpu.VMEM((2, 2 * height, tiles * depth), BF16),
            pltpu.VMEM((tiles * depth, feat), BF16),
            pltpu.VMEM((tiles * depth, feat), BF16),
            pltpu.VMEM(features.shape, F32),
            pltpu.SMEM(row_ids.shape, I32),
            pltpu.SMEM(col_ids.shape, I32),
            pltpu.SemaphoreType.DMA((slots,)),
            pltpu.SemaphoreType.DMA((feature_parts,)),
            pltpu.SemaphoreType.DMA((2,)),
        ],
        compiler_params=params(PRODUCT_VMEM_BYTES),
        cost_estimate=pl.CostEstimate(
            flops=6 * slots * rows * tiles * depth * feat,
            bytes_accessed=4 * (slots * rows * width + tiles * depth * feat),
            transcendentals=0,
        ),
        name="product",
    )(part, blocks, row_ids, col_ids, features)


def sum_kernel(slots, pieces_ref, out_ref, ids_out, ids, sem):
    peers, places = pieces_ref.shape[:2]
    tiles = out_ref.shape[1]
    ids_copy = pltpu.make_async_copy(pieces_ref.at[:, places - 1], ids, sem)
    ids_copy.start()
    out_ref[...] = jnp.zeros_like(out_ref)
    ids_copy.wait()

    def add_peer(peer, carry):
        for slot in range(slots):
            row = ids[peer, 0, slot].astype(I32)
            ids_out[peer * slots + slot] = row
            out_ref[row] = out_ref[row] + pieces_ref[peer, slot * tiles : (slot + 1) * tiles]
        return carry

    lax.fori_loop(0, peers, add_peer, 0)


def sum_pieces(pieces, row_blocks, slots):
    peers, places, rows, _ = pieces.shape
    tiles = (places - 1) // slots
    return pl.pallas_call(
        functools.partial(sum_kernel, slots),
        in_specs=[spec(pltpu.VMEM)],
        out_specs=(spec(pltpu.VMEM), spec(pltpu.SMEM)),
        out_shape=(
            jax.ShapeDtypeStruct((row_blocks, tiles, rows, LANES), F32),
            jax.ShapeDtypeStruct((peers * slots,), I32),
        ),
        scratch_shapes=[pltpu.SMEM((peers, rows, LANES), F32), pltpu.SemaphoreType.DMA],
        compiler_params=params(),
        name="sum_pieces",
    )(pieces)


def update_kernel(slots, ids_ref, pieces_ref, got_ref, factor_ref, out_ref, total, left):
    peers = pieces_ref.shape[0]
    row_blocks, tiles, rows, _ = out_ref.shape
    total[...] = got_ref[...]

    def add_peer(peer, carry):
        for slot in range(slots):
            row = ids_ref[peer * slots + slot]
            total[row] = total[row] + pieces_ref[peer, slot * tiles : (slot + 1) * tiles]
        return carry

    lax.fori_loop(0, peers, add_peer, 0)
    for row in range(row_blocks):
        for t in range(tiles):
            left[row * rows : (row + 1) * rows, t * LANES : (t + 1) * LANES] = total[row, t]
    out = dot3(*split(jnp.tanh(left[...])), *split(factor_ref[...]))
    for row in range(row_blocks):
        for t in range(tiles):
            out_ref[row, t] = out[row * rows : (row + 1) * rows, t * LANES : (t + 1) * LANES]


def update(ids, pieces, got, factor, slots):
    row_blocks, tiles, rows, _ = got.shape
    return pl.pallas_call(
        functools.partial(update_kernel, slots),
        in_specs=[spec(pltpu.SMEM), spec(pltpu.VMEM), spec(pltpu.VMEM), spec(pltpu.VMEM)],
        out_specs=spec(pltpu.VMEM),
        out_shape=jax.ShapeDtypeStruct(got.shape, F32),
        scratch_shapes=[
            pltpu.VMEM(got.shape, F32),
            pltpu.VMEM((row_blocks * rows, tiles * LANES), F32),
        ],
        compiler_params=params(),
        name="update",
    )(ids, pieces, got, factor)


def answer_kernel(slots, ids_ref, self_ref, mine_ref, mate_ref, *refs):
    out_ref, table = refs[-2:]
    chips = out_ref.shape[0]
    _, tiles, rows, _ = mine_ref.shape
    core, first = self_ref[1], self_ref[0] * chips * 2
    mine, mate = mine_ref[...], mate_ref[...]
    table[:, :, :rows] = jnp.where(core == 0, mine, mate)
    table[:, :, rows:] = jnp.where(core == 0, mate, mine)

    def pick(chip, carry):
        peer = chip * 2 + core
        for slot in range(slots):
            row = ids_ref[peer * slots + slot]
            out_ref[chip, 0, slot * tiles : (slot + 1) * tiles] = table[row]
        out_ref[chip, 0, slots * tiles :] = table[first + peer]
        return carry

    lax.fori_loop(0, chips, pick, 0)


def answer(ids, self_at, mine, mate, chips, slots, part, cost_bytes, earlier=()):
    row_blocks, tiles, rows, _ = mine.shape
    places = (slots + 1) * tiles
    block = (chips, 1, places, 2 * rows, LANES)
    return pl.pallas_call(
        functools.partial(answer_kernel, slots),
        in_specs=[spec(pltpu.SMEM), spec(pltpu.SMEM), spec(pltpu.VMEM), spec(pltpu.VMEM)]
        + [spec(pltpu.HBM)] * len(earlier),
        grid=(1,),
        out_specs=pl.BlockSpec(block, lambda i: (0, part, 0, 0, 0)),
        out_shape=jax.ShapeDtypeStruct((chips, 2, places, 2 * rows, LANES), F32),
        scratch_shapes=[pltpu.VMEM((row_blocks, tiles, 2 * rows, LANES), F32)],
        input_output_aliases={4 + i: i for i in range(len(earlier))},
        compiler_params=params(),
        cost_estimate=pl.CostEstimate(
            flops=cost_bytes << 14, bytes_accessed=cost_bytes, transcendentals=0
        ),
        name="answer",
    )(ids, self_at, mine, mate, *earlier)


def place_kernel(slots, parts_ref, answers_ref, owned_ref, returned_ref):
    chips, _, places, rows, _ = answers_ref.shape
    tiles = places // (slots + 1)
    for chip in range(chips):
        here = pl.ds(chip * rows, rows)
        for t in range(tiles):
            cut = slice(t * LANES, (t + 1) * LANES)
            for slot in range(slots):
                returned_ref[slot, here, cut] = answers_ref[chip, 0, slot * tiles + t]
            owned_ref[here, cut] = answers_ref[chip, 0, slots * tiles + t]


def place(parts, answers, slots):
    chips, _, places, rows, _ = answers.shape
    feat = places // (slots + 1) * LANES
    half_rows = chips * rows
    return pl.pallas_call(
        functools.partial(place_kernel, slots),
        grid_spec=pltpu.PrefetchScalarGridSpec(
            num_scalar_prefetch=1,
            grid=(2,),
            in_specs=[
                pl.BlockSpec((chips, 1, places, rows, LANES), lambda i, parts: (0, i, 0, 0, 0))
            ],
            out_specs=(
                pl.BlockSpec((half_rows, feat), lambda i, parts: (parts[i], 0)),
                pl.BlockSpec((slots, half_rows, feat), lambda i, parts: (0, parts[i], 0)),
            ),
        ),
        out_shape=(
            jax.ShapeDtypeStruct((2 * half_rows, feat), F32),
            jax.ShapeDtypeStruct((slots, 2 * half_rows, feat), F32),
        ),
        compiler_params=params(),
        name="place",
    )(parts, answers)


def local(blocks, features, col_ids, row_ids, factor):
    slots, rows, _ = blocks.shape
    feat = features.shape[2]
    chips = lax.axis_size("chip")
    peer_axes = ("chip", "core")
    peers = lax.axis_size(peer_axes)
    row_blocks = peers * lax.axis_size("half")
    half = lax.axis_index("half").astype(I32)
    here = half.reshape(1)
    there = 1 - here
    parts = jnp.concatenate([here, there])
    self_at = jnp.stack([half, lax.axis_index("core").astype(I32)])
    swap = [(0, 1), (1, 0)]
    parts, self_at, row_ids = lax.optimization_barrier((parts, self_at, row_ids))

    far = product(blocks, features, col_ids, row_ids, there, peers, True)
    far = lax.all_to_all(far, peer_axes, 0, 0)
    near = product(blocks, features, col_ids, row_ids, here, peers, False)
    near = lax.all_to_all(near, peer_axes, 0, 0)
    far_sums, ids = sum_pieces(far, row_blocks, slots)
    got = lax.ppermute(far_sums, "half", swap)
    near_rows = update(ids, near, got, factor, slots)

    far_rows = lax.ppermute(near_rows, "half", swap)
    near_mate = lax.ppermute(near_rows, "core", swap)
    answers = answer(ids, self_at, near_rows, near_mate, chips, slots, 0, 1 << 22)
    far_mate = lax.ppermute(far_rows, "core", swap)
    answers = answer(ids, self_at, far_rows, far_mate, chips, slots, 1, 1 << 20, (answers,))
    answers = lax.all_to_all(answers, "chip", 0, 0)
    owned_rows, returned = place(parts, answers, slots)
    return owned_rows, returned.reshape(slots * rows, feat)


def solution(mesh):
    devices = mesh.devices.reshape(2, mesh.devices.size // 4, 2)
    axes = ("half", "chip", "core")
    split_mesh = Mesh(devices, axes)
    return jax.shard_map(
        local,
        mesh=split_mesh,
        in_specs=(P(axes, None, None), P(axes, None, None), P(axes, None), P(axes), P()),
        out_specs=(P(axes, None), P(axes, None)),
        check_vma=False,
    )
```

time: 107 us -> 98.5 us (0.921)
  blocking collectives: 0 us -> 26.5 us
  starting transfers between devices: 24.1 us -> 12.7 us
  waiting for transfers between devices: 45.5 us -> 34.6 us
  Pallas kernels: 30.2 us -> 23.6 us
  local copies, waits for them, and re-layouts: 5.72 us -> 0.01 us
    all_to_all x0 -> x1, blocking collectives: none -> 26.5 us  [local(): answers = lax.all_to_all(answers, 'chip', 0, 0)]
    all_to_all x4 -> x2, waiting for transfers between devices: 31 us -> 19.6 us  [the longest x1 14.1 us: local(): near = lax.all_to_all(near, peer_axes, 0, 0)]
    all_to_all x4 -> x2, starting transfers between devices: 19.4 us -> 9.91 us  [the longest x1 6.3 us: local(): far = lax.all_to_all(far, peer_axes, 0, 0)]
    unnamed x14 -> x2, local copies, waits for them, and re-layouts: 5.72 us -> 0.01 us
    pallas_call x2, Pallas kernels: 21 us -> 16.4 us  [product(): pl.pallas_call(functools.partial(product_kernel, with_ids, groups, featur...]
    ppermute x2 -> x4, starting transfers between devices: 4.65 us -> 2.8 us  [the longest x1 2.65 us: local(): got = lax.ppermute(far_sums, 'half', swap)]
    pallas_call x2, Pallas kernels: 3.35 us -> 1.61 us  [answer(): pl.pallas_call(functools.partial(answer_kernel, slots), in_specs=[spec(pl...]
    ppermute x2 -> x4, waiting for transfers between devices: 14.4 us -> 15 us  [the longest x1 14.3 us: local(): far_rows = lax.ppermute(near_rows, 'half', swap)]
  transfers between devices with their start and end apart: 6 -> 6, of which waited for: 5 -> 4; matrix products, arithmetic and copies ran while one was open for 0% -> 0% of each run, Pallas kernels for 15% -> 11%
where the time goes in v3:
time: 98.5 us; the launch traced here: 98.2 us
  waiting for transfers between devices  34.6 us (35%)
  blocking collectives  26.5 us (27%)
  Pallas kernels  23.6 us (24%)
  starting transfers between devices  12.7 us (13%)
    all_to_all x1, blocking collectives, local(): answers = lax.all_to_all(answers, 'chip', 0, 0)  26.5 us
    pallas_call x2, Pallas kernels, product(): pl.pallas_call(functools.partial(product_kernel, with_ids, groups, featur...  16.4 us
    ppermute x1, waiting for transfers between devices, local(): far_rows = lax.ppermute(near_rows, 'half', swap)  14.3 us
    all_to_all x1, waiting for transfers between devices, local(): near = lax.all_to_all(near, peer_axes, 0, 0)  14.1 us
    all_to_all x1, starting transfers between devices, local(): far = lax.all_to_all(far, peer_axes, 0, 0)  6.3 us
    all_to_all x1, waiting for transfers between devices, local(): far = lax.all_to_all(far, peer_axes, 0, 0)  5.5 us
    all_to_all x1, starting transfers between devices, local(): near = lax.all_to_all(near, peer_axes, 0, 0)  3.61 us
    ppermute x1, starting transfers between devices, local(): got = lax.ppermute(far_sums, 'half', swap)  2.65 us
  transfers between devices with their start and end apart: 6, of which 4 were waited for; matrix products, arithmetic and copies ran while one was open for 0% of the time, Pallas kernels for 11%

profile of v3, /device:TPU:0, one launch (start us, length us, event | category | flops | bytes accessed | tf_op | source)
XLA Modules:
  0.0 98.2 jit_solution(3384061076600889236)
XLA Ops:
  0.6 0.1 pad_add_fusion
  0.7 8.2 %product.2 = f32[16,25,4,128]{3,2,1,0:T(4,128)} custom-call(s32[1]{0:T(128)S(6)} %sub.3.part_ref, f32[6,128,4096]{2,1,0:T(8,128)} %blocks_hbm.3, s32[6]{0:T(128)} %ids_hbm.1, s32[6,32]{1,0:T(8,128)} %cols_hbm.3, f32[16,128,512]{2,1,0:T(8,128)} %features_hbm.3), custom_call_target="tpu_custom_call" | custom-call | flops 2415919104 | bytes 10485760 | tf_op jit(solution)/shard_map/product/pallas_call | solution.py:130
  8.9 6.3 %all-to-all-start = ((f32[16,25,4,128]{3,2,1,0:T(4,128)}), f32[16,25,4,128]{3,2,1,0:T(4,128)S(1)}, u32[]{:S(2)}, u32[]{:S(2)}) async-start(f32[16,25,4,128]{3,2,1,0:T(4,128)} %product.2), calls=%async_computation | async-start | bytes 1638400 | tf_op jit(solution)/shard_map/all_to_all | solution.py:325
  15.2 8.2 %product.3 = f32[16,24,4,128]{3,2,1,0:T(4,128)} custom-call(s32[1]{0:T(128)} %bitcast.part_ref, f32[6,128,4096]{2,1,0:T(8,128)} %blocks_hbm.3, s32[6]{0:T(128)} %ids_hbm.1, s32[6,32]{1,0:T(8,128)} %cols_hbm.3, f32[16,128,512]{2,1,0:T(8,128)} %features_hbm.3), custom_call_target="tpu_custom_call" | custom-call | flops 2415919104 | bytes 10485760 | tf_op jit(solution)/shard_map/product/pallas_call | solution.py:130
  23.4 0.0 copy-start
  23.4 5.5 %all-to-all-done.pieces_ref = f32[16,25,4,128]{3,2,1,0:T(4,128)S(1)} async-done(((f32[16,25,4,128]{3,2,1,0:T(4,128)}), f32[16,25,4,128]{3,2,1,0:T(4,128)S(1)}, u32[]{:S(2)}, u32[]{:S(2)}) %all-to-all-start) | async-done | bytes 819232 | tf_op jit(solution)/shard_map/all_to_all | solution.py:325
  28.9 3.6 %all-to-all-start.1 = ((f32[16,24,4,128]{3,2,1,0:T(4,128)}), f32[16,24,4,128]{3,2,1,0:T(4,128)S(1)}, u32[]{:S(2)}, u32[]{:S(2)}) async-start(f32[16,24,4,128]{3,2,1,0:T(4,128)} %product.3), calls=%async_computation.1 | async-start | bytes 1572864 | tf_op jit(solution)/shard_map/all_to_all | solution.py:327
  32.5 2.2 %sum_pieces.1 = (f32[32,4,4,128]{3,2,1,0:T(4,128)S(1)}, s32[96]{0:T(128)S(1)}) custom-call(f32[16,25,4,128]{3,2,1,0:T(4,128)S(1)} %all-to-all-done.pieces_ref), custom_call_target="tpu_custom_call" | custom-call | tf_op jit(solution)/shard_map/sum_pieces/pallas_call | solution.py:179
  34.7 2.7 %collective-permute-start = (f32[32,4,4,128]{3,2,1,0:T(4,128)S(1)}, f32[32,4,4,128]{3,2,1,0:T(4,128)S(1)}, u32[]{:S(2)}, u32[]{:S(2)}) collective-permute-start(f32[32,4,4,128]{3,2,1,0:T(4,128)S(1)} %get-tuple-element.13), channel_id=1, source_target_pairs={{0,16},{16,0},{1,17},{17,1},{2,18},{18,2},{3,19},{19,3},{4,20},{20... | collective-permute-start | bytes 786440 | tf_op jit(solution)/shard_map/ppermute | solution.py:329
  37.4 14.1 %all-to-all-done.1.pieces_ref = f32[16,24,4,128]{3,2,1,0:T(4,128)S(1)} async-done(((f32[16,24,4,128]{3,2,1,0:T(4,128)}), f32[16,24,4,128]{3,2,1,0:T(4,128)S(1)}, u32[]{:S(2)}, u32[]{:S(2)}) %all-to-all-start.1) | async-done | bytes 786464 | tf_op jit(solution)/shard_map/all_to_all | solution.py:327
  51.5 0.0 collective-permute-done.got_ref
  51.5 0.0 copy-done
  51.5 1.5 %update.1.mine_ref = f32[32,4,4,128]{3,2,1,0:T(4,128)S(1)} custom-call(s32[96]{0:T(128)S(1)} %get-tuple-element.11.ids_ref, f32[16,24,4,128]{3,2,1,0:T(4,128)S(1)} %all-to-all-done.1.pieces_ref, f32[32,4,4,128]{3,2,1,0:T(4,128)S(1)} %collective-permute-done.got_ref, f32[512,512]{1,0:T(8,128)S(1)} %copy-done), custom_call_target="tpu_custom_call" | custom-call | tf_op jit(solution)/shard_map/update/pallas_call | solution.py:216
  52.9 0.1 collective-permute-start.1
  53.0 0.1 collective-permute-start.3
  53.1 14.3 %collective-permute-done.1.mine_ref = f32[32,4,4,128]{3,2,1,0:T(4,128)S(1)} collective-permute-done((f32[32,4,4,128]{3,2,1,0:T(4,128)S(1)}, f32[32,4,4,128]{3,2,1,0:T(4,128)S(1)}, u32[]{:S(2)}, u32[]{:S(2)}) %collective-permute-start.1) | collective-permute-done | bytes 262176 | tf_op jit(solution)/shard_map/ppermute | solution.py:332
  67.4 0.0 collective-permute-start.2
  67.4 0.0 collective-permute-done.3.mate_ref
  67.4 0.8 answer.2.refs_0_
  68.2 0.7 collective-permute-done.2.mate_ref
  68.9 0.8 answer.3
  69.7 26.5 %all_to_all.15.answers_ref = f32[8,2,28,8,128]{4,3,2,1,0:T(8,128)S(1)} all-to-all(f32[8,2,28,8,128]{4,3,2,1,0:T(8,128)S(1)} %answer.3), channel_id=1, replica_groups=mesh['half'=2,'chip'=8,'core'=2] {'chip'}, dimensions={0} | all-to-all | bytes 3670016 | tf_op jit(solution)/shard_map/all_to_all | solution.py:337
  96.2 2.0 %place.1 = (f32[128,512]{1,0:T(8,128)}, f32[6,128,512]{2,1,0:T(8,128)}) custom-call(s32[2]{0:T(128)S(1)} %get-tuple-element.9.parts_ref, f32[8,2,28,8,128]{4,3,2,1,0:T(8,128)S(1)} %all_to_all.15.answers_ref), custom_call_target="tpu_custom_call" | custom-call | tf_op jit(solution)/shard_map/place/pallas_call | solution.py:287
Async XLA Ops:
  8.9 20.0 %all-to-all-start = ((f32[16,25,4,128]{3,2,1,0:T(4,128)}), f32[16,25,4,128]{3,2,1,0:T(4,128)S(1)}, u32[]{:S(2)}, u32[]{:S(2)}) async-start(f32[16,25,4,128]{3,2,1,0:T(4,128)} %product.2), calls=%async_computation | async-start | bytes 1638400 | tf_op jit(solution)/shard_map/all_to_all | solution.py:325
  23.4 28.1 %copy-start = (f32[512,512]{1,0:T(8,128)S(1)}, f32[512,512]{1,0:T(8,128)}, u32[]{:S(2)}) copy-start(f32[512,512]{1,0:T(8,128)} %factor_ref.1) | copy-start | bytes 3145732
  28.9 22.6 %all-to-all-start.1 = ((f32[16,24,4,128]{3,2,1,0:T(4,128)}), f32[16,24,4,128]{3,2,1,0:T(4,128)S(1)}, u32[]{:S(2)}, u32[]{:S(2)}) async-start(f32[16,24,4,128]{3,2,1,0:T(4,128)} %product.3), calls=%async_computation.1 | async-start | bytes 1572864 | tf_op jit(solution)/shard_map/all_to_all | solution.py:327
  34.7 16.7 %collective-permute-start = (f32[32,4,4,128]{3,2,1,0:T(4,128)S(1)}, f32[32,4,4,128]{3,2,1,0:T(4,128)S(1)}, u32[]{:S(2)}, u32[]{:S(2)}) collective-permute-start(f32[32,4,4,128]{3,2,1,0:T(4,128)S(1)} %get-tuple-element.13), channel_id=1, source_target_pairs={{0,16},{16,0},{1,17},{17,1},{2,18},{18,2},{3,19},{19,3},{4,20},{20... | collective-permute-start | bytes 786440 | tf_op jit(solution)/shard_map/ppermute | solution.py:329
  52.9 14.4 %collective-permute-start.1 = (f32[32,4,4,128]{3,2,1,0:T(4,128)S(1)}, f32[32,4,4,128]{3,2,1,0:T(4,128)S(1)}, u32[]{:S(2)}, u32[]{:S(2)}) collective-permute-start(f32[32,4,4,128]{3,2,1,0:T(4,128)S(1)} %update.1.mine_ref), channel_id=1, source_target_pairs={{0,16},{16,0},{1,17},{17,1},{2,18},{18,2},{3,19},{19,3},{4,20},{20... | collective-permute-start | bytes 786440 | tf_op jit(solution)/shard_map/ppermute | solution.py:332
  53.0 14.4 %collective-permute-start.3 = (f32[32,4,4,128]{3,2,1,0:T(4,128)S(1)}, f32[32,4,4,128]{3,2,1,0:T(4,128)S(1)}, u32[]{:S(2)}, u32[]{:S(2)}) collective-permute-start(f32[32,4,4,128]{3,2,1,0:T(4,128)S(1)} %update.1.mine_ref), channel_id=1, source_target_pairs={{0,1},{1,0},{2,3},{3,2},{4,5},{5,4},{6,7},{7,6},{8,9},{9,8},{10,11... | collective-permute-start | bytes 786440 | tf_op jit(solution)/shard_map/ppermute | solution.py:333
  67.4 1.5 %collective-permute-start.2 = (f32[32,4,4,128]{3,2,1,0:T(4,128)S(1)}, f32[32,4,4,128]{3,2,1,0:T(4,128)S(1)}, u32[]{:S(2)}, u32[]{:S(2)}) collective-permute-start(f32[32,4,4,128]{3,2,1,0:T(4,128)S(1)} %collective-permute-done.1.mine_ref), channel_id=1, source_target_pairs={{0,1},{1,0},{2,3},{3,2},{4,5},{5,4},{6,7},{7,6},{8,9},{9,8},{10,11... | collective-permute-start | bytes 786440 | tf_op jit(solution)/shard_map/ppermute | solution.py:335

commit v4 on v3

--- a/solution.py
+++ b/solution.py
@@ -12,6 +12,7 @@
 BF16 = jnp.bfloat16
 I32 = jnp.int32
 LANES = 128
+UNROLL = 8
 VMEM_BYTES = 24 << 20
 PRODUCT_VMEM_BYTES = 60 << 20
 
@@ -155,22 +156,30 @@
     )(part, blocks, row_ids, col_ids, features)
 
 
-def sum_kernel(slots, pieces_ref, out_ref, ids_out, ids, sem):
-    peers, places = pieces_ref.shape[:2]
-    tiles = out_ref.shape[1]
-    ids_copy = pltpu.make_async_copy(pieces_ref.at[:, places - 1], ids, sem)
+def add_by_row(row_of, pieces_ref, tables, slots):
+    peers = pieces_ref.shape[0]
+    tiles = tables[0].shape[1]
+
+    def add_peer(peer, carry):
+        for slot in range(slots):
+            row = row_of(peer, slot)
+            table = tables[slot % len(tables)]
+            table[row] = table[row] + pieces_ref[peer, slot * tiles : (slot + 1) * tiles]
+        return carry
+
+    lax.fori_loop(0, peers, add_peer, 0, unroll=UNROLL)
+
+
+def sum_kernel(slots, pieces_ref, out_ref, ids_out, other, ids, sem):
+    ids_out[...] = pieces_ref[:, pieces_ref.shape[1] - 1].astype(I32)
+    ids_copy = pltpu.make_async_copy(ids_out, ids, sem)
     ids_copy.start()
     out_ref[...] = jnp.zeros_like(out_ref)
+    other[...] = jnp.zeros_like(other)
     ids_copy.wait()
 
-    def add_peer(peer, carry):
-        for slot in range(slots):
-            row = ids[peer, 0, slot].astype(I32)
-            ids_out[peer * slots + slot] = row
-            out_ref[row] = out_ref[row] + pieces_ref[peer, slot * tiles : (slot + 1) * tiles]
-        return carry
-
-    lax.fori_loop(0, peers, add_peer, 0)
+    add_by_row(lambda peer, slot: ids[peer, 0, slot], pieces_ref, (out_ref, other), slots)
+    out_ref[...] += other[...]
 
 
 def sum_pieces(pieces, row_blocks, slots):
@@ -179,32 +188,32 @@
     return pl.pallas_call(
         functools.partial(sum_kernel, slots),
         in_specs=[spec(pltpu.VMEM)],
-        out_specs=(spec(pltpu.VMEM), spec(pltpu.SMEM)),
+        out_specs=(spec(pltpu.VMEM), spec(pltpu.VMEM)),
         out_shape=(
             jax.ShapeDtypeStruct((row_blocks, tiles, rows, LANES), F32),
-            jax.ShapeDtypeStruct((peers * slots,), I32),
+            jax.ShapeDtypeStruct((peers, rows, LANES), I32),
         ),
-        scratch_shapes=[pltpu.SMEM((peers, rows, LANES), F32), pltpu.SemaphoreType.DMA],
+        scratch_shapes=[
+            pltpu.VMEM((row_blocks, tiles, rows, LANES), F32),
+            pltpu.SMEM((peers, rows, LANES), I32),
+            pltpu.SemaphoreType.DMA,
+        ],
         compiler_params=params(),
         name="sum_pieces",
     )(pieces)
 
 
-def update_kernel(slots, ids_ref, pieces_ref, got_ref, factor_ref, out_ref, total, left):
-    peers = pieces_ref.shape[0]
+def update_kernel(slots, ids_ref, pieces_ref, got_ref, factor_ref, out_ref, total, other, left):
     row_blocks, tiles, rows, _ = out_ref.shape
     total[...] = got_ref[...]
-
-    def add_peer(peer, carry):
-        for slot in range(slots):
-            row = ids_ref[peer * slots + slot]
-            total[row] = total[row] + pieces_ref[peer, slot * tiles : (slot + 1) * tiles]
-        return carry
-
-    lax.fori_loop(0, peers, add_peer, 0)
+    other[...] = jnp.zeros_like(other)
+    add_by_row(
+        lambda peer, slot: ids_ref[peer * slots + slot], pieces_ref, (total, other), slots
+    )
     for row in range(row_blocks):
         for t in range(tiles):
-            left[row * rows : (row + 1) * rows, t * LANES : (t + 1) * LANES] = total[row, t]
+            here = slice(row * rows, (row + 1) * rows), slice(t * LANES, (t + 1) * LANES)
+            left[here] = total[row, t] + other[row, t]
     out = dot3(*split(jnp.tanh(left[...])), *split(factor_ref[...]))
     for row in range(row_blocks):
         for t in range(tiles):
@@ -220,6 +229,7 @@
         out_shape=jax.ShapeDtypeStruct(got.shape, F32),
         scratch_shapes=[
             pltpu.VMEM(got.shape, F32),
+            pltpu.VMEM(got.shape, F32),
             pltpu.VMEM((row_blocks * rows, tiles * LANES), F32),
         ],
         compiler_params=params(),
@@ -244,7 +254,7 @@
         out_ref[chip, 0, slots * tiles :] = table[first + peer]
         return carry
 
-    lax.fori_loop(0, chips, pick, 0)
+    lax.fori_loop(0, chips, pick, 0, unroll=UNROLL)
 
 
 def answer(ids, self_at, mine, mate, chips, slots, part, cost_bytes, earlier=()):
@@ -268,47 +278,45 @@
     )(ids, self_at, mine, mate, *earlier)
 
 
-def place_kernel(slots, parts_ref, answers_ref, owned_ref, returned_ref):
-    chips, _, places, rows, _ = answers_ref.shape
+def place_kernel(parts_ref, answers_ref, owned_hbm, returned_hbm, sems):
+    chips, parts, places, _, _ = answers_ref.shape
+    slots, _, tiles, _, _ = returned_hbm.shape
+    copies = []
+    for part in range(parts):
+        at = pl.ds(parts_ref[part] * chips, chips)
+        for place in range(slots + 1):
+            source = answers_ref.at[:, part, place * tiles : (place + 1) * tiles]
+            target = returned_hbm.at[place, at] if place < slots else owned_hbm.at[at]
+            copies.append(pltpu.make_async_copy(source, target, sems.at[part, place]))
+            copies[-1].start()
+    for copy in copies:
+        copy.wait()
+
+
+def place(parts, answers, slots):
+    chips, halves, places, rows, _ = answers.shape
     tiles = places // (slots + 1)
-    for chip in range(chips):
-        here = pl.ds(chip * rows, rows)
-        for t in range(tiles):
-            cut = slice(t * LANES, (t + 1) * LANES)
-            for slot in range(slots):
-                returned_ref[slot, here, cut] = answers_ref[chip, 0, slot * tiles + t]
-            owned_ref[here, cut] = answers_ref[chip, 0, slots * tiles + t]
-
-
-def place(parts, answers, slots):
-    chips, _, places, rows, _ = answers.shape
-    feat = places // (slots + 1) * LANES
-    half_rows = chips * rows
-    return pl.pallas_call(
-        functools.partial(place_kernel, slots),
-        grid_spec=pltpu.PrefetchScalarGridSpec(
-            num_scalar_prefetch=1,
-            grid=(2,),
-            in_specs=[
-                pl.BlockSpec((chips, 1, places, rows, LANES), lambda i, parts: (0, i, 0, 0, 0))
-            ],
-            out_specs=(
-                pl.BlockSpec((half_rows, feat), lambda i, parts: (parts[i], 0)),
-                pl.BlockSpec((slots, half_rows, feat), lambda i, parts: (0, parts[i], 0)),
-            ),
+    owned = (halves * chips, tiles, rows, LANES)
+    owned_rows, returned = pl.pallas_call(
+        place_kernel,
+        in_specs=[spec(pltpu.SMEM), spec(pl.ANY)],
+        out_specs=(spec(pltpu.HBM), spec(pltpu.HBM)),
+        out_shape=(
+            jax.ShapeDtypeStruct(owned, F32),
+            jax.ShapeDtypeStruct((slots, *owned), F32),
         ),
-        out_shape=(
-            jax.ShapeDtypeStruct((2 * half_rows, feat), F32),
-            jax.ShapeDtypeStruct((slots, 2 * half_rows, feat), F32),
-        ),
+        scratch_shapes=[pltpu.SemaphoreType.DMA((halves, slots + 1))],
         compiler_params=params(),
         name="place",
     )(parts, answers)
+    feat = tiles * LANES
+    owned_rows = owned_rows.transpose(0, 2, 1, 3).reshape(-1, feat)
+    returned = returned.transpose(0, 1, 3, 2, 4).reshape(-1, feat)
+    return owned_rows, returned
 
 
 def local(blocks, features, col_ids, row_ids, factor):
-    slots, rows, _ = blocks.shape
-    feat = features.shape[2]
+    slots = blocks.shape[0]
     chips = lax.axis_size("chip")
     peer_axes = ("chip", "core")
     peers = lax.axis_size(peer_axes)
@@ -327,6 +335,7 @@
     near = lax.all_to_all(near, peer_axes, 0, 0)
     far_sums, ids = sum_pieces(far, row_blocks, slots)
     got = lax.ppermute(far_sums, "half", swap)
+    ids = ids[:, 0, :slots].reshape(-1)
     near_rows = update(ids, near, got, factor, slots)
 
     far_rows = lax.ppermute(near_rows, "half", swap)
@@ -335,8 +344,7 @@
     far_mate = lax.ppermute(far_rows, "core", swap)
     answers = answer(ids, self_at, far_rows, far_mate, chips, slots, 1, 1 << 20, (answers,))
     answers = lax.all_to_all(answers, "chip", 0, 0)
-    owned_rows, returned = place(parts, answers, slots)
-    return owned_rows, returned.reshape(slots * rows, feat)
+    return place(parts, answers, slots)
 
 
 def solution(mesh):

time: 98.5 us -> 98.3 us (level)
  Pallas kernels: 23.6 us -> 22.6 us
where the time goes in v4:
time: 98.3 us; the launch traced here: 97.9 us
  waiting for transfers between devices  35.2 us (36%)
  blocking collectives  26.5 us (27%)
  Pallas kernels  22.6 us (23%)
  starting transfers between devices  12.7 us (13%)
    all_to_all x1, blocking collectives, local(): answers = lax.all_to_all(answers, 'chip', 0, 0)  26.5 us
    pallas_call x2, Pallas kernels, product(): pl.pallas_call(functools.partial(product_kernel, with_ids, groups, featur...  16.4 us
    all_to_all x1, waiting for transfers between devices, local(): near = lax.all_to_all(near, peer_axes, 0, 0)  14.7 us
    ppermute x1, waiting for transfers between devices, local(): far_rows = lax.ppermute(near_rows, 'half', swap)  14.3 us
    all_to_all x1, starting transfers between devices, local(): far = lax.all_to_all(far, peer_axes, 0, 0)  6.3 us
    all_to_all x1, waiting for transfers between devices, local(): far = lax.all_to_all(far, peer_axes, 0, 0)  5.51 us
    all_to_all x1, starting transfers between devices, local(): near = lax.all_to_all(near, peer_axes, 0, 0)  3.61 us
    ppermute x1, starting transfers between devices, local(): got = lax.ppermute(far_sums, 'half', swap)  2.66 us
  transfers between devices with their start and end apart: 6, of which 4 were waited for; matrix products, arithmetic and copies ran while one was open for 0% of the time, Pallas kernels for 11%

profile of v4, /device:TPU:0, one launch (start us, length us, event | category | flops | bytes accessed | tf_op | source)
XLA Modules:
  0.0 97.9 jit_solution(15205328472648198881)
XLA Ops:
  0.6 0.1 pad_add_fusion
  0.7 8.2 %product.2 = f32[16,25,4,128]{3,2,1,0:T(4,128)} custom-call(s32[1]{0:T(128)S(6)} %sub.3.part_ref, f32[6,128,4096]{2,1,0:T(8,128)} %blocks_hbm.3, s32[6]{0:T(128)} %ids_hbm.1, s32[6,32]{1,0:T(8,128)} %cols_hbm.3, f32[16,128,512]{2,1,0:T(8,128)} %features_hbm.3), custom_call_target="tpu_custom_call" | custom-call | flops 2415919104 | bytes 10485760 | tf_op jit(solution)/shard_map/product/pallas_call | solution.py:131
  8.9 6.3 %all-to-all-start = ((f32[16,25,4,128]{3,2,1,0:T(4,128)}), f32[16,25,4,128]{3,2,1,0:T(4,128)S(1)}, u32[]{:S(2)}, u32[]{:S(2)}) async-start(f32[16,25,4,128]{3,2,1,0:T(4,128)} %product.2), calls=%async_computation | async-start | bytes 1638400 | tf_op jit(solution)/shard_map/all_to_all | solution.py:333
  15.2 8.2 %product.3 = f32[16,24,4,128]{3,2,1,0:T(4,128)} custom-call(s32[1]{0:T(128)} %bitcast.part_ref, f32[6,128,4096]{2,1,0:T(8,128)} %blocks_hbm.3, s32[6]{0:T(128)} %ids_hbm.1, s32[6,32]{1,0:T(8,128)} %cols_hbm.3, f32[16,128,512]{2,1,0:T(8,128)} %features_hbm.3), custom_call_target="tpu_custom_call" | custom-call | flops 2415919104 | bytes 10485760 | tf_op jit(solution)/shard_map/product/pallas_call | solution.py:131
  23.4 0.0 copy-start
  23.4 5.5 %all-to-all-done.pieces_ref = f32[16,25,4,128]{3,2,1,0:T(4,128)S(1)} async-done(((f32[16,25,4,128]{3,2,1,0:T(4,128)}), f32[16,25,4,128]{3,2,1,0:T(4,128)S(1)}, u32[]{:S(2)}, u32[]{:S(2)}) %all-to-all-start) | async-done | bytes 819232 | tf_op jit(solution)/shard_map/all_to_all | solution.py:333
  28.9 3.6 %all-to-all-start.1 = ((f32[16,24,4,128]{3,2,1,0:T(4,128)}), f32[16,24,4,128]{3,2,1,0:T(4,128)S(1)}, u32[]{:S(2)}, u32[]{:S(2)}) async-start(f32[16,24,4,128]{3,2,1,0:T(4,128)} %product.3), calls=%async_computation.1 | async-start | bytes 1572864 | tf_op jit(solution)/shard_map/all_to_all | solution.py:335
  32.5 1.5 %sum_pieces.1 = (f32[32,4,4,128]{3,2,1,0:T(4,128)S(1)}, s32[16,4,128]{2,1,0:T(4,128)S(1)}) custom-call(f32[16,25,4,128]{3,2,1,0:T(4,128)S(1)} %all-to-all-done.pieces_ref), custom_call_target="tpu_custom_call" | custom-call | tf_op jit(solution)/shard_map/sum_pieces/pallas_call | solution.py:188
  34.0 2.7 %collective-permute-start = (f32[32,4,4,128]{3,2,1,0:T(4,128)S(1)}, f32[32,4,4,128]{3,2,1,0:T(4,128)S(1)}, u32[]{:S(2)}, u32[]{:S(2)}) collective-permute-start(f32[32,4,4,128]{3,2,1,0:T(4,128)S(1)} %get-tuple-element.13), channel_id=1, source_target_pairs={{0,16},{16,0},{1,17},{17,1},{2,18},{18,2},{3,19},{19,3},{4,20},{20... | collective-permute-start | bytes 786440 | tf_op jit(solution)/shard_map/ppermute | solution.py:337
  36.7 0.1 reshape_squeeze.3.ids_ref
  36.8 14.7 %all-to-all-done.1.pieces_ref = f32[16,24,4,128]{3,2,1,0:T(4,128)S(1)} async-done(((f32[16,24,4,128]{3,2,1,0:T(4,128)}), f32[16,24,4,128]{3,2,1,0:T(4,128)S(1)}, u32[]{:S(2)}, u32[]{:S(2)}) %all-to-all-start.1) | async-done | bytes 786464 | tf_op jit(solution)/shard_map/all_to_all | solution.py:335
  51.5 0.0 collective-permute-done.got_ref
  51.5 0.0 copy-done
  51.5 1.4 %update.1.mine_ref = f32[32,4,4,128]{3,2,1,0:T(4,128)S(1)} custom-call(s32[96]{0:T(128)S(1)} %reshape_squeeze.3.ids_ref, f32[16,24,4,128]{3,2,1,0:T(4,128)S(1)} %all-to-all-done.1.pieces_ref, f32[32,4,4,128]{3,2,1,0:T(4,128)S(1)} %collective-permute-done.got_ref, f32[512,512]{1,0:T(8,128)S(1)} %copy-done), custom_call_target="tpu_custom_call" | custom-call | tf_op jit(solution)/shard_map/update/pallas_call | solution.py:225
  52.8 0.1 collective-permute-start.1
  52.9 0.1 collective-permute-start.3
  53.0 14.3 %collective-permute-done.1.mine_ref = f32[32,4,4,128]{3,2,1,0:T(4,128)S(1)} collective-permute-done((f32[32,4,4,128]{3,2,1,0:T(4,128)S(1)}, f32[32,4,4,128]{3,2,1,0:T(4,128)S(1)}, u32[]{:S(2)}, u32[]{:S(2)}) %collective-permute-start.1) | collective-permute-done | bytes 262176 | tf_op jit(solution)/shard_map/ppermute | solution.py:341
  67.3 0.0 collective-permute-start.2
  67.3 0.0 collective-permute-done.3.mate_ref
  67.3 0.7 answer.2.refs_0_
  68.0 0.8 collective-permute-done.2.mate_ref
  68.8 0.7 answer.3
  69.6 26.5 %all_to_all.15.answers_ref = f32[8,2,28,8,128]{4,3,2,1,0:T(8,128)S(1)} all-to-all(f32[8,2,28,8,128]{4,3,2,1,0:T(8,128)S(1)} %answer.3), channel_id=1, replica_groups=mesh['half'=2,'chip'=8,'core'=2] {'chip'}, dimensions={0} | all-to-all | bytes 3670016 | tf_op jit(solution)/shard_map/all_to_all | solution.py:346
  96.0 1.9 %place.1 = (f32[16,4,8,128]{3,2,1,0:T(8,128)}, f32[6,16,4,8,128]{4,3,2,1,0:T(8,128)}) custom-call(s32[2]{0:T(128)S(1)} %get-tuple-element.9.parts_ref, f32[8,2,28,8,128]{4,3,2,1,0:T(8,128)S(1)} %all_to_all.15.answers_ref), custom_call_target="tpu_custom_call" | custom-call | tf_op jit(solution)/shard_map/place/pallas_call | solution.py:300
  (1 shorter events, 0.0 us)
Async XLA Ops:
  8.9 20.0 %all-to-all-start = ((f32[16,25,4,128]{3,2,1,0:T(4,128)}), f32[16,25,4,128]{3,2,1,0:T(4,128)S(1)}, u32[]{:S(2)}, u32[]{:S(2)}) async-start(f32[16,25,4,128]{3,2,1,0:T(4,128)} %product.2), calls=%async_computation | async-start | bytes 1638400 | tf_op jit(solution)/shard_map/all_to_all | solution.py:333
  23.4 28.1 %copy-start = (f32[512,512]{1,0:T(8,128)S(1)}, f32[512,512]{1,0:T(8,128)}, u32[]{:S(2)}) copy-start(f32[512,512]{1,0:T(8,128)} %factor_ref.1) | copy-start | bytes 3145732
  28.9 22.6 %all-to-all-start.1 = ((f32[16,24,4,128]{3,2,1,0:T(4,128)}), f32[16,24,4,128]{3,2,1,0:T(4,128)S(1)}, u32[]{:S(2)}, u32[]{:S(2)}) async-start(f32[16,24,4,128]{3,2,1,0:T(4,128)} %product.3), calls=%async_computation.1 | async-start | bytes 1572864 | tf_op jit(solution)/shard_map/all_to_all | solution.py:335
  34.0 17.4 %collective-permute-start = (f32[32,4,4,128]{3,2,1,0:T(4,128)S(1)}, f32[32,4,4,128]{3,2,1,0:T(4,128)S(1)}, u32[]{:S(2)}, u32[]{:S(2)}) collective-permute-start(f32[32,4,4,128]{3,2,1,0:T(4,128)S(1)} %get-tuple-element.13), channel_id=1, source_target_pairs={{0,16},{16,0},{1,17},{17,1},{2,18},{18,2},{3,19},{19,3},{4,20},{20... | collective-permute-start | bytes 786440 | tf_op jit(solution)/shard_map/ppermute | solution.py:337
  52.8 14.4 %collective-permute-start.1 = (f32[32,4,4,128]{3,2,1,0:T(4,128)S(1)}, f32[32,4,4,128]{3,2,1,0:T(4,128)S(1)}, u32[]{:S(2)}, u32[]{:S(2)}) collective-permute-start(f32[32,4,4,128]{3,2,1,0:T(4,128)S(1)} %update.1.mine_ref), channel_id=1, source_target_pairs={{0,16},{16,0},{1,17},{17,1},{2,18},{18,2},{3,19},{19,3},{4,20},{20... | collective-permute-start | bytes 786440 | tf_op jit(solution)/shard_map/ppermute | solution.py:341
  52.9 14.4 %collective-permute-start.3 = (f32[32,4,4,128]{3,2,1,0:T(4,128)S(1)}, f32[32,4,4,128]{3,2,1,0:T(4,128)S(1)}, u32[]{:S(2)}, u32[]{:S(2)}) collective-permute-start(f32[32,4,4,128]{3,2,1,0:T(4,128)S(1)} %update.1.mine_ref), channel_id=1, source_target_pairs={{0,1},{1,0},{2,3},{3,2},{4,5},{5,4},{6,7},{7,6},{8,9},{9,8},{10,11... | collective-permute-start | bytes 786440 | tf_op jit(solution)/shard_map/ppermute | solution.py:342
  67.3 1.5 %collective-permute-start.2 = (f32[32,4,4,128]{3,2,1,0:T(4,128)S(1)}, f32[32,4,4,128]{3,2,1,0:T(4,128)S(1)}, u32[]{:S(2)}, u32[]{:S(2)}) collective-permute-start(f32[32,4,4,128]{3,2,1,0:T(4,128)S(1)} %collective-permute-done.1.mine_ref), channel_id=1, source_target_pairs={{0,1},{1,0},{2,3},{3,2},{4,5},{5,4},{6,7},{7,6},{8,9},{9,8},{10,11... | collective-permute-start | bytes 786440 | tf_op jit(solution)/shard_map/ppermute | solution.py:344

commit v5 on v4

--- a/solution.py
+++ b/solution.py
@@ -95,7 +95,9 @@
                 for t in range(0, width, LANES):
                     piece = both[s * rows : (s + 1) * rows, t : t + LANES]
                     place = ((group * in_group + s) * feat + n + t) // LANES
-                    out_ref[:, place] = piece.reshape(peers, piece_rows, LANES)
+                    piece = piece.reshape(peers // 2, 2, piece_rows, LANES)
+                    out_ref[: peers // 2, place] = piece[:, 0]
+                    out_ref[peers // 2 :, place] = piece[:, 1]
 
     def split_tile(tile, carry):
         high, low = split(features[tile])
@@ -247,11 +249,11 @@
     table[:, :, rows:] = jnp.where(core == 0, mate, mine)
 
     def pick(chip, carry):
-        peer = chip * 2 + core
+        peer = core * chips + chip
         for slot in range(slots):
             row = ids_ref[peer * slots + slot]
             out_ref[chip, 0, slot * tiles : (slot + 1) * tiles] = table[row]
-        out_ref[chip, 0, slots * tiles :] = table[first + peer]
+        out_ref[chip, 0, slots * tiles :] = table[first + chip * 2 + core]
         return carry
 
     lax.fori_loop(0, chips, pick, 0, unroll=UNROLL)
@@ -318,7 +320,7 @@
 def local(blocks, features, col_ids, row_ids, factor):
     slots = blocks.shape[0]
     chips = lax.axis_size("chip")
-    peer_axes = ("chip", "core")
+    peer_axes = ("core", "chip")
     peers = lax.axis_size(peer_axes)
     row_blocks = peers * lax.axis_size("half")
     half = lax.axis_index("half").astype(I32)

time: 98.3 us -> 96.5 us (0.982)
  waiting for transfers between devices: 35.2 us -> 32.3 us
  starting transfers between devices: 12.7 us -> 13.9 us
    all_to_all x1, waiting for transfers between devices: 14.7 us -> 13.3 us  [local(): near = lax.all_to_all(near, peer_axes, 0, 0)]
    all_to_all x1, waiting for transfers between devices: 5.51 us -> 4.17 us  [local(): far = lax.all_to_all(far, peer_axes, 0, 0)]
    ppermute x1, starting transfers between devices: 0.07 us -> 1.07 us  [local(): far_rows = lax.ppermute(near_rows, 'half', swap)]
where the time goes in v5:
time: 96.5 us; the launch traced here: 96.2 us
  waiting for transfers between devices  32.3 us (33%)
  blocking collectives  26.5 us (27%)
  Pallas kernels  22.6 us (23%)
  starting transfers between devices  13.9 us (14%)
    all_to_all x1, blocking collectives, local(): answers = lax.all_to_all(answers, 'chip', 0, 0)  26.5 us
    pallas_call x2, Pallas kernels, product(): pl.pallas_call(functools.partial(product_kernel, with_ids, groups, featur...  16.4 us
    ppermute x1, waiting for transfers between devices, local(): far_rows = lax.ppermute(near_rows, 'half', swap)  14 us
    all_to_all x1, waiting for transfers between devices, local(): near = lax.all_to_all(near, peer_axes, 0, 0)  13.3 us
    all_to_all x1, starting transfers between devices, local(): far = lax.all_to_all(far, peer_axes, 0, 0)  6.3 us
    all_to_all x1, waiting for transfers between devices, local(): far = lax.all_to_all(far, peer_axes, 0, 0)  4.17 us
    all_to_all x1, starting transfers between devices, local(): near = lax.all_to_all(near, peer_axes, 0, 0)  3.91 us
    ppermute x1, starting transfers between devices, local(): got = lax.ppermute(far_sums, 'half', swap)  2.65 us
  transfers between devices with their start and end apart: 6, of which 4 were waited for; matrix products, arithmetic and copies ran while one was open for 0% of the time, Pallas kernels for 11%

profile of v5, /device:TPU:0, one launch (start us, length us, event | category | flops | bytes accessed | tf_op | source)
XLA Modules:
  0.0 96.2 jit_solution(18007492646423315751)
XLA Ops:
  0.6 0.1 pad_add_fusion
  0.7 8.2 %product.2 = f32[16,25,4,128]{3,2,1,0:T(4,128)} custom-call(s32[1]{0:T(128)S(6)} %sub.3.part_ref, f32[6,128,4096]{2,1,0:T(8,128)} %blocks_hbm.3, s32[6]{0:T(128)} %ids_hbm.1, s32[6,32]{1,0:T(8,128)} %cols_hbm.3, f32[16,128,512]{2,1,0:T(8,128)} %features_hbm.3), custom_call_target="tpu_custom_call" | custom-call | flops 2415919104 | bytes 10485760 | tf_op jit(solution)/shard_map/product/pallas_call | solution.py:133
  8.9 6.3 %all-to-all-start = ((f32[16,25,4,128]{3,2,1,0:T(4,128)}), f32[16,25,4,128]{3,2,1,0:T(4,128)S(1)}, u32[]{:S(2)}, u32[]{:S(2)}) async-start(f32[16,25,4,128]{3,2,1,0:T(4,128)} %product.2), calls=%async_computation | async-start | bytes 1638400 | tf_op jit(solution)/shard_map/all_to_all | solution.py:335
  15.2 8.2 %product.3 = f32[16,24,4,128]{3,2,1,0:T(4,128)} custom-call(s32[1]{0:T(128)} %bitcast.part_ref, f32[6,128,4096]{2,1,0:T(8,128)} %blocks_hbm.3, s32[6]{0:T(128)} %ids_hbm.1, s32[6,32]{1,0:T(8,128)} %cols_hbm.3, f32[16,128,512]{2,1,0:T(8,128)} %features_hbm.3), custom_call_target="tpu_custom_call" | custom-call | flops 2415919104 | bytes 10485760 | tf_op jit(solution)/shard_map/product/pallas_call | solution.py:133
  23.4 0.0 copy-start
  23.4 4.2 %all-to-all-done.pieces_ref = f32[16,25,4,128]{3,2,1,0:T(4,128)S(1)} async-done(((f32[16,25,4,128]{3,2,1,0:T(4,128)}), f32[16,25,4,128]{3,2,1,0:T(4,128)S(1)}, u32[]{:S(2)}, u32[]{:S(2)}) %all-to-all-start) | async-done | bytes 819232 | tf_op jit(solution)/shard_map/all_to_all | solution.py:335
  27.6 3.9 %all-to-all-start.1 = ((f32[16,24,4,128]{3,2,1,0:T(4,128)}), f32[16,24,4,128]{3,2,1,0:T(4,128)S(1)}, u32[]{:S(2)}, u32[]{:S(2)}) async-start(f32[16,24,4,128]{3,2,1,0:T(4,128)} %product.3), calls=%async_computation.1 | async-start | bytes 1572864 | tf_op jit(solution)/shard_map/all_to_all | solution.py:337
  31.5 1.5 %sum_pieces.1 = (f32[32,4,4,128]{3,2,1,0:T(4,128)S(1)}, s32[16,4,128]{2,1,0:T(4,128)S(1)}) custom-call(f32[16,25,4,128]{3,2,1,0:T(4,128)S(1)} %all-to-all-done.pieces_ref), custom_call_target="tpu_custom_call" | custom-call | tf_op jit(solution)/shard_map/sum_pieces/pallas_call | solution.py:190
  33.0 2.7 %collective-permute-start = (f32[32,4,4,128]{3,2,1,0:T(4,128)S(1)}, f32[32,4,4,128]{3,2,1,0:T(4,128)S(1)}, u32[]{:S(2)}, u32[]{:S(2)}) collective-permute-start(f32[32,4,4,128]{3,2,1,0:T(4,128)S(1)} %get-tuple-element.13), channel_id=1, source_target_pairs={{0,16},{16,0},{1,17},{17,1},{2,18},{18,2},{3,19},{19,3},{4,20},{20... | collective-permute-start | bytes 786440 | tf_op jit(solution)/shard_map/ppermute | solution.py:339
  35.7 0.1 reshape_squeeze.3.ids_ref
  35.8 13.3 %all-to-all-done.1.pieces_ref = f32[16,24,4,128]{3,2,1,0:T(4,128)S(1)} async-done(((f32[16,24,4,128]{3,2,1,0:T(4,128)}), f32[16,24,4,128]{3,2,1,0:T(4,128)S(1)}, u32[]{:S(2)}, u32[]{:S(2)}) %all-to-all-start.1) | async-done | bytes 786464 | tf_op jit(solution)/shard_map/all_to_all | solution.py:337
  49.1 0.0 collective-permute-done.got_ref
  49.1 0.0 copy-done
  49.1 1.4 %update.1.mine_ref = f32[32,4,4,128]{3,2,1,0:T(4,128)S(1)} custom-call(s32[96]{0:T(128)S(1)} %reshape_squeeze.3.ids_ref, f32[16,24,4,128]{3,2,1,0:T(4,128)S(1)} %all-to-all-done.1.pieces_ref, f32[32,4,4,128]{3,2,1,0:T(4,128)S(1)} %collective-permute-done.got_ref, f32[512,512]{1,0:T(8,128)S(1)} %copy-done), custom_call_target="tpu_custom_call" | custom-call | tf_op jit(solution)/shard_map/update/pallas_call | solution.py:227
  50.4 1.1 %collective-permute-start.1 = (f32[32,4,4,128]{3,2,1,0:T(4,128)S(1)}, f32[32,4,4,128]{3,2,1,0:T(4,128)S(1)}, u32[]{:S(2)}, u32[]{:S(2)}) collective-permute-start(f32[32,4,4,128]{3,2,1,0:T(4,128)S(1)} %update.1.mine_ref), channel_id=1, source_target_pairs={{0,16},{16,0},{1,17},{17,1},{2,18},{18,2},{3,19},{19,3},{4,20},{20... | collective-permute-start | bytes 786440 | tf_op jit(solution)/shard_map/ppermute | solution.py:343
  51.5 0.0 collective-permute-start.3
  51.5 14.0 %collective-permute-done.1.mine_ref = f32[32,4,4,128]{3,2,1,0:T(4,128)S(1)} collective-permute-done((f32[32,4,4,128]{3,2,1,0:T(4,128)S(1)}, f32[32,4,4,128]{3,2,1,0:T(4,128)S(1)}, u32[]{:S(2)}, u32[]{:S(2)}) %collective-permute-start.1) | collective-permute-done | bytes 262176 | tf_op jit(solution)/shard_map/ppermute | solution.py:343
  65.5 0.0 collective-permute-start.2
  65.5 0.0 collective-permute-done.3.mate_ref
  65.5 0.7 answer.2.refs_0_
  66.3 0.8 collective-permute-done.2.mate_ref
  67.1 0.7 answer.3
  67.8 26.5 %all_to_all.15.answers_ref = f32[8,2,28,8,128]{4,3,2,1,0:T(8,128)S(1)} all-to-all(f32[8,2,28,8,128]{4,3,2,1,0:T(8,128)S(1)} %answer.3), channel_id=1, replica_groups=mesh['half'=2,'chip'=8,'core'=2] {'chip'}, dimensions={0} | all-to-all | bytes 3670016 | tf_op jit(solution)/shard_map/all_to_all | solution.py:348
  94.3 1.9 %place.1 = (f32[16,4,8,128]{3,2,1,0:T(8,128)}, f32[6,16,4,8,128]{4,3,2,1,0:T(8,128)}) custom-call(s32[2]{0:T(128)S(1)} %get-tuple-element.9.parts_ref, f32[8,2,28,8,128]{4,3,2,1,0:T(8,128)S(1)} %all_to_all.15.answers_ref), custom_call_target="tpu_custom_call" | custom-call | tf_op jit(solution)/shard_map/place/pallas_call | solution.py:302
  (1 shorter events, 0.0 us)
Async XLA Ops:
  8.9 18.7 %all-to-all-start = ((f32[16,25,4,128]{3,2,1,0:T(4,128)}), f32[16,25,4,128]{3,2,1,0:T(4,128)S(1)}, u32[]{:S(2)}, u32[]{:S(2)}) async-start(f32[16,25,4,128]{3,2,1,0:T(4,128)} %product.2), calls=%async_computation | async-start | bytes 1638400 | tf_op jit(solution)/shard_map/all_to_all | solution.py:335
  23.4 25.7 %copy-start = (f32[512,512]{1,0:T(8,128)S(1)}, f32[512,512]{1,0:T(8,128)}, u32[]{:S(2)}) copy-start(f32[512,512]{1,0:T(8,128)} %factor_ref.1) | copy-start | bytes 3145732
  27.6 21.5 %all-to-all-start.1 = ((f32[16,24,4,128]{3,2,1,0:T(4,128)}), f32[16,24,4,128]{3,2,1,0:T(4,128)S(1)}, u32[]{:S(2)}, u32[]{:S(2)}) async-start(f32[16,24,4,128]{3,2,1,0:T(4,128)} %product.3), calls=%async_computation.1 | async-start | bytes 1572864 | tf_op jit(solution)/shard_map/all_to_all | solution.py:337
  33.0 16.1 %collective-permute-start = (f32[32,4,4,128]{3,2,1,0:T(4,128)S(1)}, f32[32,4,4,128]{3,2,1,0:T(4,128)S(1)}, u32[]{:S(2)}, u32[]{:S(2)}) collective-permute-start(f32[32,4,4,128]{3,2,1,0:T(4,128)S(1)} %get-tuple-element.13), channel_id=1, source_target_pairs={{0,16},{16,0},{1,17},{17,1},{2,18},{18,2},{3,19},{19,3},{4,20},{20... | collective-permute-start | bytes 786440 | tf_op jit(solution)/shard_map/ppermute | solution.py:339
  50.4 15.1 %collective-permute-start.1 = (f32[32,4,4,128]{3,2,1,0:T(4,128)S(1)}, f32[32,4,4,128]{3,2,1,0:T(4,128)S(1)}, u32[]{:S(2)}, u32[]{:S(2)}) collective-permute-start(f32[32,4,4,128]{3,2,1,0:T(4,128)S(1)} %update.1.mine_ref), channel_id=1, source_target_pairs={{0,16},{16,0},{1,17},{17,1},{2,18},{18,2},{3,19},{19,3},{4,20},{20... | collective-permute-start | bytes 786440 | tf_op jit(solution)/shard_map/ppermute | solution.py:343
  51.5 14.0 %collective-permute-start.3 = (f32[32,4,4,128]{3,2,1,0:T(4,128)S(1)}, f32[32,4,4,128]{3,2,1,0:T(4,128)S(1)}, u32[]{:S(2)}, u32[]{:S(2)}) collective-permute-start(f32[32,4,4,128]{3,2,1,0:T(4,128)S(1)} %update.1.mine_ref), channel_id=1, source_target_pairs={{0,1},{1,0},{2,3},{3,2},{4,5},{5,4},{6,7},{7,6},{8,9},{9,8},{10,11... | collective-permute-start | bytes 786440 | tf_op jit(solution)/shard_map/ppermute | solution.py:344
  65.5 1.5 %collective-permute-start.2 = (f32[32,4,4,128]{3,2,1,0:T(4,128)S(1)}, f32[32,4,4,128]{3,2,1,0:T(4,128)S(1)}, u32[]{:S(2)}, u32[]{:S(2)}) collective-permute-start(f32[32,4,4,128]{3,2,1,0:T(4,128)S(1)} %collective-permute-done.1.mine_ref), channel_id=1, source_target_pairs={{0,1},{1,0},{2,3},{3,2},{4,5},{5,4},{6,7},{7,6},{8,9},{9,8},{10,11... | collective-permute-start | bytes 786440 | tf_op jit(solution)/shard_map/ppermute | solution.py:346

commit v6 on v5

--- a/solution.py
+++ b/solution.py
@@ -239,75 +239,84 @@
     )(ids, pieces, got, factor)
 
 
-def answer_kernel(slots, ids_ref, self_ref, mine_ref, mate_ref, *refs):
-    out_ref, table = refs[-2:]
-    chips = out_ref.shape[0]
-    _, tiles, rows, _ = mine_ref.shape
-    core, first = self_ref[1], self_ref[0] * chips * 2
-    mine, mate = mine_ref[...], mate_ref[...]
-    table[:, :, :rows] = jnp.where(core == 0, mine, mate)
-    table[:, :, rows:] = jnp.where(core == 0, mate, mine)
+def answer_kernel(slots, ids_ref, half_ref, table_ref, *refs):
+    out_ref = refs[-1]
+    peers = out_ref.shape[0]
+    tiles = table_ref.shape[1]
+    chips = peers // 2
+    first = half_ref[0] * peers
 
     def pick(chip, carry):
-        peer = core * chips + chip
-        for slot in range(slots):
-            row = ids_ref[peer * slots + slot]
-            out_ref[chip, 0, slot * tiles : (slot + 1) * tiles] = table[row]
-        out_ref[chip, 0, slots * tiles :] = table[first + chip * 2 + core]
+        for core in range(2):
+            peer = core * chips + chip
+            for slot in range(slots):
+                row = ids_ref[peer * slots + slot]
+                out_ref[peer, 0, slot * tiles : (slot + 1) * tiles] = table_ref[row]
+            out_ref[peer, 0, slots * tiles :] = table_ref[first + chip * 2 + core]
         return carry
 
     lax.fori_loop(0, chips, pick, 0, unroll=UNROLL)
 
 
-def answer(ids, self_at, mine, mate, chips, slots, part, cost_bytes, earlier=()):
-    row_blocks, tiles, rows, _ = mine.shape
+def answer(ids, half, table, peers, slots, part, earlier=()):
+    _, tiles, rows, _ = table.shape
     places = (slots + 1) * tiles
-    block = (chips, 1, places, 2 * rows, LANES)
+    block = (peers, 1, places, rows, LANES)
     return pl.pallas_call(
         functools.partial(answer_kernel, slots),
-        in_specs=[spec(pltpu.SMEM), spec(pltpu.SMEM), spec(pltpu.VMEM), spec(pltpu.VMEM)]
+        in_specs=[spec(pltpu.SMEM), spec(pltpu.SMEM), spec(pltpu.VMEM)]
         + [spec(pltpu.HBM)] * len(earlier),
         grid=(1,),
         out_specs=pl.BlockSpec(block, lambda i: (0, part, 0, 0, 0)),
-        out_shape=jax.ShapeDtypeStruct((chips, 2, places, 2 * rows, LANES), F32),
-        scratch_shapes=[pltpu.VMEM((row_blocks, tiles, 2 * rows, LANES), F32)],
-        input_output_aliases={4 + i: i for i in range(len(earlier))},
+        out_shape=jax.ShapeDtypeStruct((peers, 2, places, rows, LANES), F32),
+        input_output_aliases={3 + i: i for i in range(len(earlier))},
         compiler_params=params(),
         cost_estimate=pl.CostEstimate(
-            flops=cost_bytes << 14, bytes_accessed=cost_bytes, transcendentals=0
+            flops=0, bytes_accessed=8 * peers * places * rows * LANES, transcendentals=0
         ),
         name="answer",
-    )(ids, self_at, mine, mate, *earlier)
-
-
-def place_kernel(parts_ref, answers_ref, owned_hbm, returned_hbm, sems):
-    chips, parts, places, _, _ = answers_ref.shape
-    slots, _, tiles, _, _ = returned_hbm.shape
+    )(ids, half, table, *earlier)
+
+
+def place_kernel(slots, parts_ref, answers_ref, owned_hbm, returned_hbm, whole, sems):
+    peers, parts, places, rows, _ = answers_ref.shape
+    chips = peers // 2
+    tiles = places // (slots + 1)
     copies = []
     for part in range(parts):
         at = pl.ds(parts_ref[part] * chips, chips)
         for place in range(slots + 1):
-            source = answers_ref.at[:, part, place * tiles : (place + 1) * tiles]
+            cut = slice(place * tiles, (place + 1) * tiles)
+            for core in range(2):
+                whole[part, place, :, :, core * rows : (core + 1) * rows] = answers_ref[
+                    core * chips : (core + 1) * chips, part, cut
+                ]
             target = returned_hbm.at[place, at] if place < slots else owned_hbm.at[at]
-            copies.append(pltpu.make_async_copy(source, target, sems.at[part, place]))
+            copies.append(
+                pltpu.make_async_copy(whole.at[part, place], target, sems.at[part, place])
+            )
             copies[-1].start()
     for copy in copies:
         copy.wait()
 
 
 def place(parts, answers, slots):
-    chips, halves, places, rows, _ = answers.shape
+    peers, halves, places, rows, _ = answers.shape
+    chips = peers // 2
     tiles = places // (slots + 1)
-    owned = (halves * chips, tiles, rows, LANES)
+    owned = (halves * chips, tiles, 2 * rows, LANES)
     owned_rows, returned = pl.pallas_call(
-        place_kernel,
-        in_specs=[spec(pltpu.SMEM), spec(pl.ANY)],
+        functools.partial(place_kernel, slots),
+        in_specs=[spec(pltpu.SMEM), spec(pltpu.VMEM)],
         out_specs=(spec(pltpu.HBM), spec(pltpu.HBM)),
         out_shape=(
             jax.ShapeDtypeStruct(owned, F32),
             jax.ShapeDtypeStruct((slots, *owned), F32),
         ),
-        scratch_shapes=[pltpu.SemaphoreType.DMA((halves, slots + 1))],
+        scratch_shapes=[
+            pltpu.VMEM((halves, slots + 1, chips, tiles, 2 * rows, LANES), F32),
+            pltpu.SemaphoreType.DMA((halves, slots + 1)),
+        ],
         compiler_params=params(),
         name="place",
     )(parts, answers)
@@ -319,17 +328,14 @@
 
 def local(blocks, features, col_ids, row_ids, factor):
     slots = blocks.shape[0]
-    chips = lax.axis_size("chip")
     peer_axes = ("core", "chip")
     peers = lax.axis_size(peer_axes)
     row_blocks = peers * lax.axis_size("half")
-    half = lax.axis_index("half").astype(I32)
-    here = half.reshape(1)
+    here = lax.axis_index("half").astype(I32).reshape(1)
     there = 1 - here
     parts = jnp.concatenate([here, there])
-    self_at = jnp.stack([half, lax.axis_index("core").astype(I32)])
     swap = [(0, 1), (1, 0)]
-    parts, self_at, row_ids = lax.optimization_barrier((parts, self_at, row_ids))
+    parts, here, row_ids = lax.optimization_barrier((parts, here, row_ids))
 
     far = product(blocks, features, col_ids, row_ids, there, peers, True)
     far = lax.all_to_all(far, peer_axes, 0, 0)
@@ -341,11 +347,9 @@
     near_rows = update(ids, near, got, factor, slots)
 
     far_rows = lax.ppermute(near_rows, "half", swap)
-    near_mate = lax.ppermute(near_rows, "core", swap)
-    answers = answer(ids, self_at, near_rows, near_mate, chips, slots, 0, 1 << 22)
-    far_mate = lax.ppermute(far_rows, "core", swap)
-    answers = answer(ids, self_at, far_rows, far_mate, chips, slots, 1, 1 << 20, (answers,))
-    answers = lax.all_to_all(answers, "chip", 0, 0)
+    answers = answer(ids, here, near_rows, peers, slots, 0)
+    answers = answer(ids, here, far_rows, peers, slots, 1, (answers,))
+    answers = lax.all_to_all(answers, peer_axes, 0, 0)
     return place(parts, answers, slots)
 
 

time: 96.5 us -> 95.5 us (0.990)
  waiting for transfers between devices: 32.3 us -> 30.8 us
  transfers between devices with their start and end apart: 6 -> 4, of which waited for: 4 -> 3; matrix products, arithmetic and copies ran while one was open for 0% -> 0% of each run, Pallas kernels for 11% -> 11%
where the time goes in v6:
time: 95.5 us; the launch traced here: 95.1 us
  waiting for transfers between devices  30.8 us (32%)
  blocking collectives  27 us (28%)
  Pallas kernels  22.5 us (24%)
  starting transfers between devices  13.9 us (15%)
    all_to_all x1, blocking collectives, local(): answers = lax.all_to_all(answers, peer_axes, 0, 0)  27 us
    pallas_call x2, Pallas kernels, product(): pl.pallas_call(functools.partial(product_kernel, with_ids, groups, featur...  16.4 us
    ppermute x1, waiting for transfers between devices, local(): far_rows = lax.ppermute(near_rows, 'half', swap)  13.3 us
    all_to_all x1, waiting for transfers between devices, local(): near = lax.all_to_all(near, peer_axes, 0, 0)  13.3 us
    all_to_all x1, starting transfers between devices, local(): far = lax.all_to_all(far, peer_axes, 0, 0)  6.3 us
    all_to_all x1, waiting for transfers between devices, local(): far = lax.all_to_all(far, peer_axes, 0, 0)  4.16 us
    all_to_all x1, starting transfers between devices, local(): near = lax.all_to_all(near, peer_axes, 0, 0)  3.91 us
    ppermute x1, starting transfers between devices, local(): got = lax.ppermute(far_sums, 'half', swap)  2.65 us
  transfers between devices with their start and end apart: 4, of which 3 were waited for; matrix products, arithmetic and copies ran while one was open for 0% of the time, Pallas kernels for 11%

profile of v6, /device:TPU:0, one launch (start us, length us, event | category | flops | bytes accessed | tf_op | source)
XLA Modules:
  0.0 95.1 jit_solution(15320769564495568061)
XLA Ops:
  0.6 0.1 pad_add_fusion.parts_ref
  0.7 8.2 %product.2 = f32[16,25,4,128]{3,2,1,0:T(4,128)} custom-call(s32[1]{0:T(128)S(6)} %sub.3.part_ref, f32[6,128,4096]{2,1,0:T(8,128)} %blocks_hbm.3, s32[6]{0:T(128)} %ids_hbm.1, s32[6,32]{1,0:T(8,128)} %cols_hbm.3, f32[16,128,512]{2,1,0:T(8,128)} %features_hbm.3), custom_call_target="tpu_custom_call" | custom-call | flops 2415919104 | bytes 10485760 | tf_op jit(solution)/shard_map/product/pallas_call | solution.py:133
  8.9 6.3 %all-to-all-start = ((f32[16,25,4,128]{3,2,1,0:T(4,128)}), f32[16,25,4,128]{3,2,1,0:T(4,128)S(1)}, u32[]{:S(2)}, u32[]{:S(2)}) async-start(f32[16,25,4,128]{3,2,1,0:T(4,128)} %product.2), calls=%async_computation | async-start | bytes 1638400 | tf_op jit(solution)/shard_map/all_to_all | solution.py:341
  15.2 8.2 %product.3 = f32[16,24,4,128]{3,2,1,0:T(4,128)} custom-call(s32[1]{0:T(128)} %bitcast.part_ref.half_ref, f32[6,128,4096]{2,1,0:T(8,128)} %blocks_hbm.3, s32[6]{0:T(128)} %ids_hbm.1, s32[6,32]{1,0:T(8,128)} %cols_hbm.3, f32[16,128,512]{2,1,0:T(8,128)} %features_hbm.3), custom_call_target="tpu_custom_call" | custom-call | flops 2415919104 | bytes 10485760 | tf_op jit(solution)/shard_map/product/pallas_call | solution.py:133
  23.4 0.0 copy-start
  23.4 4.2 %all-to-all-done.pieces_ref = f32[16,25,4,128]{3,2,1,0:T(4,128)S(1)} async-done(((f32[16,25,4,128]{3,2,1,0:T(4,128)}), f32[16,25,4,128]{3,2,1,0:T(4,128)S(1)}, u32[]{:S(2)}, u32[]{:S(2)}) %all-to-all-start) | async-done | bytes 819232 | tf_op jit(solution)/shard_map/all_to_all | solution.py:341
  27.6 3.9 %all-to-all-start.1 = ((f32[16,24,4,128]{3,2,1,0:T(4,128)}), f32[16,24,4,128]{3,2,1,0:T(4,128)S(1)}, u32[]{:S(2)}, u32[]{:S(2)}) async-start(f32[16,24,4,128]{3,2,1,0:T(4,128)} %product.3), calls=%async_computation.1 | async-start | bytes 1572864 | tf_op jit(solution)/shard_map/all_to_all | solution.py:343
  31.5 1.5 %sum_pieces.1 = (f32[32,4,4,128]{3,2,1,0:T(4,128)S(1)}, s32[16,4,128]{2,1,0:T(4,128)S(1)}) custom-call(f32[16,25,4,128]{3,2,1,0:T(4,128)S(1)} %all-to-all-done.pieces_ref), custom_call_target="tpu_custom_call" | custom-call | tf_op jit(solution)/shard_map/sum_pieces/pallas_call | solution.py:190
  33.0 2.6 %collective-permute-start = (f32[32,4,4,128]{3,2,1,0:T(4,128)S(1)}, f32[32,4,4,128]{3,2,1,0:T(4,128)S(1)}, u32[]{:S(2)}, u32[]{:S(2)}) collective-permute-start(f32[32,4,4,128]{3,2,1,0:T(4,128)S(1)} %get-tuple-element.13), channel_id=1, source_target_pairs={{0,16},{16,0},{1,17},{17,1},{2,18},{18,2},{3,19},{19,3},{4,20},{20... | collective-permute-start | bytes 786440 | tf_op jit(solution)/shard_map/ppermute | solution.py:345
  35.7 0.1 reshape_squeeze.3.ids_ref
  35.8 13.3 %all-to-all-done.1.pieces_ref = f32[16,24,4,128]{3,2,1,0:T(4,128)S(1)} async-done(((f32[16,24,4,128]{3,2,1,0:T(4,128)}), f32[16,24,4,128]{3,2,1,0:T(4,128)S(1)}, u32[]{:S(2)}, u32[]{:S(2)}) %all-to-all-start.1) | async-done | bytes 786464 | tf_op jit(solution)/shard_map/all_to_all | solution.py:343
  49.1 0.0 collective-permute-done.got_ref
  49.1 0.0 copy-done
  49.1 1.4 %update.1.table_ref = f32[32,4,4,128]{3,2,1,0:T(4,128)S(1)} custom-call(s32[96]{0:T(128)S(1)} %reshape_squeeze.3.ids_ref, f32[16,24,4,128]{3,2,1,0:T(4,128)S(1)} %all-to-all-done.1.pieces_ref, f32[32,4,4,128]{3,2,1,0:T(4,128)S(1)} %collective-permute-done.got_ref, f32[512,512]{1,0:T(8,128)S(1)} %copy-done), custom_call_target="tpu_custom_call" | custom-call | tf_op jit(solution)/shard_map/update/pallas_call | solution.py:227
  50.4 1.1 %collective-permute-start.1 = (f32[32,4,4,128]{3,2,1,0:T(4,128)S(1)}, f32[32,4,4,128]{3,2,1,0:T(4,128)S(1)}, u32[]{:S(2)}, u32[]{:S(2)}) collective-permute-start(f32[32,4,4,128]{3,2,1,0:T(4,128)S(1)} %update.1.table_ref), channel_id=1, source_target_pairs={{0,16},{16,0},{1,17},{17,1},{2,18},{18,2},{3,19},{19,3},{4,20},{20... | collective-permute-start | bytes 786440 | tf_op jit(solution)/shard_map/ppermute | solution.py:349
  51.5 0.7 answer.2.refs_0_
  52.2 13.3 %collective-permute-done.1.table_ref = f32[32,4,4,128]{3,2,1,0:T(4,128)S(1)} collective-permute-done((f32[32,4,4,128]{3,2,1,0:T(4,128)S(1)}, f32[32,4,4,128]{3,2,1,0:T(4,128)S(1)}, u32[]{:S(2)}, u32[]{:S(2)}) %collective-permute-start.1) | collective-permute-done | bytes 262176 | tf_op jit(solution)/shard_map/ppermute | solution.py:349
  65.5 0.7 answer.3
  66.2 27.0 %all_to_all.15.answers_ref = f32[16,2,28,4,128]{4,3,2,1,0:T(4,128)S(1)} all-to-all(f32[16,2,28,4,128]{4,3,2,1,0:T(4,128)S(1)} %answer.3), channel_id=1, replica_groups=mesh['half'=2,'chip'=8,'core'=2] {'core','chip'}, dimensions={0} | all-to-all | bytes 3670016 | tf_op jit(solution)/shard_map/all_to_all | solution.py:352
  93.2 1.9 %place.1 = (f32[16,4,8,128]{3,2,1,0:T(8,128)}, f32[6,16,4,8,128]{4,3,2,1,0:T(8,128)}) custom-call(s32[2]{0:T(128)S(1)} %pad_add_fusion.parts_ref, f32[16,2,28,4,128]{4,3,2,1,0:T(4,128)S(1)} %all_to_all.15.answers_ref), custom_call_target="tpu_custom_call" | custom-call | tf_op jit(solution)/shard_map/place/pallas_call | solution.py:308
  (1 shorter events, 0.0 us)
Async XLA Ops:
  8.9 18.7 %all-to-all-start = ((f32[16,25,4,128]{3,2,1,0:T(4,128)}), f32[16,25,4,128]{3,2,1,0:T(4,128)S(1)}, u32[]{:S(2)}, u32[]{:S(2)}) async-start(f32[16,25,4,128]{3,2,1,0:T(4,128)} %product.2), calls=%async_computation | async-start | bytes 1638400 | tf_op jit(solution)/shard_map/all_to_all | solution.py:341
  23.4 25.7 %copy-start = (f32[512,512]{1,0:T(8,128)S(1)}, f32[512,512]{1,0:T(8,128)}, u32[]{:S(2)}) copy-start(f32[512,512]{1,0:T(8,128)} %factor_ref.1) | copy-start | bytes 3145732
  27.6 21.5 %all-to-all-start.1 = ((f32[16,24,4,128]{3,2,1,0:T(4,128)}), f32[16,24,4,128]{3,2,1,0:T(4,128)S(1)}, u32[]{:S(2)}, u32[]{:S(2)}) async-start(f32[16,24,4,128]{3,2,1,0:T(4,128)} %product.3), calls=%async_computation.1 | async-start | bytes 1572864 | tf_op jit(solution)/shard_map/all_to_all | solution.py:343
  33.0 16.1 %collective-permute-start = (f32[32,4,4,128]{3,2,1,0:T(4,128)S(1)}, f32[32,4,4,128]{3,2,1,0:T(4,128)S(1)}, u32[]{:S(2)}, u32[]{:S(2)}) collective-permute-start(f32[32,4,4,128]{3,2,1,0:T(4,128)S(1)} %get-tuple-element.13), channel_id=1, source_target_pairs={{0,16},{16,0},{1,17},{17,1},{2,18},{18,2},{3,19},{19,3},{4,20},{20... | collective-permute-start | bytes 786440 | tf_op jit(solution)/shard_map/ppermute | solution.py:345
  50.4 15.1 %collective-permute-start.1 = (f32[32,4,4,128]{3,2,1,0:T(4,128)S(1)}, f32[32,4,4,128]{3,2,1,0:T(4,128)S(1)}, u32[]{:S(2)}, u32[]{:S(2)}) collective-permute-start(f32[32,4,4,128]{3,2,1,0:T(4,128)S(1)} %update.1.table_ref), channel_id=1, source_target_pairs={{0,16},{16,0},{1,17},{17,1},{2,18},{18,2},{3,19},{19,3},{4,20},{20... | collective-permute-start | bytes 786440 | tf_op jit(solution)/shard_map/ppermute | solution.py:349

commit v7 on v6

--- a/solution.py
+++ b/solution.py
@@ -239,8 +239,7 @@
     )(ids, pieces, got, factor)
 
 
-def answer_kernel(slots, ids_ref, half_ref, table_ref, *refs):
-    out_ref = refs[-1]
+def answer_kernel(slots, ids_ref, half_ref, table_ref, out_ref):
     peers = out_ref.shape[0]
     tiles = table_ref.shape[1]
     chips = peers // 2
@@ -251,79 +250,70 @@
             peer = core * chips + chip
             for slot in range(slots):
                 row = ids_ref[peer * slots + slot]
-                out_ref[peer, 0, slot * tiles : (slot + 1) * tiles] = table_ref[row]
-            out_ref[peer, 0, slots * tiles :] = table_ref[first + chip * 2 + core]
+                out_ref[peer, slot * tiles : (slot + 1) * tiles] = table_ref[row]
+            out_ref[peer, slots * tiles :] = table_ref[first + chip * 2 + core]
         return carry
 
     lax.fori_loop(0, chips, pick, 0, unroll=UNROLL)
 
 
-def answer(ids, half, table, peers, slots, part, earlier=()):
+def answer(ids, half, table, peers, slots, flops):
     _, tiles, rows, _ = table.shape
-    places = (slots + 1) * tiles
-    block = (peers, 1, places, rows, LANES)
+    out = (peers, (slots + 1) * tiles, rows, LANES)
     return pl.pallas_call(
         functools.partial(answer_kernel, slots),
-        in_specs=[spec(pltpu.SMEM), spec(pltpu.SMEM), spec(pltpu.VMEM)]
-        + [spec(pltpu.HBM)] * len(earlier),
-        grid=(1,),
-        out_specs=pl.BlockSpec(block, lambda i: (0, part, 0, 0, 0)),
-        out_shape=jax.ShapeDtypeStruct((peers, 2, places, rows, LANES), F32),
-        input_output_aliases={3 + i: i for i in range(len(earlier))},
+        in_specs=[spec(pltpu.SMEM), spec(pltpu.SMEM), spec(pltpu.VMEM)],
+        out_specs=spec(pltpu.VMEM),
+        out_shape=jax.ShapeDtypeStruct(out, F32),
         compiler_params=params(),
         cost_estimate=pl.CostEstimate(
-            flops=0, bytes_accessed=8 * peers * places * rows * LANES, transcendentals=0
+            flops=flops, bytes_accessed=8 * peers * out[1] * rows * LANES, transcendentals=0
         ),
         name="answer",
-    )(ids, half, table, *earlier)
-
-
-def place_kernel(slots, parts_ref, answers_ref, owned_hbm, returned_hbm, whole, sems):
-    peers, parts, places, rows, _ = answers_ref.shape
+    )(ids, half, table)
+
+
+def place_kernel(slots, part_ref, answers_ref, *refs):
+    owned_hbm, returned_hbm, whole, sems = refs[-4:]
+    peers, places, rows, _ = answers_ref.shape
     chips = peers // 2
     tiles = places // (slots + 1)
+    at = pl.ds(part_ref[0] * chips, chips)
     copies = []
-    for part in range(parts):
-        at = pl.ds(parts_ref[part] * chips, chips)
-        for place in range(slots + 1):
-            cut = slice(place * tiles, (place + 1) * tiles)
-            for core in range(2):
-                whole[part, place, :, :, core * rows : (core + 1) * rows] = answers_ref[
-                    core * chips : (core + 1) * chips, part, cut
-                ]
-            target = returned_hbm.at[place, at] if place < slots else owned_hbm.at[at]
-            copies.append(
-                pltpu.make_async_copy(whole.at[part, place], target, sems.at[part, place])
-            )
-            copies[-1].start()
+    for place in range(slots + 1):
+        cut = slice(place * tiles, (place + 1) * tiles)
+        for core in range(2):
+            whole[place, :, :, core * rows : (core + 1) * rows] = answers_ref[
+                core * chips : (core + 1) * chips, cut
+            ]
+        target = returned_hbm.at[place, at] if place < slots else owned_hbm.at[at]
+        copies.append(pltpu.make_async_copy(whole.at[place], target, sems.at[place]))
+        copies[-1].start()
     for copy in copies:
         copy.wait()
 
 
-def place(parts, answers, slots):
-    peers, halves, places, rows, _ = answers.shape
+def place(part, answers, slots, earlier=()):
+    peers, places, rows, _ = answers.shape
     chips = peers // 2
     tiles = places // (slots + 1)
-    owned = (halves * chips, tiles, 2 * rows, LANES)
-    owned_rows, returned = pl.pallas_call(
+    owned = (2 * chips, tiles, 2 * rows, LANES)
+    return pl.pallas_call(
         functools.partial(place_kernel, slots),
-        in_specs=[spec(pltpu.SMEM), spec(pltpu.VMEM)],
+        in_specs=[spec(pltpu.SMEM), spec(pltpu.VMEM)] + [spec(pltpu.HBM)] * len(earlier),
         out_specs=(spec(pltpu.HBM), spec(pltpu.HBM)),
         out_shape=(
             jax.ShapeDtypeStruct(owned, F32),
             jax.ShapeDtypeStruct((slots, *owned), F32),
         ),
         scratch_shapes=[
-            pltpu.VMEM((halves, slots + 1, chips, tiles, 2 * rows, LANES), F32),
-            pltpu.SemaphoreType.DMA((halves, slots + 1)),
+            pltpu.VMEM((slots + 1, chips, tiles, 2 * rows, LANES), F32),
+            pltpu.SemaphoreType.DMA((slots + 1,)),
         ],
+        input_output_aliases={2 + i: i for i in range(len(earlier))},
         compiler_params=params(),
         name="place",
-    )(parts, answers)
-    feat = tiles * LANES
-    owned_rows = owned_rows.transpose(0, 2, 1, 3).reshape(-1, feat)
-    returned = returned.transpose(0, 1, 3, 2, 4).reshape(-1, feat)
-    return owned_rows, returned
+    )(part, answers, *earlier)
 
 
 def local(blocks, features, col_ids, row_ids, factor):
@@ -333,9 +323,8 @@
     row_blocks = peers * lax.axis_size("half")
     here = lax.axis_index("half").astype(I32).reshape(1)
     there = 1 - here
-    parts = jnp.concatenate([here, there])
     swap = [(0, 1), (1, 0)]
-    parts, here, row_ids = lax.optimization_barrier((parts, here, row_ids))
+    here, there, row_ids = lax.optimization_barrier((here, there, row_ids))
 
     far = product(blocks, features, col_ids, row_ids, there, peers, True)
     far = lax.all_to_all(far, peer_axes, 0, 0)
@@ -347,10 +336,15 @@
     near_rows = update(ids, near, got, factor, slots)
 
     far_rows = lax.ppermute(near_rows, "half", swap)
-    answers = answer(ids, here, near_rows, peers, slots, 0)
-    answers = answer(ids, here, far_rows, peers, slots, 1, (answers,))
-    answers = lax.all_to_all(answers, peer_axes, 0, 0)
-    return place(parts, answers, slots)
+    near_answers = lax.all_to_all(answer(ids, here, near_rows, peers, slots, 0), peer_axes, 0, 0)
+    far_answers = answer(ids, here, far_rows, peers, slots, 1 << 34)
+    far_answers = lax.all_to_all(far_answers, peer_axes, 0, 0)
+    outputs = place(here, near_answers, slots)
+    owned_rows, returned = place(there, far_answers, slots, outputs)
+    feat = returned.shape[2] * LANES
+    owned_rows = owned_rows.transpose(0, 2, 1, 3).reshape(-1, feat)
+    returned = returned.transpose(0, 1, 3, 2, 4).reshape(-1, feat)
+    return owned_rows, returned
 
 
 def solution(mesh):

time: 95.5 us -> 94.4 us (0.988)
  blocking collectives: 27 us -> 0 us
  waiting for transfers between devices: 30.8 us -> 45.6 us
  starting transfers between devices: 13.9 us -> 23.1 us
  Pallas kernels: 22.5 us -> 24.3 us
    all_to_all x1 -> x0, blocking collectives: 27 us -> none  [local(): answers = lax.all_to_all(answers, peer_axes, 0, 0)]
    all_to_all x0 -> x2, waiting for transfers between devices: none -> 21.2 us  [the longest x1 12.3 us: local(): far_answers = lax.all_to_all(far_answers, peer_axes, 0, 0)]
    all_to_all x0 -> x2, starting transfers between devices: none -> 9.21 us  [the longest x1 5.58 us: local(): lax.all_to_all(answer(ids, here, near_rows, peers, slots, 0), peer_axes,...]
    ppermute x1, waiting for transfers between devices: 13.3 us -> 7 us  [local(): far_rows = lax.ppermute(near_rows, 'half', swap)]
    pallas_call x2, Pallas kernels: 1.36 us -> 3.09 us  [answer(): pl.pallas_call(functools.partial(answer_kernel, slots), in_specs=[spec(pl...]
    pallas_call x1 -> x2, Pallas kernels: 1.9 us -> 1.99 us  [place(): pl.pallas_call(functools.partial(place_kernel, slots), in_specs=[spec(plt...]
  transfers between devices with their start and end apart: 4 -> 6, of which waited for: 3 -> 5; matrix products, arithmetic and copies ran while one was open for 0% -> 0% of each run, Pallas kernels for 11% -> 15%
where the time goes in v7:
time: 94.4 us; the launch traced here: 93.9 us
  waiting for transfers between devices  45.6 us (48%)
  Pallas kernels  24.3 us (26%)
  starting transfers between devices  23.1 us (24%)
    pallas_call x2, Pallas kernels, product(): pl.pallas_call(functools.partial(product_kernel, with_ids, groups, featur...  16.4 us
    all_to_all x1, waiting for transfers between devices, local(): near = lax.all_to_all(near, peer_axes, 0, 0)  13.3 us
    all_to_all x1, waiting for transfers between devices, local(): far_answers = lax.all_to_all(far_answers, peer_axes, 0, 0)  12.3 us
    all_to_all x1, waiting for transfers between devices, local(): lax.all_to_all(answer(ids, here, near_rows, peers, slots, 0), peer_axes,...  8.85 us
    ppermute x1, waiting for transfers between devices, local(): far_rows = lax.ppermute(near_rows, 'half', swap)  7 us
    all_to_all x1, starting transfers between devices, local(): far = lax.all_to_all(far, peer_axes, 0, 0)  6.3 us
    all_to_all x1, starting transfers between devices, local(): lax.all_to_all(answer(ids, here, near_rows, peers, slots, 0), peer_axes,...  5.58 us
    all_to_all x1, waiting for transfers between devices, local(): far = lax.all_to_all(far, peer_axes, 0, 0)  4.1 us
  transfers between devices with their start and end apart: 6, of which 5 were waited for; matrix products, arithmetic and copies ran while one was open for 0% of the time, Pallas kernels for 15%

profile of v7, /device:TPU:0, one launch (start us, length us, event | category | flops | bytes accessed | tf_op | source)
XLA Modules:
  0.0 93.9 jit_solution(15578419674198730183)
XLA Ops:
  0.6 8.2 %product.2 = f32[16,25,4,128]{3,2,1,0:T(4,128)} custom-call(s32[1]{0:T(128)S(6)} %sub.3.part_ref, f32[6,128,4096]{2,1,0:T(8,128)} %blocks_hbm.3, s32[6]{0:T(128)} %ids_hbm.1, s32[6,32]{1,0:T(8,128)} %cols_hbm.3, f32[16,128,512]{2,1,0:T(8,128)} %features_hbm.3), custom_call_target="tpu_custom_call" | custom-call | flops 2415919104 | bytes 10485760 | tf_op jit(solution)/shard_map/product/pallas_call | solution.py:133
  8.8 6.3 %all-to-all-start = ((f32[16,25,4,128]{3,2,1,0:T(4,128)}), f32[16,25,4,128]{3,2,1,0:T(4,128)S(1)}, u32[]{:S(2)}, u32[]{:S(2)}) async-start(f32[16,25,4,128]{3,2,1,0:T(4,128)} %product.2), calls=%async_computation | async-start | bytes 1638400 | tf_op jit(solution)/shard_map/all_to_all | solution.py:330
  15.1 0.0 copy-start
  15.1 8.2 %product.3 = f32[16,24,4,128]{3,2,1,0:T(4,128)} custom-call(s32[1]{0:T(128)} %bitcast.part_ref.half_ref, f32[6,128,4096]{2,1,0:T(8,128)} %blocks_hbm.3, s32[6]{0:T(128)} %ids_hbm.1, s32[6,32]{1,0:T(8,128)} %cols_hbm.3, f32[16,128,512]{2,1,0:T(8,128)} %features_hbm.3), custom_call_target="tpu_custom_call" | custom-call | flops 2415919104 | bytes 10485760 | tf_op jit(solution)/shard_map/product/pallas_call | solution.py:133
  23.4 4.1 %all-to-all-done.pieces_ref = f32[16,25,4,128]{3,2,1,0:T(4,128)S(1)} async-done(((f32[16,25,4,128]{3,2,1,0:T(4,128)}), f32[16,25,4,128]{3,2,1,0:T(4,128)S(1)}, u32[]{:S(2)}, u32[]{:S(2)}) %all-to-all-start) | async-done | bytes 819232 | tf_op jit(solution)/shard_map/all_to_all | solution.py:330
  27.5 3.9 %all-to-all-start.1 = ((f32[16,24,4,128]{3,2,1,0:T(4,128)}), f32[16,24,4,128]{3,2,1,0:T(4,128)S(1)}, u32[]{:S(2)}, u32[]{:S(2)}) async-start(f32[16,24,4,128]{3,2,1,0:T(4,128)} %product.3), calls=%async_computation.1 | async-start | bytes 1572864 | tf_op jit(solution)/shard_map/all_to_all | solution.py:332
  31.4 1.5 %sum_pieces.1 = (f32[32,4,4,128]{3,2,1,0:T(4,128)S(1)}, s32[16,4,128]{2,1,0:T(4,128)S(1)}) custom-call(f32[16,25,4,128]{3,2,1,0:T(4,128)S(1)} %all-to-all-done.pieces_ref), custom_call_target="tpu_custom_call" | custom-call | tf_op jit(solution)/shard_map/sum_pieces/pallas_call | solution.py:190
  32.9 2.6 %collective-permute-start = (f32[32,4,4,128]{3,2,1,0:T(4,128)S(1)}, f32[32,4,4,128]{3,2,1,0:T(4,128)S(1)}, u32[]{:S(2)}, u32[]{:S(2)}) collective-permute-start(f32[32,4,4,128]{3,2,1,0:T(4,128)S(1)} %get-tuple-element.15), channel_id=1, source_target_pairs={{0,16},{16,0},{1,17},{17,1},{2,18},{18,2},{3,19},{19,3},{4,20},{20... | collective-permute-start | bytes 786440 | tf_op jit(solution)/shard_map/ppermute | solution.py:334
  35.6 0.1 reshape_squeeze.3.ids_ref
  35.6 13.3 %all-to-all-done.1.pieces_ref = f32[16,24,4,128]{3,2,1,0:T(4,128)S(1)} async-done(((f32[16,24,4,128]{3,2,1,0:T(4,128)}), f32[16,24,4,128]{3,2,1,0:T(4,128)S(1)}, u32[]{:S(2)}, u32[]{:S(2)}) %all-to-all-start.1) | async-done | bytes 786464 | tf_op jit(solution)/shard_map/all_to_all | solution.py:332
  49.0 0.0 collective-permute-done.got_ref
  49.0 0.0 copy-done
  49.0 1.3 %update.1.table_ref = f32[32,4,4,128]{3,2,1,0:T(4,128)S(1)} custom-call(s32[96]{0:T(128)S(1)} %reshape_squeeze.3.ids_ref, f32[16,24,4,128]{3,2,1,0:T(4,128)S(1)} %all-to-all-done.1.pieces_ref, f32[32,4,4,128]{3,2,1,0:T(4,128)S(1)} %collective-permute-done.got_ref, f32[512,512]{1,0:T(8,128)S(1)} %copy-done), custom_call_target="tpu_custom_call" | custom-call | tf_op jit(solution)/shard_map/update/pallas_call | solution.py:227
  50.3 1.1 %collective-permute-start.1 = (f32[32,4,4,128]{3,2,1,0:T(4,128)S(1)}, f32[32,4,4,128]{3,2,1,0:T(4,128)S(1)}, u32[]{:S(2)}, u32[]{:S(2)}) collective-permute-start(f32[32,4,4,128]{3,2,1,0:T(4,128)S(1)} %update.1.table_ref), channel_id=1, source_target_pairs={{0,16},{16,0},{1,17},{17,1},{2,18},{18,2},{3,19},{19,3},{4,20},{20... | collective-permute-start | bytes 786440 | tf_op jit(solution)/shard_map/ppermute | solution.py:338
  51.4 1.5 %answer.3 = f32[16,28,4,128]{3,2,1,0:T(4,128)} custom-call(s32[96]{0:T(128)S(1)} %reshape_squeeze.3.ids_ref, s32[1]{0:T(128)} %bitcast.part_ref.half_ref, f32[32,4,4,128]{3,2,1,0:T(4,128)S(1)} %update.1.table_ref), custom_call_target="tpu_custom_call" | custom-call | bytes 1835008 | tf_op jit(solution)/shard_map/answer/pallas_call | solution.py:263
  53.0 5.6 %all-to-all-start.3 = ((f32[16,28,4,128]{3,2,1,0:T(4,128)}), f32[16,28,4,128]{3,2,1,0:T(4,128)S(1)}, u32[]{:S(2)}, u32[]{:S(2)}) async-start(f32[16,28,4,128]{3,2,1,0:T(4,128)} %answer.3), calls=%async_computation.3 | async-start | bytes 1835008 | tf_op jit(solution)/shard_map/all_to_all | solution.py:339
  58.5 7.0 %collective-permute-done.1.table_ref = f32[32,4,4,128]{3,2,1,0:T(4,128)S(1)} collective-permute-done((f32[32,4,4,128]{3,2,1,0:T(4,128)S(1)}, f32[32,4,4,128]{3,2,1,0:T(4,128)S(1)}, u32[]{:S(2)}, u32[]{:S(2)}) %collective-permute-start.1) | collective-permute-done | bytes 262176 | tf_op jit(solution)/shard_map/ppermute | solution.py:338
  65.5 1.5 %answer.2 = f32[16,28,4,128]{3,2,1,0:T(4,128)} custom-call(s32[96]{0:T(128)S(1)} %reshape_squeeze.3.ids_ref, s32[1]{0:T(128)} %bitcast.part_ref.half_ref, f32[32,4,4,128]{3,2,1,0:T(4,128)S(1)} %collective-permute-done.1.table_ref), custom_call_target="tpu_custom_call" | custom-call | flops 17179869184 | bytes 1835008 | tf_op jit(solution)/shard_map/answer/pallas_call | solution.py:263
  67.1 8.8 %all-to-all-done.3.answers_ref = f32[16,28,4,128]{3,2,1,0:T(4,128)S(1)} async-done(((f32[16,28,4,128]{3,2,1,0:T(4,128)}), f32[16,28,4,128]{3,2,1,0:T(4,128)S(1)}, u32[]{:S(2)}, u32[]{:S(2)}) %all-to-all-start.3) | async-done | bytes 917536 | tf_op jit(solution)/shard_map/all_to_all | solution.py:339
  75.9 3.6 %all-to-all-start.2 = ((f32[16,28,4,128]{3,2,1,0:T(4,128)}), f32[16,28,4,128]{3,2,1,0:T(4,128)S(1)}, u32[]{:S(2)}, u32[]{:S(2)}) async-start(f32[16,28,4,128]{3,2,1,0:T(4,128)} %answer.2), calls=%async_computation.2 | async-start | bytes 1835008 | tf_op jit(solution)/shard_map/all_to_all | solution.py:341
  79.6 1.0 %place.2 = (f32[16,4,8,128]{3,2,1,0:T(8,128)}, f32[6,16,4,8,128]{4,3,2,1,0:T(8,128)}) custom-call(s32[1]{0:T(128)} %bitcast.part_ref.half_ref, f32[16,28,4,128]{3,2,1,0:T(4,128)S(1)} %all-to-all-done.3.answers_ref), custom_call_target="tpu_custom_call" | custom-call | tf_op jit(solution)/shard_map/place/pallas_call | solution.py:301
  80.6 12.3 %all-to-all-done.2.answers_ref = f32[16,28,4,128]{3,2,1,0:T(4,128)S(1)} async-done(((f32[16,28,4,128]{3,2,1,0:T(4,128)}), f32[16,28,4,128]{3,2,1,0:T(4,128)S(1)}, u32[]{:S(2)}, u32[]{:S(2)}) %all-to-all-start.2) | async-done | bytes 917536 | tf_op jit(solution)/shard_map/all_to_all | solution.py:341
  92.9 1.0 %place.3 = (f32[16,4,8,128]{3,2,1,0:T(8,128)}, f32[6,16,4,8,128]{4,3,2,1,0:T(8,128)}) custom-call(s32[1]{0:T(128)S(6)} %sub.3.part_ref, f32[16,28,4,128]{3,2,1,0:T(4,128)S(1)} %all-to-all-done.2.answers_ref, f32[16,4,8,128]{3,2,1,0:T(8,128)} %get-tuple-element.16.refs_0_, ...), custom_call_target="tpu_custom_call", output_to_operand_aliasing={{0}: (2, {}), {1}: (3, {})} | custom-call | tf_op jit(solution)/shard_map/place/pallas_call | solution.py:301
  (1 shorter events, 0.0 us)
Async XLA Ops:
  8.8 18.7 %all-to-all-start = ((f32[16,25,4,128]{3,2,1,0:T(4,128)}), f32[16,25,4,128]{3,2,1,0:T(4,128)S(1)}, u32[]{:S(2)}, u32[]{:S(2)}) async-start(f32[16,25,4,128]{3,2,1,0:T(4,128)} %product.2), calls=%async_computation | async-start | bytes 1638400 | tf_op jit(solution)/shard_map/all_to_all | solution.py:330
  15.1 33.9 %copy-start = (f32[512,512]{1,0:T(8,128)S(1)}, f32[512,512]{1,0:T(8,128)}, u32[]{:S(2)}) copy-start(f32[512,512]{1,0:T(8,128)} %factor_ref.1) | copy-start | bytes 3145732
  27.5 21.5 %all-to-all-start.1 = ((f32[16,24,4,128]{3,2,1,0:T(4,128)}), f32[16,24,4,128]{3,2,1,0:T(4,128)S(1)}, u32[]{:S(2)}, u32[]{:S(2)}) async-start(f32[16,24,4,128]{3,2,1,0:T(4,128)} %product.3), calls=%async_computation.1 | async-start | bytes 1572864 | tf_op jit(solution)/shard_map/all_to_all | solution.py:332
  32.9 16.1 %collective-permute-start = (f32[32,4,4,128]{3,2,1,0:T(4,128)S(1)}, f32[32,4,4,128]{3,2,1,0:T(4,128)S(1)}, u32[]{:S(2)}, u32[]{:S(2)}) collective-permute-start(f32[32,4,4,128]{3,2,1,0:T(4,128)S(1)} %get-tuple-element.15), channel_id=1, source_target_pairs={{0,16},{16,0},{1,17},{17,1},{2,18},{18,2},{3,19},{19,3},{4,20},{20... | collective-permute-start | bytes 786440 | tf_op jit(solution)/shard_map/ppermute | solution.py:334
  50.3 15.2 %collective-permute-start.1 = (f32[32,4,4,128]{3,2,1,0:T(4,128)S(1)}, f32[32,4,4,128]{3,2,1,0:T(4,128)S(1)}, u32[]{:S(2)}, u32[]{:S(2)}) collective-permute-start(f32[32,4,4,128]{3,2,1,0:T(4,128)S(1)} %update.1.table_ref), channel_id=1, source_target_pairs={{0,16},{16,0},{1,17},{17,1},{2,18},{18,2},{3,19},{19,3},{4,20},{20... | collective-permute-start | bytes 786440 | tf_op jit(solution)/shard_map/ppermute | solution.py:338
  53.0 23.0 %all-to-all-start.3 = ((f32[16,28,4,128]{3,2,1,0:T(4,128)}), f32[16,28,4,128]{3,2,1,0:T(4,128)S(1)}, u32[]{:S(2)}, u32[]{:S(2)}) async-start(f32[16,28,4,128]{3,2,1,0:T(4,128)} %answer.3), calls=%async_computation.3 | async-start | bytes 1835008 | tf_op jit(solution)/shard_map/all_to_all | solution.py:339
  75.9 17.0 %all-to-all-start.2 = ((f32[16,28,4,128]{3,2,1,0:T(4,128)}), f32[16,28,4,128]{3,2,1,0:T(4,128)S(1)}, u32[]{:S(2)}, u32[]{:S(2)}) async-start(f32[16,28,4,128]{3,2,1,0:T(4,128)} %answer.2), calls=%async_computation.2 | async-start | bytes 1835008 | tf_op jit(solution)/shard_map/all_to_all | solution.py:341

commit v8 on v7

--- a/solution.py
+++ b/solution.py
@@ -205,7 +205,9 @@
     )(pieces)
 
 
-def update_kernel(slots, ids_ref, pieces_ref, got_ref, factor_ref, out_ref, total, other, left):
+def update_kernel(
+    slots, ids_ref, half_ref, pieces_ref, got_ref, factor_ref, out_ref, answers_ref, total, other, left
+):
     row_blocks, tiles, rows, _ = out_ref.shape
     total[...] = got_ref[...]
     other[...] = jnp.zeros_like(other)
@@ -220,15 +222,20 @@
     for row in range(row_blocks):
         for t in range(tiles):
             out_ref[row, t] = out[row * rows : (row + 1) * rows, t * LANES : (t + 1) * LANES]
-
-
-def update(ids, pieces, got, factor, slots):
+    answer_kernel(slots, ids_ref, half_ref, out_ref, answers_ref)
+
+
+def update(ids, half, pieces, got, factor, slots):
     row_blocks, tiles, rows, _ = got.shape
+    answers = (pieces.shape[0], (slots + 1) * tiles, rows, LANES)
     return pl.pallas_call(
         functools.partial(update_kernel, slots),
-        in_specs=[spec(pltpu.SMEM), spec(pltpu.VMEM), spec(pltpu.VMEM), spec(pltpu.VMEM)],
-        out_specs=spec(pltpu.VMEM),
-        out_shape=jax.ShapeDtypeStruct(got.shape, F32),
+        in_specs=[spec(pltpu.SMEM)] * 2 + [spec(pltpu.VMEM)] * 3,
+        out_specs=(spec(pltpu.VMEM), spec(pltpu.VMEM)),
+        out_shape=(
+            jax.ShapeDtypeStruct(got.shape, F32),
+            jax.ShapeDtypeStruct(answers, F32),
+        ),
         scratch_shapes=[
             pltpu.VMEM(got.shape, F32),
             pltpu.VMEM(got.shape, F32),
@@ -236,7 +243,7 @@
         ],
         compiler_params=params(),
         name="update",
-    )(ids, pieces, got, factor)
+    )(ids, half, pieces, got, factor)
 
 
 def answer_kernel(slots, ids_ref, half_ref, table_ref, out_ref):
@@ -333,10 +340,10 @@
     far_sums, ids = sum_pieces(far, row_blocks, slots)
     got = lax.ppermute(far_sums, "half", swap)
     ids = ids[:, 0, :slots].reshape(-1)
-    near_rows = update(ids, near, got, factor, slots)
+    near_rows, near_answers = update(ids, here, near, got, factor, slots)
 
     far_rows = lax.ppermute(near_rows, "half", swap)
-    near_answers = lax.all_to_all(answer(ids, here, near_rows, peers, slots, 0), peer_axes, 0, 0)
+    near_answers = lax.all_to_all(near_answers, peer_axes, 0, 0)
     far_answers = answer(ids, here, far_rows, peers, slots, 1 << 34)
     far_answers = lax.all_to_all(far_answers, peer_axes, 0, 0)
     outputs = place(here, near_answers, slots)

time: 94.4 us -> 94.1 us (level)
    pallas_call x2 -> x1, Pallas kernels: 3.09 us -> 1.54 us  [answer(): pl.pallas_call(functools.partial(answer_kernel, slots), in_specs=[spec(pl...]
    ppermute x1, waiting for transfers between devices: 7 us -> 8.53 us  [local(): far_rows = lax.ppermute(near_rows, 'half', swap)]
    all_to_all x1, waiting for transfers between devices: 8.85 us -> 7.65 us  [local(): near_answers = lax.all_to_all(near_answers, peer_axes, 0, 0)]
    pallas_call x1, Pallas kernels: 1.35 us -> 2.34 us  [update(): pl.pallas_call(functools.partial(update_kernel, slots), in_specs=[spec(pl...]
  transfers between devices with their start and end apart: 6 -> 6, of which waited for: 5 -> 5; matrix products, arithmetic and copies ran while one was open for 0% -> 0% of each run, Pallas kernels for 15% -> 13%
where the time goes in v8:
time: 94.1 us; the launch traced here: 93.7 us
  waiting for transfers between devices  46 us (49%)
  Pallas kernels  23.8 us (25%)
  starting transfers between devices  23.1 us (25%)
    pallas_call x2, Pallas kernels, product(): pl.pallas_call(functools.partial(product_kernel, with_ids, groups, featur...  16.4 us
    all_to_all x1, waiting for transfers between devices, local(): near = lax.all_to_all(near, peer_axes, 0, 0)  13.3 us
    all_to_all x1, waiting for transfers between devices, local(): far_answers = lax.all_to_all(far_answers, peer_axes, 0, 0)  12.4 us
    ppermute x1, waiting for transfers between devices, local(): far_rows = lax.ppermute(near_rows, 'half', swap)  8.53 us
    all_to_all x1, waiting for transfers between devices, local(): near_answers = lax.all_to_all(near_answers, peer_axes, 0, 0)  7.65 us
    all_to_all x1, starting transfers between devices, local(): far = lax.all_to_all(far, peer_axes, 0, 0)  6.29 us
    all_to_all x1, starting transfers between devices, local(): near_answers = lax.all_to_all(near_answers, peer_axes, 0, 0)  5.59 us
    all_to_all x1, waiting for transfers between devices, local(): far = lax.all_to_all(far, peer_axes, 0, 0)  4.1 us
  transfers between devices with their start and end apart: 6, of which 5 were waited for; matrix products, arithmetic and copies ran while one was open for 0% of the time, Pallas kernels for 13%

profile of v8, /device:TPU:0, one launch (start us, length us, event | category | flops | bytes accessed | tf_op | source)
XLA Modules:
  0.0 93.7 jit_solution(12035453774411734478)
XLA Ops:
  0.6 8.2 %product.2 = f32[16,25,4,128]{3,2,1,0:T(4,128)} custom-call(s32[1]{0:T(128)S(6)} %sub.3.part_ref, f32[6,128,4096]{2,1,0:T(8,128)} %blocks_hbm.3, s32[6]{0:T(128)} %ids_hbm.1, s32[6,32]{1,0:T(8,128)} %cols_hbm.3, f32[16,128,512]{2,1,0:T(8,128)} %features_hbm.3), custom_call_target="tpu_custom_call" | custom-call | flops 2415919104 | bytes 10485760 | tf_op jit(solution)/shard_map/product/pallas_call | solution.py:133
  8.8 6.3 %all-to-all-start = ((f32[16,25,4,128]{3,2,1,0:T(4,128)}), f32[16,25,4,128]{3,2,1,0:T(4,128)S(1)}, u32[]{:S(2)}, u32[]{:S(2)}) async-start(f32[16,25,4,128]{3,2,1,0:T(4,128)} %product.2), calls=%async_computation | async-start | bytes 1638400 | tf_op jit(solution)/shard_map/all_to_all | solution.py:337
  15.1 0.0 copy-start
  15.1 8.2 %product.3 = f32[16,24,4,128]{3,2,1,0:T(4,128)} custom-call(s32[1]{0:T(128)} %bitcast.part_ref.half_ref, f32[6,128,4096]{2,1,0:T(8,128)} %blocks_hbm.3, s32[6]{0:T(128)} %ids_hbm.1, s32[6,32]{1,0:T(8,128)} %cols_hbm.3, f32[16,128,512]{2,1,0:T(8,128)} %features_hbm.3), custom_call_target="tpu_custom_call" | custom-call | flops 2415919104 | bytes 10485760 | tf_op jit(solution)/shard_map/product/pallas_call | solution.py:133
  23.4 4.1 %all-to-all-done.pieces_ref = f32[16,25,4,128]{3,2,1,0:T(4,128)S(1)} async-done(((f32[16,25,4,128]{3,2,1,0:T(4,128)}), f32[16,25,4,128]{3,2,1,0:T(4,128)S(1)}, u32[]{:S(2)}, u32[]{:S(2)}) %all-to-all-start) | async-done | bytes 819232 | tf_op jit(solution)/shard_map/all_to_all | solution.py:337
  27.5 3.9 %all-to-all-start.1 = ((f32[16,24,4,128]{3,2,1,0:T(4,128)}), f32[16,24,4,128]{3,2,1,0:T(4,128)S(1)}, u32[]{:S(2)}, u32[]{:S(2)}) async-start(f32[16,24,4,128]{3,2,1,0:T(4,128)} %product.3), calls=%async_computation.1 | async-start | bytes 1572864 | tf_op jit(solution)/shard_map/all_to_all | solution.py:339
  31.4 1.5 %sum_pieces.1 = (f32[32,4,4,128]{3,2,1,0:T(4,128)S(1)}, s32[16,4,128]{2,1,0:T(4,128)S(1)}) custom-call(f32[16,25,4,128]{3,2,1,0:T(4,128)S(1)} %all-to-all-done.pieces_ref), custom_call_target="tpu_custom_call" | custom-call | tf_op jit(solution)/shard_map/sum_pieces/pallas_call | solution.py:190
  32.9 2.7 %collective-permute-start = (f32[32,4,4,128]{3,2,1,0:T(4,128)S(1)}, f32[32,4,4,128]{3,2,1,0:T(4,128)S(1)}, u32[]{:S(2)}, u32[]{:S(2)}) collective-permute-start(f32[32,4,4,128]{3,2,1,0:T(4,128)S(1)} %get-tuple-element.17), channel_id=1, source_target_pairs={{0,16},{16,0},{1,17},{17,1},{2,18},{18,2},{3,19},{19,3},{4,20},{20... | collective-permute-start | bytes 786440 | tf_op jit(solution)/shard_map/ppermute | solution.py:341
  35.6 0.1 reshape_squeeze.3.ids_ref
  35.7 13.3 %all-to-all-done.1.pieces_ref = f32[16,24,4,128]{3,2,1,0:T(4,128)S(1)} async-done(((f32[16,24,4,128]{3,2,1,0:T(4,128)}), f32[16,24,4,128]{3,2,1,0:T(4,128)S(1)}, u32[]{:S(2)}, u32[]{:S(2)}) %all-to-all-start.1) | async-done | bytes 786464 | tf_op jit(solution)/shard_map/all_to_all | solution.py:339
  49.0 0.0 collective-permute-done.got_ref
  49.0 0.0 copy-done
  49.0 2.3 %update.1 = (f32[32,4,4,128]{3,2,1,0:T(4,128)S(1)}, f32[16,28,4,128]{3,2,1,0:T(4,128)}) custom-call(s32[96]{0:T(128)S(1)} %reshape_squeeze.3.ids_ref, s32[1]{0:T(128)} %bitcast.part_ref.half_ref, f32[16,24,4,128]{3,2,1,0:T(4,128)S(1)} %all-to-all-done.1.pieces_ref, f32[32,4,4,128]{3,2,1,0:T(4,128)S(1)} %collective-permute-done.got_ref, f32[512,512]{1,0:T(8,128)S(1)} %copy-done), custom_call_target="tpu_custom_call" | custom-call | tf_op jit(solution)/shard_map/update/pallas_call | solution.py:231
  51.3 1.0 %collective-permute-start.1 = (f32[32,4,4,128]{3,2,1,0:T(4,128)S(1)}, f32[32,4,4,128]{3,2,1,0:T(4,128)S(1)}, u32[]{:S(2)}, u32[]{:S(2)}) collective-permute-start(f32[32,4,4,128]{3,2,1,0:T(4,128)S(1)} %get-tuple-element.18), channel_id=1, source_target_pairs={{0,16},{16,0},{1,17},{17,1},{2,18},{18,2},{3,19},{19,3},{4,20},{20... | collective-permute-start | bytes 786440 | tf_op jit(solution)/shard_map/ppermute | solution.py:345
  52.3 5.6 %all-to-all-start.3 = ((f32[16,28,4,128]{3,2,1,0:T(4,128)}), f32[16,28,4,128]{3,2,1,0:T(4,128)S(1)}, u32[]{:S(2)}, u32[]{:S(2)}) async-start(f32[16,28,4,128]{3,2,1,0:T(4,128)} %get-tuple-element.19), calls=%async_computation.3 | async-start | bytes 1835008 | tf_op jit(solution)/shard_map/all_to_all | solution.py:346
  57.9 8.5 %collective-permute-done.1.table_ref = f32[32,4,4,128]{3,2,1,0:T(4,128)S(1)} collective-permute-done((f32[32,4,4,128]{3,2,1,0:T(4,128)S(1)}, f32[32,4,4,128]{3,2,1,0:T(4,128)S(1)}, u32[]{:S(2)}, u32[]{:S(2)}) %collective-permute-start.1) | collective-permute-done | bytes 262176 | tf_op jit(solution)/shard_map/ppermute | solution.py:345
  66.4 1.5 %answer.1 = f32[16,28,4,128]{3,2,1,0:T(4,128)} custom-call(s32[96]{0:T(128)S(1)} %reshape_squeeze.3.ids_ref, s32[1]{0:T(128)} %bitcast.part_ref.half_ref, f32[32,4,4,128]{3,2,1,0:T(4,128)S(1)} %collective-permute-done.1.table_ref), custom_call_target="tpu_custom_call" | custom-call | flops 17179869184 | bytes 1835008 | tf_op jit(solution)/shard_map/answer/pallas_call | solution.py:270
  68.0 7.7 %all-to-all-done.3.answers_ref = f32[16,28,4,128]{3,2,1,0:T(4,128)S(1)} async-done(((f32[16,28,4,128]{3,2,1,0:T(4,128)}), f32[16,28,4,128]{3,2,1,0:T(4,128)S(1)}, u32[]{:S(2)}, u32[]{:S(2)}) %all-to-all-start.3) | async-done | bytes 917536 | tf_op jit(solution)/shard_map/all_to_all | solution.py:346
  75.6 3.6 %all-to-all-start.2 = ((f32[16,28,4,128]{3,2,1,0:T(4,128)}), f32[16,28,4,128]{3,2,1,0:T(4,128)S(1)}, u32[]{:S(2)}, u32[]{:S(2)}) async-start(f32[16,28,4,128]{3,2,1,0:T(4,128)} %answer.1), calls=%async_computation.2 | async-start | bytes 1835008 | tf_op jit(solution)/shard_map/all_to_all | solution.py:348
  79.3 1.0 %place.2 = (f32[16,4,8,128]{3,2,1,0:T(8,128)}, f32[6,16,4,8,128]{4,3,2,1,0:T(8,128)}) custom-call(s32[1]{0:T(128)} %bitcast.part_ref.half_ref, f32[16,28,4,128]{3,2,1,0:T(4,128)S(1)} %all-to-all-done.3.answers_ref), custom_call_target="tpu_custom_call" | custom-call | tf_op jit(solution)/shard_map/place/pallas_call | solution.py:308
  80.3 12.4 %all-to-all-done.2.answers_ref = f32[16,28,4,128]{3,2,1,0:T(4,128)S(1)} async-done(((f32[16,28,4,128]{3,2,1,0:T(4,128)}), f32[16,28,4,128]{3,2,1,0:T(4,128)S(1)}, u32[]{:S(2)}, u32[]{:S(2)}) %all-to-all-start.2) | async-done | bytes 917536 | tf_op jit(solution)/shard_map/all_to_all | solution.py:348
  92.7 1.0 %place.3 = (f32[16,4,8,128]{3,2,1,0:T(8,128)}, f32[6,16,4,8,128]{4,3,2,1,0:T(8,128)}) custom-call(s32[1]{0:T(128)S(6)} %sub.3.part_ref, f32[16,28,4,128]{3,2,1,0:T(4,128)S(1)} %all-to-all-done.2.answers_ref, f32[16,4,8,128]{3,2,1,0:T(8,128)} %get-tuple-element.20.refs_0_, ...), custom_call_target="tpu_custom_call", output_to_operand_aliasing={{0}: (2, {}), {1}: (3, {})} | custom-call | tf_op jit(solution)/shard_map/place/pallas_call | solution.py:308
  (1 shorter events, 0.0 us)
Async XLA Ops:
  8.8 18.7 %all-to-all-start = ((f32[16,25,4,128]{3,2,1,0:T(4,128)}), f32[16,25,4,128]{3,2,1,0:T(4,128)S(1)}, u32[]{:S(2)}, u32[]{:S(2)}) async-start(f32[16,25,4,128]{3,2,1,0:T(4,128)} %product.2), calls=%async_computation | async-start | bytes 1638400 | tf_op jit(solution)/shard_map/all_to_all | solution.py:337
  15.1 33.9 %copy-start = (f32[512,512]{1,0:T(8,128)S(1)}, f32[512,512]{1,0:T(8,128)}, u32[]{:S(2)}) copy-start(f32[512,512]{1,0:T(8,128)} %factor_ref.1) | copy-start | bytes 3145732
  27.5 21.5 %all-to-all-start.1 = ((f32[16,24,4,128]{3,2,1,0:T(4,128)}), f32[16,24,4,128]{3,2,1,0:T(4,128)S(1)}, u32[]{:S(2)}, u32[]{:S(2)}) async-start(f32[16,24,4,128]{3,2,1,0:T(4,128)} %product.3), calls=%async_computation.1 | async-start | bytes 1572864 | tf_op jit(solution)/shard_map/all_to_all | solution.py:339
  32.9 16.1 %collective-permute-start = (f32[32,4,4,128]{3,2,1,0:T(4,128)S(1)}, f32[32,4,4,128]{3,2,1,0:T(4,128)S(1)}, u32[]{:S(2)}, u32[]{:S(2)}) collective-permute-start(f32[32,4,4,128]{3,2,1,0:T(4,128)S(1)} %get-tuple-element.17), channel_id=1, source_target_pairs={{0,16},{16,0},{1,17},{17,1},{2,18},{18,2},{3,19},{19,3},{4,20},{20... | collective-permute-start | bytes 786440 | tf_op jit(solution)/shard_map/ppermute | solution.py:341
  51.3 15.1 %collective-permute-start.1 = (f32[32,4,4,128]{3,2,1,0:T(4,128)S(1)}, f32[32,4,4,128]{3,2,1,0:T(4,128)S(1)}, u32[]{:S(2)}, u32[]{:S(2)}) collective-permute-start(f32[32,4,4,128]{3,2,1,0:T(4,128)S(1)} %get-tuple-element.18), channel_id=1, source_target_pairs={{0,16},{16,0},{1,17},{17,1},{2,18},{18,2},{3,19},{19,3},{4,20},{20... | collective-permute-start | bytes 786440 | tf_op jit(solution)/shard_map/ppermute | solution.py:345
  52.3 23.3 %all-to-all-start.3 = ((f32[16,28,4,128]{3,2,1,0:T(4,128)}), f32[16,28,4,128]{3,2,1,0:T(4,128)S(1)}, u32[]{:S(2)}, u32[]{:S(2)}) async-start(f32[16,28,4,128]{3,2,1,0:T(4,128)} %get-tuple-element.19), calls=%async_computation.3 | async-start | bytes 1835008 | tf_op jit(solution)/shard_map/all_to_all | solution.py:346
  75.6 17.0 %all-to-all-start.2 = ((f32[16,28,4,128]{3,2,1,0:T(4,128)}), f32[16,28,4,128]{3,2,1,0:T(4,128)S(1)}, u32[]{:S(2)}, u32[]{:S(2)}) async-start(f32[16,28,4,128]{3,2,1,0:T(4,128)} %answer.1), calls=%async_computation.2 | async-start | bytes 1835008 | tf_op jit(solution)/shard_map/all_to_all | solution.py:348

commit v9 on v8

--- a/solution.py
+++ b/solution.py
@@ -65,7 +65,7 @@
         pltpu.make_async_copy(cols_hbm, cols, id_sems.at[0]),
         pltpu.make_async_copy(ids_hbm, ids, id_sems.at[1]),
     ]
-    for copy in id_copies + block_copies[:in_group] + feature_copies + block_copies[in_group:]:
+    for copy in id_copies + feature_copies + block_copies:
         copy.start()
     for copy in id_copies:
         copy.wait()
@@ -106,10 +106,10 @@
         f_low[here, :] = low
         return carry
 
-    combine(0)
     for k in range(feature_parts):
         feature_copies[k].wait()
         lax.fori_loop(k * part_tiles, (k + 1) * part_tiles, split_tile, 0)
+    combine(0)
     for group in range(groups):
         if group + 1 < groups:
             combine(group + 1)

time: 94.1 us -> 95.2 us (1.012)
  Pallas kernels: 23.8 us -> 25.8 us
  waiting for transfers between devices: 46 us -> 44.9 us
    pallas_call x2, Pallas kernels: 16.4 us -> 18.4 us  [product(): pl.pallas_call(functools.partial(product_kernel, with_ids, groups, featur...]
    all_to_all x1, waiting for transfers between devices: 4.1 us -> 3.09 us  [local(): far = lax.all_to_all(far, peer_axes, 0, 0)]
  transfers between devices with their start and end apart: 6 -> 6, of which waited for: 5 -> 5; matrix products, arithmetic and copies ran while one was open for 0% -> 0% of each run, Pallas kernels for 13% -> 14%
where the time goes in v9:
time: 95.2 us; the launch traced here: 94.7 us
  waiting for transfers between devices  44.9 us (47%)
  Pallas kernels  25.8 us (27%)
  starting transfers between devices  23.1 us (24%)
    pallas_call x2, Pallas kernels, product(): pl.pallas_call(functools.partial(product_kernel, with_ids, groups, featur...  18.4 us
    all_to_all x1, waiting for transfers between devices, local(): near = lax.all_to_all(near, peer_axes, 0, 0)  13.3 us
    all_to_all x1, waiting for transfers between devices, local(): far_answers = lax.all_to_all(far_answers, peer_axes, 0, 0)  12.4 us
    ppermute x1, waiting for transfers between devices, local(): far_rows = lax.ppermute(near_rows, 'half', swap)  8.52 us
    all_to_all x1, waiting for transfers between devices, local(): near_answers = lax.all_to_all(near_answers, peer_axes, 0, 0)  7.66 us
    all_to_all x1, starting transfers between devices, local(): far = lax.all_to_all(far, peer_axes, 0, 0)  6.3 us
    all_to_all x1, starting transfers between devices, local(): near_answers = lax.all_to_all(near_answers, peer_axes, 0, 0)  5.6 us
    all_to_all x1, starting transfers between devices, local(): near = lax.all_to_all(near, peer_axes, 0, 0)  3.91 us
  transfers between devices with their start and end apart: 6, of which 5 were waited for; matrix products, arithmetic and copies ran while one was open for 0% of the time, Pallas kernels for 14%

profile of v9, /device:TPU:0, one launch (start us, length us, event | category | flops | bytes accessed | tf_op | source)
XLA Modules:
  0.0 94.7 jit_solution(10796544685357362213)
XLA Ops:
  0.6 9.2 %product.2 = f32[16,25,4,128]{3,2,1,0:T(4,128)} custom-call(s32[1]{0:T(128)S(6)} %sub.3.part_ref, f32[6,128,4096]{2,1,0:T(8,128)} %blocks_hbm.3, s32[6]{0:T(128)} %ids_hbm.1, s32[6,32]{1,0:T(8,128)} %cols_hbm.3, f32[16,128,512]{2,1,0:T(8,128)} %features_hbm.3), custom_call_target="tpu_custom_call" | custom-call | flops 2415919104 | bytes 10485760 | tf_op jit(solution)/shard_map/product/pallas_call | solution.py:133
  9.8 6.3 %all-to-all-start = ((f32[16,25,4,128]{3,2,1,0:T(4,128)}), f32[16,25,4,128]{3,2,1,0:T(4,128)S(1)}, u32[]{:S(2)}, u32[]{:S(2)}) async-start(f32[16,25,4,128]{3,2,1,0:T(4,128)} %product.2), calls=%async_computation | async-start | bytes 1638400 | tf_op jit(solution)/shard_map/all_to_all | solution.py:337
  16.1 0.0 copy-start
  16.1 9.3 %product.3 = f32[16,24,4,128]{3,2,1,0:T(4,128)} custom-call(s32[1]{0:T(128)} %bitcast.part_ref.half_ref, f32[6,128,4096]{2,1,0:T(8,128)} %blocks_hbm.3, s32[6]{0:T(128)} %ids_hbm.1, s32[6,32]{1,0:T(8,128)} %cols_hbm.3, f32[16,128,512]{2,1,0:T(8,128)} %features_hbm.3), custom_call_target="tpu_custom_call" | custom-call | flops 2415919104 | bytes 10485760 | tf_op jit(solution)/shard_map/product/pallas_call | solution.py:133
  25.4 3.1 %all-to-all-done.pieces_ref = f32[16,25,4,128]{3,2,1,0:T(4,128)S(1)} async-done(((f32[16,25,4,128]{3,2,1,0:T(4,128)}), f32[16,25,4,128]{3,2,1,0:T(4,128)S(1)}, u32[]{:S(2)}, u32[]{:S(2)}) %all-to-all-start) | async-done | bytes 819232 | tf_op jit(solution)/shard_map/all_to_all | solution.py:337
  28.5 3.9 %all-to-all-start.1 = ((f32[16,24,4,128]{3,2,1,0:T(4,128)}), f32[16,24,4,128]{3,2,1,0:T(4,128)S(1)}, u32[]{:S(2)}, u32[]{:S(2)}) async-start(f32[16,24,4,128]{3,2,1,0:T(4,128)} %product.3), calls=%async_computation.1 | async-start | bytes 1572864 | tf_op jit(solution)/shard_map/all_to_all | solution.py:339
  32.4 1.5 %sum_pieces.1 = (f32[32,4,4,128]{3,2,1,0:T(4,128)S(1)}, s32[16,4,128]{2,1,0:T(4,128)S(1)}) custom-call(f32[16,25,4,128]{3,2,1,0:T(4,128)S(1)} %all-to-all-done.pieces_ref), custom_call_target="tpu_custom_call" | custom-call | tf_op jit(solution)/shard_map/sum_pieces/pallas_call | solution.py:190
  33.9 2.7 %collective-permute-start = (f32[32,4,4,128]{3,2,1,0:T(4,128)S(1)}, f32[32,4,4,128]{3,2,1,0:T(4,128)S(1)}, u32[]{:S(2)}, u32[]{:S(2)}) collective-permute-start(f32[32,4,4,128]{3,2,1,0:T(4,128)S(1)} %get-tuple-element.17), channel_id=1, source_target_pairs={{0,16},{16,0},{1,17},{17,1},{2,18},{18,2},{3,19},{19,3},{4,20},{20... | collective-permute-start | bytes 786440 | tf_op jit(solution)/shard_map/ppermute | solution.py:341
  36.6 0.1 reshape_squeeze.3.ids_ref
  36.7 13.3 %all-to-all-done.1.pieces_ref = f32[16,24,4,128]{3,2,1,0:T(4,128)S(1)} async-done(((f32[16,24,4,128]{3,2,1,0:T(4,128)}), f32[16,24,4,128]{3,2,1,0:T(4,128)S(1)}, u32[]{:S(2)}, u32[]{:S(2)}) %all-to-all-start.1) | async-done | bytes 786464 | tf_op jit(solution)/shard_map/all_to_all | solution.py:339
  50.0 0.0 collective-permute-done.got_ref
  50.0 0.0 copy-done
  50.0 2.3 %update.1 = (f32[32,4,4,128]{3,2,1,0:T(4,128)S(1)}, f32[16,28,4,128]{3,2,1,0:T(4,128)}) custom-call(s32[96]{0:T(128)S(1)} %reshape_squeeze.3.ids_ref, s32[1]{0:T(128)} %bitcast.part_ref.half_ref, f32[16,24,4,128]{3,2,1,0:T(4,128)S(1)} %all-to-all-done.1.pieces_ref, f32[32,4,4,128]{3,2,1,0:T(4,128)S(1)} %collective-permute-done.got_ref, f32[512,512]{1,0:T(8,128)S(1)} %copy-done), custom_call_target="tpu_custom_call" | custom-call | tf_op jit(solution)/shard_map/update/pallas_call | solution.py:231
  52.3 1.0 %collective-permute-start.1 = (f32[32,4,4,128]{3,2,1,0:T(4,128)S(1)}, f32[32,4,4,128]{3,2,1,0:T(4,128)S(1)}, u32[]{:S(2)}, u32[]{:S(2)}) collective-permute-start(f32[32,4,4,128]{3,2,1,0:T(4,128)S(1)} %get-tuple-element.18), channel_id=1, source_target_pairs={{0,16},{16,0},{1,17},{17,1},{2,18},{18,2},{3,19},{19,3},{4,20},{20... | collective-permute-start | bytes 786440 | tf_op jit(solution)/shard_map/ppermute | solution.py:345
  53.4 5.6 %all-to-all-start.3 = ((f32[16,28,4,128]{3,2,1,0:T(4,128)}), f32[16,28,4,128]{3,2,1,0:T(4,128)S(1)}, u32[]{:S(2)}, u32[]{:S(2)}) async-start(f32[16,28,4,128]{3,2,1,0:T(4,128)} %get-tuple-element.19), calls=%async_computation.3 | async-start | bytes 1835008 | tf_op jit(solution)/shard_map/all_to_all | solution.py:346
  59.0 8.5 %collective-permute-done.1.table_ref = f32[32,4,4,128]{3,2,1,0:T(4,128)S(1)} collective-permute-done((f32[32,4,4,128]{3,2,1,0:T(4,128)S(1)}, f32[32,4,4,128]{3,2,1,0:T(4,128)S(1)}, u32[]{:S(2)}, u32[]{:S(2)}) %collective-permute-start.1) | collective-permute-done | bytes 262176 | tf_op jit(solution)/shard_map/ppermute | solution.py:345
  67.5 1.5 %answer.1 = f32[16,28,4,128]{3,2,1,0:T(4,128)} custom-call(s32[96]{0:T(128)S(1)} %reshape_squeeze.3.ids_ref, s32[1]{0:T(128)} %bitcast.part_ref.half_ref, f32[32,4,4,128]{3,2,1,0:T(4,128)S(1)} %collective-permute-done.1.table_ref), custom_call_target="tpu_custom_call" | custom-call | flops 17179869184 | bytes 1835008 | tf_op jit(solution)/shard_map/answer/pallas_call | solution.py:270
  69.0 7.7 %all-to-all-done.3.answers_ref = f32[16,28,4,128]{3,2,1,0:T(4,128)S(1)} async-done(((f32[16,28,4,128]{3,2,1,0:T(4,128)}), f32[16,28,4,128]{3,2,1,0:T(4,128)S(1)}, u32[]{:S(2)}, u32[]{:S(2)}) %all-to-all-start.3) | async-done | bytes 917536 | tf_op jit(solution)/shard_map/all_to_all | solution.py:346
  76.7 3.6 %all-to-all-start.2 = ((f32[16,28,4,128]{3,2,1,0:T(4,128)}), f32[16,28,4,128]{3,2,1,0:T(4,128)S(1)}, u32[]{:S(2)}, u32[]{:S(2)}) async-start(f32[16,28,4,128]{3,2,1,0:T(4,128)} %answer.1), calls=%async_computation.2 | async-start | bytes 1835008 | tf_op jit(solution)/shard_map/all_to_all | solution.py:348
  80.3 1.0 %place.2 = (f32[16,4,8,128]{3,2,1,0:T(8,128)}, f32[6,16,4,8,128]{4,3,2,1,0:T(8,128)}) custom-call(s32[1]{0:T(128)} %bitcast.part_ref.half_ref, f32[16,28,4,128]{3,2,1,0:T(4,128)S(1)} %all-to-all-done.3.answers_ref), custom_call_target="tpu_custom_call" | custom-call | tf_op jit(solution)/shard_map/place/pallas_call | solution.py:308
  81.3 12.4 %all-to-all-done.2.answers_ref = f32[16,28,4,128]{3,2,1,0:T(4,128)S(1)} async-done(((f32[16,28,4,128]{3,2,1,0:T(4,128)}), f32[16,28,4,128]{3,2,1,0:T(4,128)S(1)}, u32[]{:S(2)}, u32[]{:S(2)}) %all-to-all-start.2) | async-done | bytes 917536 | tf_op jit(solution)/shard_map/all_to_all | solution.py:348
  93.7 1.0 %place.3 = (f32[16,4,8,128]{3,2,1,0:T(8,128)}, f32[6,16,4,8,128]{4,3,2,1,0:T(8,128)}) custom-call(s32[1]{0:T(128)S(6)} %sub.3.part_ref, f32[16,28,4,128]{3,2,1,0:T(4,128)S(1)} %all-to-all-done.2.answers_ref, f32[16,4,8,128]{3,2,1,0:T(8,128)} %get-tuple-element.20.refs_0_, ...), custom_call_target="tpu_custom_call", output_to_operand_aliasing={{0}: (2, {}), {1}: (3, {})} | custom-call | tf_op jit(solution)/shard_map/place/pallas_call | solution.py:308
  (1 shorter events, 0.0 us)
Async XLA Ops:
  9.8 18.7 %all-to-all-start = ((f32[16,25,4,128]{3,2,1,0:T(4,128)}), f32[16,25,4,128]{3,2,1,0:T(4,128)S(1)}, u32[]{:S(2)}, u32[]{:S(2)}) async-start(f32[16,25,4,128]{3,2,1,0:T(4,128)} %product.2), calls=%async_computation | async-start | bytes 1638400 | tf_op jit(solution)/shard_map/all_to_all | solution.py:337
  16.1 33.9 %copy-start = (f32[512,512]{1,0:T(8,128)S(1)}, f32[512,512]{1,0:T(8,128)}, u32[]{:S(2)}) copy-start(f32[512,512]{1,0:T(8,128)} %factor_ref.1) | copy-start | bytes 3145732
  28.5 21.5 %all-to-all-start.1 = ((f32[16,24,4,128]{3,2,1,0:T(4,128)}), f32[16,24,4,128]{3,2,1,0:T(4,128)S(1)}, u32[]{:S(2)}, u32[]{:S(2)}) async-start(f32[16,24,4,128]{3,2,1,0:T(4,128)} %product.3), calls=%async_computation.1 | async-start | bytes 1572864 | tf_op jit(solution)/shard_map/all_to_all | solution.py:339
  33.9 16.1 %collective-permute-start = (f32[32,4,4,128]{3,2,1,0:T(4,128)S(1)}, f32[32,4,4,128]{3,2,1,0:T(4,128)S(1)}, u32[]{:S(2)}, u32[]{:S(2)}) collective-permute-start(f32[32,4,4,128]{3,2,1,0:T(4,128)S(1)} %get-tuple-element.17), channel_id=1, source_target_pairs={{0,16},{16,0},{1,17},{17,1},{2,18},{18,2},{3,19},{19,3},{4,20},{20... | collective-permute-start | bytes 786440 | tf_op jit(solution)/shard_map/ppermute | solution.py:341
  52.3 15.1 %collective-permute-start.1 = (f32[32,4,4,128]{3,2,1,0:T(4,128)S(1)}, f32[32,4,4,128]{3,2,1,0:T(4,128)S(1)}, u32[]{:S(2)}, u32[]{:S(2)}) collective-permute-start(f32[32,4,4,128]{3,2,1,0:T(4,128)S(1)} %get-tuple-element.18), channel_id=1, source_target_pairs={{0,16},{16,0},{1,17},{17,1},{2,18},{18,2},{3,19},{19,3},{4,20},{20... | collective-permute-start | bytes 786440 | tf_op jit(solution)/shard_map/ppermute | solution.py:345
  53.4 23.3 %all-to-all-start.3 = ((f32[16,28,4,128]{3,2,1,0:T(4,128)}), f32[16,28,4,128]{3,2,1,0:T(4,128)S(1)}, u32[]{:S(2)}, u32[]{:S(2)}) async-start(f32[16,28,4,128]{3,2,1,0:T(4,128)} %get-tuple-element.19), calls=%async_computation.3 | async-start | bytes 1835008 | tf_op jit(solution)/shard_map/all_to_all | solution.py:346
  76.7 17.0 %all-to-all-start.2 = ((f32[16,28,4,128]{3,2,1,0:T(4,128)}), f32[16,28,4,128]{3,2,1,0:T(4,128)S(1)}, u32[]{:S(2)}, u32[]{:S(2)}) async-start(f32[16,28,4,128]{3,2,1,0:T(4,128)} %answer.1), calls=%async_computation.2 | async-start | bytes 1835008 | tf_op jit(solution)/shard_map/all_to_all | solution.py:348
